TPU v7x, 256 devices: a whole 4x4x8 slice. The times are simulated.
256 devices in a mesh: tm: 4 (over y), rows: 64 (over z, x, core).
Axes of the slice: x: 4, y: 4, z: 8, core: 2. Of those that a mesh axis runs over, the one named last changes fastest.
Arguments:
- latents: bfloat16 [8, 512, 48, 384], P('tm', 'rows'), may hold values from -27 to 27
- gain_first: float32 [384], replicated, may hold values from 0.1 to 1.9
- kernel_first: bfloat16 [3, 3, 3, 384, 192], replicated, may hold values from -0.0625 to 0.0625
- gain_second: float32 [192], replicated, may hold values from 0.1 to 1.9
- kernel_second: bfloat16 [3, 3, 3, 192, 192], replicated, may hold values from -0.078125 to 0.078125
- shortcut: bfloat16 [384, 192], replicated, may hold values from -0.3125 to 0.3125
- gain_third: float32 [192], replicated, may hold values from 0.1 to 1.9
- kernel_third: bfloat16 [3, 3, 3, 192, 192], replicated, may hold values from -0.078125 to 0.078125
Outputs:
- block_out: bfloat16 [8, 512, 48, 192], P('tm', 'rows')
- decoded: bfloat16 [8, 1024, 96, 192], P('tm', 'rows')
All inputs are finite; a program needn't handle non-finite values.
Results may differ from a plain program's by a relative error of at most 0.015.
Values may be sent and summed in bfloat16 or wider, within the bound.
No kernel may reach another device: no remote copies, remote signals or barrier semaphores. Data moves between devices by JAX's collectives and lax.ppermute only.
A program may use at most 128 MiB of HBM per device.

v0:
```python
import jax
import jax.numpy as jnp
from jax import lax
from jax.sharding import PartitionSpec as P


def from_behind(value, axis, steps):
    count = lax.axis_size(axis)
    initial, last = (max(0, -steps), min(count, count - steps))
    return lax.ppermute(value, axis, [(source, source + steps) for source in range(initial, last)])


def extended_2(block, sides, width):
    for axis, dim in sides:
        count = lax.axis_size(axis)
        forward = [(i, i + 1) for i in range(count - 1)]
        backward = [(target, source) for source, target in forward]
        low = lax.ppermute(
            lax.slice_in_dim(block, block.shape[dim] - width, None, axis=dim), axis, forward
        )
        high = lax.ppermute(lax.slice_in_dim(block, 0, width, axis=dim), axis, backward)
        block = jnp.concatenate([low, block, high], axis=dim)
    return block


def activate(values, scales):
    wide_values = values.astype(jnp.float32)
    mean_square = jnp.mean(wide_values * wide_values, axis=-1, keepdims=True)
    return jax.nn.silu(wide_values * lax.rsqrt(mean_square + 1e-06) * scales).astype(jnp.bfloat16)


def convolve(extended, kernel):
    frames = extended.shape[0] - 2
    slab_rows = extended.shape[1] - 2
    breadth = extended.shape[2]
    padded = jnp.pad(extended, ((0, 0), (0, 0), (1, 1), (0, 0)))
    columns = jnp.concatenate(
        [padded[:, :, 0:breadth], padded[:, :, 1 : breadth + 1], padded[:, :, 2 : breadth + 2]],
        axis=3,
    )
    folded = kernel.reshape(3, 3, 3 * kernel.shape[3], kernel.shape[4])
    summed = jnp.zeros((frames, slab_rows, breadth, kernel.shape[4]), jnp.float32)
    for offset_time in range(3):
        for offset_row in range(3):
            window = columns[
                offset_time : offset_time + frames, offset_row : offset_row + slab_rows
            ]
            summed = summed + jnp.einsum(
                "fhwk,ko->fhwo",
                window,
                folded[offset_time, offset_row],
                preferred_element_type=jnp.float32,
            )
    return summed


def with_cache(active):
    earlier = from_behind(active, "tm", 1)
    return jnp.concatenate([earlier, active], axis=0)


def rim_rows(extended):
    return extended_2(extended, (("rows", 1),), 1)


def fine_reach(active):
    earlier = from_behind(active, "tm", 1)
    joined = jnp.concatenate([earlier, active], axis=0)
    return extended_2(joined, (("rows", 1),), 1)


def upsample(values):
    return jnp.repeat(jnp.repeat(values, 2, axis=1), 2, axis=2)


def body(
    latents,
    gain_first,
    kernel_first,
    gain_second,
    kernel_second,
    shortcut,
    gain_third,
    kernel_third,
):
    normed_in = activate(latents, gain_first)
    first_out = convolve(rim_rows(with_cache(normed_in)), kernel_first).astype(jnp.bfloat16)
    second_in = activate(first_out, gain_second)
    second_out = convolve(rim_rows(with_cache(second_in)), kernel_second)
    skipped = jnp.einsum("fhwc,co->fhwo", latents, shortcut, preferred_element_type=jnp.float32)
    block_out = (skipped + second_out).astype(jnp.bfloat16)
    third_in = activate(block_out, gain_third)
    widened = fine_reach(upsample(third_in))
    decoded = convolve(widened, kernel_third).astype(jnp.bfloat16)
    return (block_out, decoded)


def solution(mesh):
    return jax.shard_map(
        body,
        mesh=mesh,
        in_specs=(P("tm", "rows", None, None), P(), P(), P(), P(), P(), P(), P()),
        out_specs=(P("tm", "rows", None, None), P("tm", "rows", None, None)),
        check_vma=False,
    )
```

profile of v0, /device:TPU:119, one launch (start us, length us, event | category | flops | bytes accessed | tf_op | source)
XLA Modules:
  0.0 165.6 jit_solution(8208207092761475087)
XLA Ops:
  0.6 1.3 fusion.29
  1.9 1.5 fusion.36
  3.4 2.9 %collective-permute-start = (bf16[2,8,48,384]{3,2,1,0:T(8,128)(2,1)S(1)}, bf16[2,8,48,384]{3,2,1,0:T(8,128)(2,1)S(1)}, u32[]{:S(2)}, u32[]{:S(2)}) collective-permute-start(bf16[2,8,48,384]{3,2,1,0:T(8,128)(2,1)S(1)} %fusion.36), channel_id=1, source_target_pairs={{0,64},{64,128},{128,192},{1,65},{65,129},{129,193},{2,66},{66,130... | collective-permute-start | bytes 1769480 | tf_op jit(solution)/shard_map/ppermute | solution.py:10
  6.4 13.2 %collective-permute-done = bf16[2,8,48,384]{3,2,1,0:T(8,128)(2,1)S(1)} collective-permute-done((bf16[2,8,48,384]{3,2,1,0:T(8,128)(2,1)S(1)}, bf16[2,8,48,384]{3,2,1,0:T(8,128)(2,1)S(1)}, u32[]{:S(2)}, u32[]{:S(2)}) %collective-permute-start) | collective-permute-done | bytes 589856 | tf_op jit(solution)/shard_map/ppermute | solution.py:10
  19.6 6.1 %collective-permute-start.1 = (bf16[4,1,48,384]{3,2,1,0:T(8,128)(2,1)S(1)}, bf16[4,1,48,384]{3,2,1,0:T(8,128)(2,1)S(1)}, u32[]{:S(2)}, u32[]{:S(2)}) collective-permute-start(bf16[4,1,48,384]{3,2,1,0:T(8,128)(2,1)S(1)} %get-tuple-element.8), channel_id=1, source_target_pairs={{0,1},{1,2},{2,3},{3,4},{4,5},{5,6},{6,7},{7,8},{8,9},{9,10},{10,1... | collective-permute-start | bytes 442376 | tf_op jit(solution)/shard_map/ppermute | solution.py:18
  25.7 1.9 %collective-permute-start.2 = (bf16[4,1,48,384]{3,2,1,0:T(8,128)(2,1)S(1)}, bf16[4,1,48,384]{3,2,1,0:T(8,128)(2,1)S(1)}, u32[]{:S(2)}, u32[]{:S(2)}) collective-permute-start(bf16[4,1,48,384]{3,2,1,0:T(8,128)(2,1)S(1)} %get-tuple-element.9), channel_id=1, source_target_pairs={{1,0},{2,1},{3,2},{4,3},{5,4},{6,5},{7,6},{8,7},{9,8},{10,9},{11,1... | collective-permute-start | bytes 442376 | tf_op jit(solution)/shard_map/ppermute | solution.py:21
  27.6 2.6 %copy.78 = bf16[3,3,3,24,8,384]{5,4,2,3,1,0:T(8,128)(2,1)S(1)} copy(bf16[3,3,3,24,8,384]{5,4,3,2,1,0:T(8,128)(2,1)} %bitcast.258) | data formatting | bytes 7962624 | tf_op jit(solution)/shard_map/reshape | solution.py:41
  30.3 5.2 %collective-permute-done.2 = bf16[4,1,48,384]{3,2,1,0:T(8,128)(2,1)S(1)} collective-permute-done((bf16[4,1,48,384]{3,2,1,0:T(8,128)(2,1)S(1)}, bf16[4,1,48,384]{3,2,1,0:T(8,128)(2,1)S(1)}, u32[]{:S(2)}, u32[]{:S(2)}) %collective-permute-start.2) | collective-permute-done | bytes 147488 | tf_op jit(solution)/shard_map/ppermute | solution.py:21
  35.5 0.9 select_maximum_fusion
  36.4 0.9 fusion.76
  37.3 0.4 pad_maximum_fusion.1
  37.7 0.7 fusion.48
  38.4 0.7 fusion.49
  39.1 0.7 fusion.50
  39.8 0.7 fusion.51
  40.5 0.7 fusion.52
  41.2 0.7 fusion.53
  41.9 0.7 fusion.54
  42.6 0.7 fusion.55
  43.4 1.0 multiply_reduce_fusion
  44.4 0.3 multiply_convert_fusion
  44.7 2.9 %collective-permute-start.3 = (bf16[2,8,48,192]{3,2,1,0:T(8,128)(2,1)S(1)}, bf16[2,8,48,192]{3,2,1,0:T(8,128)(2,1)S(1)}, u32[]{:S(2)}, u32[]{:S(2)}) collective-permute-start(bf16[2,8,48,192]{3,2,1,0:T(8,128)(2,1)S(1)} %multiply_convert_fusion), channel_id=1, source_target_pairs={{0,64},{64,128},{128,192},{1,65},{65,129},{129,193},{2,66},{66,130... | collective-permute-start | bytes 884744 | tf_op jit(solution)/shard_map/ppermute | solution.py:10
  47.6 5.6 %collective-permute-done.3 = bf16[2,8,48,192]{3,2,1,0:T(8,128)(2,1)S(1)} collective-permute-done((bf16[2,8,48,192]{3,2,1,0:T(8,128)(2,1)S(1)}, bf16[2,8,48,192]{3,2,1,0:T(8,128)(2,1)S(1)}, u32[]{:S(2)}, u32[]{:S(2)}) %collective-permute-start.3) | collective-permute-done | bytes 294944 | tf_op jit(solution)/shard_map/ppermute | solution.py:10
  53.3 4.6 %collective-permute-start.4 = (bf16[4,1,48,192]{3,2,1,0:T(8,128)(2,1)S(1)}, bf16[4,1,48,192]{3,2,1,0:T(8,128)(2,1)S(1)}, u32[]{:S(2)}, u32[]{:S(2)}) collective-permute-start(bf16[4,1,48,192]{3,2,1,0:T(8,128)(2,1)S(1)} %get-tuple-element.12), channel_id=1, source_target_pairs={{0,1},{1,2},{2,3},{3,4},{4,5},{5,6},{6,7},{7,8},{8,9},{9,10},{10,1... | collective-permute-start | bytes 221192 | tf_op jit(solution)/shard_map/ppermute | solution.py:18
  57.9 2.1 %collective-permute-start.5 = (bf16[4,1,48,192]{3,2,1,0:T(8,128)(2,1)S(1)}, bf16[4,1,48,192]{3,2,1,0:T(8,128)(2,1)S(1)}, u32[]{:S(2)}, u32[]{:S(2)}) collective-permute-start(bf16[4,1,48,192]{3,2,1,0:T(8,128)(2,1)S(1)} %get-tuple-element.13), channel_id=1, source_target_pairs={{1,0},{2,1},{3,2},{4,3},{5,4},{6,5},{7,6},{8,7},{9,8},{10,9},{11,1... | collective-permute-start | bytes 221192 | tf_op jit(solution)/shard_map/ppermute | solution.py:21
  60.0 0.4 fusion.72
  60.4 6.7 %collective-permute-done.5 = bf16[4,1,48,192]{3,2,1,0:T(8,128)(2,1)S(1)} collective-permute-done((bf16[4,1,48,192]{3,2,1,0:T(8,128)(2,1)S(1)}, bf16[4,1,48,192]{3,2,1,0:T(8,128)(2,1)S(1)}, u32[]{:S(2)}, u32[]{:S(2)}) %collective-permute-start.5) | collective-permute-done | bytes 73760 | tf_op jit(solution)/shard_map/ppermute | solution.py:21
  67.1 0.6 select_maximum_fusion.2
  67.8 0.6 fusion.77
  68.4 1.6 pad_maximum_fusion.2
  70.1 0.1 copy-done.3
  70.2 0.5 fusion.64
  70.6 0.5 fusion.65
  71.1 0.5 fusion.66
  71.6 0.5 fusion.67
  72.1 0.5 fusion.68
  72.6 0.5 fusion.69
  73.0 0.5 fusion.70
  73.5 0.5 fusion.71
  74.0 0.8 fusion.40
  74.8 0.3 fusion.47
  75.2 0.3 copy-done.5
  75.5 1.4 broadcast_in_dim.5
  77.0 1.5 reshape.49
  78.5 2.9 %collective-permute-start.6 = (bf16[2,16,96,192]{3,2,1,0:T(8,128)(2,1)S(1)}, bf16[2,16,96,192]{3,2,1,0:T(8,128)(2,1)S(1)}, u32[]{:S(2)}, u32[]{:S(2)}) collective-permute-start(bf16[2,16,96,192]{3,2,1,0:T(8,128)(2,1)S(1)} %reshape.49), channel_id=1, source_target_pairs={{0,64},{64,128},{128,192},{1,65},{65,129},{129,193},{2,66},{66,130... | collective-permute-start | bytes 3538952 | tf_op jit(solution)/shard_map/ppermute | solution.py:10
  81.4 29.5 %collective-permute-done.6 = bf16[2,16,96,192]{3,2,1,0:T(8,128)(2,1)S(1)} collective-permute-done((bf16[2,16,96,192]{3,2,1,0:T(8,128)(2,1)S(1)}, bf16[2,16,96,192]{3,2,1,0:T(8,128)(2,1)S(1)}, u32[]{:S(2)}, u32[]{:S(2)}) %collective-permute-start.6) | collective-permute-done | bytes 1179680 | tf_op jit(solution)/shard_map/ppermute | solution.py:10
  110.9 0.1 constant_dynamic-update-slice_fusion.1
  111.0 0.1 constant_dynamic-update-slice_fusion
  111.2 4.7 %collective-permute-start.7 = (bf16[4,1,96,192]{3,2,1,0:T(8,128)(2,1)S(1)}, bf16[4,1,96,192]{3,2,1,0:T(8,128)(2,1)S(1)}, u32[]{:S(2)}, u32[]{:S(2)}) collective-permute-start(bf16[4,1,96,192]{3,2,1,0:T(8,128)(2,1)S(1)} %get-tuple-element.4), channel_id=1, source_target_pairs={{0,1},{1,2},{2,3},{3,4},{4,5},{5,6},{6,7},{7,8},{8,9},{9,10},{10,1... | collective-permute-start | bytes 442376 | tf_op jit(solution)/shard_map/ppermute | solution.py:18
  115.9 1.9 %collective-permute-start.8 = (bf16[4,1,96,192]{3,2,1,0:T(8,128)(2,1)S(1)}, bf16[4,1,96,192]{3,2,1,0:T(8,128)(2,1)S(1)}, u32[]{:S(2)}, u32[]{:S(2)}) collective-permute-start(bf16[4,1,96,192]{3,2,1,0:T(8,128)(2,1)S(1)} %get-tuple-element.5), channel_id=1, source_target_pairs={{1,0},{2,1},{3,2},{4,3},{5,4},{6,5},{7,6},{8,7},{9,8},{10,9},{11,1... | collective-permute-start | bytes 442376 | tf_op jit(solution)/shard_map/ppermute | solution.py:21
  117.9 0.7 collective-permute-done.7
  118.5 7.7 %collective-permute-done.8 = bf16[4,1,96,192]{3,2,1,0:T(8,128)(2,1)S(1)} collective-permute-done((bf16[4,1,96,192]{3,2,1,0:T(8,128)(2,1)S(1)}, bf16[4,1,96,192]{3,2,1,0:T(8,128)(2,1)S(1)}, u32[]{:S(2)}, u32[]{:S(2)}) %collective-permute-start.8) | collective-permute-done | bytes 147488 | tf_op jit(solution)/shard_map/ppermute | solution.py:21
  126.2 1.8 %fusion.5 = bf16[4,18,98,192]{3,2,1,0:T(8,128)(2,1)S(1)} fusion(bf16[4,1,96,192]{3,2,1,0:T(8,128)(2,1)S(1)} %collective-permute-done.8, bf16[4,16,96,192]{3,2,1,0:T(8,128)(2,1)S(1)} %constant_dynamic-update-slice_fusion, bf16[4,1,96,192]{3,2,1,0:T(8,128)(2,1)S(1)} %collective-permute-done.7), kind=kLoop, calls=%fused_computation.11 | loop fusion | flops 16257024 | bytes 5363712 | tf_op jit(solution)/shard_map/concatenate | solution.py:22
  128.1 2.7 %fusion.74 = (bf16[4,18,96,192]{3,2,1,0:T(8,128)(2,1)S(1)}, bf16[4,18,96,192]{3,2,1,0:T(8,128)(2,1)S(1)}) fusion(bf16[4,18,98,192]{3,2,1,0:T(8,128)(2,1)S(1)} %fusion.5), kind=kLoop, calls=%fused_computation.132 | loop fusion | bytes 10616832 | tf_op jit(solution)/shard_map/slice | solution.py:38
  130.8 5.6 %pad_maximum_fusion = bf16[4,18,96,576]{3,2,1,0:T(8,128)(2,1)S(1)} fusion(bf16[4,18,96,192]{3,2,1,0:T(8,128)(2,1)S(1)} %get-tuple-element.3, bf16[4,1,96,192]{3,2,1,0:T(8,128)(2,1)S(1)} %collective-permute-done.8, bf16[4,16,96,192]{3,2,1,0:T(8,128)(2,1)S(1)} %constant_dynamic-update-slice_fusion, bf16[4,1,96,192]{3,2,1,0:T(8,128)(2,1)S(1)} %collective-permute-done.7, ...), kind=kLoop, calls=%fused_computation.2 | loop fusion | flops 39813120 | bytes 15925248 | tf_op jit(solution)/shard_map/concatenate | solution.py:37
  136.4 1.4 fusion.56
  137.8 1.4 fusion.57
  139.2 1.4 fusion.58
  140.6 3.1 %fusion.59 = f32[2,16,96,192]{3,2,1,0:T(8,128)} fusion(bf16[4,18,96,576]{3,2,1,0:T(8,128)(2,1)S(1)} %pad_maximum_fusion, bf16[3,3,576,192]{3,2,1,0:T(8,128)(2,1)S(1)} %bitcast.273), kind=kOutput, calls=%fused_computation.95 | convolution fusion | flops 679477248 | bytes 11501568 | tf_op jit(solution)/shard_map/fhwk,ko->fhwo/dot_general | solution.py:48
  143.6 3.1 %fusion.60 = f32[2,16,96,192]{3,2,1,0:T(8,128)} fusion(bf16[4,18,96,576]{3,2,1,0:T(8,128)(2,1)S(1)} %pad_maximum_fusion, bf16[3,3,576,192]{3,2,1,0:T(8,128)(2,1)S(1)} %bitcast.274), kind=kOutput, calls=%fused_computation.97 | convolution fusion | flops 679477248 | bytes 11501568 | tf_op jit(solution)/shard_map/fhwk,ko->fhwo/dot_general | solution.py:48
  146.7 3.1 %fusion.61 = f32[2,16,96,192]{3,2,1,0:T(8,128)} fusion(bf16[4,18,96,576]{3,2,1,0:T(8,128)(2,1)S(1)} %pad_maximum_fusion, bf16[3,3,576,192]{3,2,1,0:T(8,128)(2,1)S(1)} %bitcast.275), kind=kOutput, calls=%fused_computation.99 | convolution fusion | flops 679477248 | bytes 11501568 | tf_op jit(solution)/shard_map/fhwk,ko->fhwo/dot_general | solution.py:48
  149.8 3.0 %fusion.62 = f32[2,16,96,192]{3,2,1,0:T(8,128)} fusion(bf16[4,18,96,576]{3,2,1,0:T(8,128)(2,1)S(1)} %pad_maximum_fusion, bf16[3,3,576,192]{3,2,1,0:T(8,128)(2,1)S(1)} %bitcast.276), kind=kOutput, calls=%fused_computation.101 | convolution fusion | flops 679477248 | bytes 11501568 | tf_op jit(solution)/shard_map/fhwk,ko->fhwo/dot_general | solution.py:48
  152.9 3.1 %fusion.63 = f32[2,16,96,192]{3,2,1,0:T(8,128)} fusion(bf16[4,18,96,576]{3,2,1,0:T(8,128)(2,1)S(1)} %pad_maximum_fusion, bf16[3,3,576,192]{3,2,1,0:T(8,128)(2,1)S(1)} %bitcast.277), kind=kOutput, calls=%fused_computation.103 | convolution fusion | flops 679477248 | bytes 11501568 | tf_op jit(solution)/shard_map/fhwk,ko->fhwo/dot_general | solution.py:48
  156.0 9.6 %add_convert_fusion = bf16[2,16,96,192]{3,2,1,0:T(8,128)(2,1)} fusion(f32[2,16,96,192]{3,2,1,0:T(8,128)S(1)} %fusion.56, f32[2,16,96,192]{3,2,1,0:T(8,128)S(1)} %fusion.57, f32[2,16,96,192]{3,2,1,0:T(8,128)S(1)} %fusion.58, f32[2,16,96,192]{3,2,1,0:T(8,128)} %fusion.59, f32[2,16,96,192]{3,2,1,0:T(8,128)} %fusion.60, f32[2,16,96,192]{3,2,1,0:T(8,128)} %fusion.61, ...), kind=kOutput, calls=%fused_computation.15 | convolution fusion | flops 684785664 | bytes 32243712 | tf_op jit(solution)/shard_map/fhwk,ko->fhwo/dot_general | solution.py:48
  (23 shorter events, 0.2 us)
Async XLA Ops:
  0.6 59.4 %copy-start = (bf16[384,192]{0,1:T(8,128)(2,1)S(1)}, bf16[384,192]{0,1:T(8,128)(2,1)}, u32[]{:S(2)}) copy-start(bf16[384,192]{0,1:T(8,128)(2,1)} %param.13) | copy-start | bytes 442372
  3.4 16.1 %collective-permute-start = (bf16[2,8,48,384]{3,2,1,0:T(8,128)(2,1)S(1)}, bf16[2,8,48,384]{3,2,1,0:T(8,128)(2,1)S(1)}, u32[]{:S(2)}, u32[]{:S(2)}) collective-permute-start(bf16[2,8,48,384]{3,2,1,0:T(8,128)(2,1)S(1)} %fusion.36), channel_id=1, source_target_pairs={{0,64},{64,128},{128,192},{1,65},{65,129},{129,193},{2,66},{66,130... | collective-permute-start | bytes 1769480 | tf_op jit(solution)/shard_map/ppermute | solution.py:10
  19.6 10.7 %collective-permute-start.1 = (bf16[4,1,48,384]{3,2,1,0:T(8,128)(2,1)S(1)}, bf16[4,1,48,384]{3,2,1,0:T(8,128)(2,1)S(1)}, u32[]{:S(2)}, u32[]{:S(2)}) collective-permute-start(bf16[4,1,48,384]{3,2,1,0:T(8,128)(2,1)S(1)} %get-tuple-element.8), channel_id=1, source_target_pairs={{0,1},{1,2},{2,3},{3,4},{4,5},{5,6},{6,7},{7,8},{8,9},{9,10},{10,1... | collective-permute-start | bytes 442376 | tf_op jit(solution)/shard_map/ppermute | solution.py:18
  25.7 9.8 %collective-permute-start.2 = (bf16[4,1,48,384]{3,2,1,0:T(8,128)(2,1)S(1)}, bf16[4,1,48,384]{3,2,1,0:T(8,128)(2,1)S(1)}, u32[]{:S(2)}, u32[]{:S(2)}) collective-permute-start(bf16[4,1,48,384]{3,2,1,0:T(8,128)(2,1)S(1)} %get-tuple-element.9), channel_id=1, source_target_pairs={{1,0},{2,1},{3,2},{4,3},{5,4},{6,5},{7,6},{8,7},{9,8},{10,9},{11,1... | collective-permute-start | bytes 442376 | tf_op jit(solution)/shard_map/ppermute | solution.py:21
  43.3 1.1 copy-start.7
  43.4 16.7 %copy-start.2 = (bf16[2,8,48,384]{3,2,1,0:T(8,128)(2,1)S(1)}, bf16[2,8,48,384]{3,2,1,0:T(8,128)(2,1)}, u32[]{:S(2)}) copy-start(bf16[2,8,48,384]{3,2,1,0:T(8,128)(2,1)} %param.8) | copy-start | bytes 1769476
  44.7 8.5 %collective-permute-start.3 = (bf16[2,8,48,192]{3,2,1,0:T(8,128)(2,1)S(1)}, bf16[2,8,48,192]{3,2,1,0:T(8,128)(2,1)S(1)}, u32[]{:S(2)}, u32[]{:S(2)}) collective-permute-start(bf16[2,8,48,192]{3,2,1,0:T(8,128)(2,1)S(1)} %multiply_convert_fusion), channel_id=1, source_target_pairs={{0,64},{64,128},{128,192},{1,65},{65,129},{129,193},{2,66},{66,130... | collective-permute-start | bytes 884744 | tf_op jit(solution)/shard_map/ppermute | solution.py:10
  53.3 7.1 %collective-permute-start.4 = (bf16[4,1,48,192]{3,2,1,0:T(8,128)(2,1)S(1)}, bf16[4,1,48,192]{3,2,1,0:T(8,128)(2,1)S(1)}, u32[]{:S(2)}, u32[]{:S(2)}) collective-permute-start(bf16[4,1,48,192]{3,2,1,0:T(8,128)(2,1)S(1)} %get-tuple-element.12), channel_id=1, source_target_pairs={{0,1},{1,2},{2,3},{3,4},{4,5},{5,6},{6,7},{7,8},{8,9},{9,10},{10,1... | collective-permute-start | bytes 221192 | tf_op jit(solution)/shard_map/ppermute | solution.py:18
  57.9 9.3 %collective-permute-start.5 = (bf16[4,1,48,192]{3,2,1,0:T(8,128)(2,1)S(1)}, bf16[4,1,48,192]{3,2,1,0:T(8,128)(2,1)S(1)}, u32[]{:S(2)}, u32[]{:S(2)}) collective-permute-start(bf16[4,1,48,192]{3,2,1,0:T(8,128)(2,1)S(1)} %get-tuple-element.13), channel_id=1, source_target_pairs={{1,0},{2,1},{3,2},{4,3},{5,4},{6,5},{7,6},{8,7},{9,8},{10,9},{11,1... | collective-permute-start | bytes 221192 | tf_op jit(solution)/shard_map/ppermute | solution.py:21
  68.4 1.8 %copy-start.3 = (bf16[3,3,3,192,192]{4,3,2,1,0:T(8,128)(2,1)S(1)}, bf16[3,3,3,192,192]{4,3,2,1,0:T(8,128)(2,1)}, u32[]{:S(2)}) copy-start(bf16[3,3,3,192,192]{4,3,2,1,0:T(8,128)(2,1)} %param.12) | copy-start | bytes 5971972
  74.0 0.8 copy-start.6
  74.8 0.8 copy-start.5
  78.5 32.4 %collective-permute-start.6 = (bf16[2,16,96,192]{3,2,1,0:T(8,128)(2,1)S(1)}, bf16[2,16,96,192]{3,2,1,0:T(8,128)(2,1)S(1)}, u32[]{:S(2)}, u32[]{:S(2)}) collective-permute-start(bf16[2,16,96,192]{3,2,1,0:T(8,128)(2,1)S(1)} %reshape.49), channel_id=1, source_target_pairs={{0,64},{64,128},{128,192},{1,65},{65,129},{129,193},{2,66},{66,130... | collective-permute-start | bytes 3538952 | tf_op jit(solution)/shard_map/ppermute | solution.py:10
  111.2 7.3 %collective-permute-start.7 = (bf16[4,1,96,192]{3,2,1,0:T(8,128)(2,1)S(1)}, bf16[4,1,96,192]{3,2,1,0:T(8,128)(2,1)S(1)}, u32[]{:S(2)}, u32[]{:S(2)}) collective-permute-start(bf16[4,1,96,192]{3,2,1,0:T(8,128)(2,1)S(1)} %get-tuple-element.4), channel_id=1, source_target_pairs={{0,1},{1,2},{2,3},{3,4},{4,5},{5,6},{6,7},{7,8},{8,9},{9,10},{10,1... | collective-permute-start | bytes 442376 | tf_op jit(solution)/shard_map/ppermute | solution.py:18
  115.9 10.3 %collective-permute-start.8 = (bf16[4,1,96,192]{3,2,1,0:T(8,128)(2,1)S(1)}, bf16[4,1,96,192]{3,2,1,0:T(8,128)(2,1)S(1)}, u32[]{:S(2)}, u32[]{:S(2)}) collective-permute-start(bf16[4,1,96,192]{3,2,1,0:T(8,128)(2,1)S(1)} %get-tuple-element.5), channel_id=1, source_target_pairs={{1,0},{2,1},{3,2},{4,3},{5,4},{6,5},{7,6},{8,7},{9,8},{10,9},{11,1... | collective-permute-start | bytes 442376 | tf_op jit(solution)/shard_map/ppermute | solution.py:21
  130.8 5.6 %copy-start.4 = (bf16[3,3,3,192,192]{4,3,2,1,0:T(8,128)(2,1)S(1)}, bf16[3,3,3,192,192]{4,3,2,1,0:T(8,128)(2,1)}, u32[]{:S(2)}) copy-start(bf16[3,3,3,192,192]{4,3,2,1,0:T(8,128)(2,1)} %param.15) | copy-start | bytes 5971972
  156.0 9.6 %copy-start.1 = (bf16[384,192]{0,1:T(8,128)(2,1)S(1)}, bf16[384,192]{0,1:T(8,128)(2,1)}, u32[]{:S(2)}) copy-start(bf16[384,192]{0,1:T(8,128)(2,1)} %param.13) | copy-start | bytes 442372
where the time goes:
time: 166 us
  waiting for transfers between devices  68.6 us (41%)
  matrix products  40.7 us (25%)
  starting transfers between devices  30.1 us (18%)
  other arithmetic  14.4 us (9%)
  local copies, waits for them, and re-layouts  10.6 us (6%)
    ppermute x3, waiting for transfers between devices, from_behind(): lax.ppermute(value, axis, [(source, source + steps) for source in range(i...  48.3 us
    dot_general x27, matrix products, convolve(): jnp.einsum('fhwk,ko->fhwo', window, folded[offset_time, offset_row], pref...  40.3 us
    ppermute x3, waiting for transfers between devices, extended_2(): lax.ppermute(lax.slice_in_dim(block, 0, width, axis=dim), axis, backward)  19.6 us
    ppermute x3, starting transfers between devices, extended_2(): lax.ppermute(lax.slice_in_dim(block, block.shape[dim] - width, None, axis...  15.4 us
    ppermute x3, starting transfers between devices, from_behind(): lax.ppermute(value, axis, [(source, source + steps) for source in range(i...  8.73 us
    concatenate x3, other arithmetic, convolve(): jnp.concatenate([padded[:, :, 0:breadth], padded[:, :, 1:breadth + 1], pa...  7.63 us
    ppermute x3, starting transfers between devices, extended_2(): lax.ppermute(lax.slice_in_dim(block, 0, width, axis=dim), axis, backward)  5.94 us
    slice x3, local copies, waits for them, and re-layouts, convolve(): padded[:, :, 0:breadth]  4.24 us
  transfers between devices with their start and end apart: 9, of which 7 were waited for; matrix products, arithmetic and copies ran while one was open for 2% of the time, Pallas kernels for 0%

commit v1 on v0

v1 whole, which is shorter than its diff:
```python
import jax
import jax.numpy as jnp
from jax import lax
from jax.experimental import pallas as pl
from jax.experimental.pallas import tpu as pltpu
from jax.sharding import PartitionSpec as P

F32 = jnp.float32
BF16 = jnp.bfloat16
HALO = 3


def dot(a, b):
    return jnp.dot(a, b, preferred_element_type=F32)


def normed(v, gain):
    mean_square = jnp.mean(v * v, axis=-1, keepdims=True)
    u = v * lax.rsqrt(mean_square + 1e-06) * gain
    return u * (0.5 + 0.5 * jnp.tanh(0.5 * u))


def beside(v):
    width = v.shape[0]
    column = lax.broadcasted_iota(jnp.int32, v.shape, 0)
    left = jnp.where(column == 0, 0.0, pltpu.roll(v, 1, 0))
    right = jnp.where(column == width - 1, 0.0, pltpu.roll(v, width - 1, 0))
    return left, right


def call(kernel, out_shape, scratch, flops, nbytes, limit, *args):
    smem = pl.BlockSpec(memory_space=pltpu.SMEM)
    vmem = pl.BlockSpec(memory_space=pltpu.VMEM)
    return pl.pallas_call(
        kernel,
        out_shape=out_shape,
        in_specs=[smem] + [vmem] * (len(args) - 1),
        out_specs=jax.tree.map(lambda _: vmem, out_shape),
        scratch_shapes=scratch,
        compiler_params=pltpu.CompilerParams(vmem_limit_bytes=limit << 20),
        cost_estimate=pl.CostEstimate(flops=flops, bytes_accessed=nbytes, transcendentals=0),
    )(*args)


def pack_rows(ref, value):
    half = value.shape[1] // 2
    ref[:, :, :, 0:192] = value[:, :half].astype(BF16)
    ref[:, :, :, 192:384] = value[:, half:].astype(BF16)


def first_kernel(place, latents, near, far, gain, kernel, partial, cols, acc):
    frames, rows, width, channels = latents.shape
    tall = rows + 2 * HALO
    odd = place[1] % 2
    inner = jnp.logical_and(place[1] > 0, place[1] < place[3] - 1)

    def put(frame, row, values):
        v = normed(values.astype(F32), gain[...])
        left, right = beside(v)
        cols[frame, row, :, 0:channels] = left.astype(BF16)
        cols[frame, row, :, channels : 2 * channels] = v.astype(BF16)
        cols[frame, row, :, 2 * channels : 3 * channels] = right.astype(BF16)

    for frame in range(frames):
        @pl.loop(0, rows)
        def _(row):
            put(frame, row + HALO, latents[frame, row])

        @pl.loop(0, HALO)
        def _(row):
            put(frame, jnp.where(odd == 1, 0, tall - HALO) + row, near[frame, row])
            values = far[frame, row]
            put(
                frame,
                jnp.where(odd == 1, tall - HALO, 0) + row,
                jnp.where(inner, values, jnp.zeros_like(values)),
            )

    wide = tall - 2
    pixels = wide * width

    @pl.loop(0, 3)
    def _(b):
        window = cols[:, pl.ds(b, wide)].reshape(2 * pixels, 3 * channels)
        first = dot(window, kernel[0, b])
        second = dot(window[pixels:], kernel[1, b])

        @pl.when(b == 0)
        def _():
            acc[0] = first[:pixels] + second
            acc[1] = first[pixels:]

        @pl.when(b > 0)
        def _():
            acc[0] += first[:pixels] + second
            acc[1] += first[pixels:]

    pack_rows(partial, acc[...].reshape(2, wide, width, 192))


def first_own_kernel(place, cols, kernel, own):
    wide = cols.shape[1] - 2
    width = cols.shape[2]
    pixels = wide * width

    @pl.loop(0, 3)
    def _(b):
        window = cols[:, pl.ds(b, wide)].reshape(2 * pixels, cols.shape[3])
        last = dot(window, kernel[2, b])
        middle = dot(window[:pixels], kernel[1, b])

        @pl.when(b == 0)
        def _():
            own[0] = last[:pixels]
            own[1] = last[pixels:] + middle

        @pl.when(b > 0)
        def _():
            own[0] += last[:pixels]
            own[1] += last[pixels:] + middle


def three(window, kernel, a, b):
    total = dot(window[0], kernel[a, b, 0])
    total += dot(window[1], kernel[a, b, 1])
    return total + dot(window[2], kernel[a, b, 2])


def second_kernel(place, own, before, gain, kernel, partial, cols, acc):
    frames = own.shape[0]
    half, width = before.shape[1], before.shape[2]
    tall = 2 * half
    beyond = (tall - 8) // 2
    start = place[1] * 8 - beyond
    follows = place[0] > 0

    for frame in range(frames):
        @pl.loop(0, half)
        def _(row):
            pair = before[frame, row].astype(F32)
            for side in range(2):
                at = row + side * half
                earlier = jnp.where(follows, pair[:, 192 * side : 192 * side + 192], 0.0)
                first_out = (own[frame, pl.ds(at * width, width)] + earlier).astype(BF16)
                inside = jnp.logical_and(start + at >= 0, start + at < place[3] * 8)
                v = jnp.where(inside, normed(first_out.astype(F32), gain[...]), 0.0)
                left, right = beside(v)
                cols[0, frame, at] = left.astype(BF16)
                cols[1, frame, at] = v.astype(BF16)
                cols[2, frame, at] = right.astype(BF16)

    wide = tall - 2
    pixels = wide * width

    @pl.loop(0, 3)
    def _(b):
        window = [cols[e, :, pl.ds(b, wide)].reshape(2 * pixels, 192) for e in range(3)]
        first = three(window, kernel, 0, b)
        second = three([w[pixels:] for w in window], kernel, 1, b)

        @pl.when(b == 0)
        def _():
            acc[0] = first[:pixels] + second
            acc[1] = first[pixels:]

        @pl.when(b > 0)
        def _():
            acc[0] += first[:pixels] + second
            acc[1] += first[pixels:]

    pack_rows(partial, acc[...].reshape(2, wide, width, 192))


def second_own_kernel(place, cols, kernel, latents, near, far, shortcut, own):
    wide = cols.shape[2] - 2
    width = cols.shape[3]
    pixels = wide * width
    rows, channels = latents.shape[1], latents.shape[3]
    odd = place[1] % 2
    inner = wide - 1

    @pl.loop(0, 3)
    def _(b):
        window = [cols[e, :, pl.ds(b, wide)].reshape(2 * pixels, 192) for e in range(3)]
        last = three(window, kernel, 2, b)
        middle = three([w[:pixels] for w in window], kernel, 1, b)

        @pl.when(b == 0)
        def _():
            own[0] = last[:pixels]
            own[1] = last[pixels:] + middle

        @pl.when(b > 0)
        def _():
            own[0] += last[:pixels]
            own[1] += last[pixels:] + middle

    for frame in range(2):
        body = latents[frame].reshape(rows * width, channels)
        own[frame, width : pixels - width] += dot(body, shortcut[...])
        other = dot(near[frame, jnp.where(odd == 1, HALO - 1, 0)], shortcut[...])
        own[frame, pl.ds(jnp.where(odd == 1, 0, inner * width), width)] += other
        other = dot(far[frame, jnp.where(odd == 1, 0, HALO - 1)], shortcut[...])
        own[frame, pl.ds(jnp.where(odd == 1, inner * width, 0), width)] += other


def third_kernel(place, own, before, gain, block_out, packed, active):
    half, width = before.shape[1], before.shape[2]
    tall = 2 * half
    start = place[1] * 8 - 1
    follows = place[0] > 0
    for frame in range(2):
        for row in range(half):
            pair = before[frame, row].astype(F32)
            for side in range(2):
                at = row + side * half
                earlier = jnp.where(follows, pair[:, 192 * side : 192 * side + 192], 0.0)
                total = (own[frame, at * width : (at + 1) * width] + earlier).astype(BF16)
                if 0 < at < tall - 1:
                    block_out[frame, at - 1] = total
                v = normed(total.astype(F32), gain[...])
                if at in (0, tall - 1):
                    inside = jnp.logical_and(start + at >= 0, start + at < place[3] * 8)
                    v = jnp.where(inside, v, 0.0)
                v = v.astype(BF16)
                active[frame, at] = v
                packed[frame, row, :, 192 * side : 192 * side + 192] = v


def weights_kernel(place, kernel, out):
    for a in range(3):
        by_row = []
        for b in range(3):
            k = [kernel[a, b, e].astype(F32) for e in range(3)]
            by_row.append((-k[0], k[0] + k[1] + k[2], k[2]))
        for q in range(3):
            out[a, 0, q] = (-by_row[0][q]).astype(BF16)
            out[a, 1, q] = (by_row[0][q] + by_row[1][q] + by_row[2][q]).astype(BF16)
            out[a, 2, q] = by_row[2][q].astype(BF16)


def differences(get, level, steps, frame, tall):
    last = None
    for at in range(tall):
        v = get(at).astype(F32)
        left, right = beside(v)
        now = (v - left, v, right - v)
        for q in range(3):
            if 0 < at < tall - 1:
                level[q, frame, at - 1] = now[q].astype(BF16)
            if at > 0:
                steps[q, frame, at - 1] = (now[q] - last[q]).astype(BF16)
        last = now


def products(level, steps, kernel, taps, rows, width, p, q):
    total = None
    for frame, a in taps:
        if p == 1:
            window = level[q, frame]
        else:
            window = steps[q, frame, 0:rows] if p == 0 else steps[q, frame, 1 : rows + 1]
        term = dot(window.reshape(rows * width, 192), kernel[a, p, q])
        total = term if total is None else total + term
    return total


def phases(level, steps, kernel, taps, rows, width):
    by = []
    for q in range(3):
        m = [products(level, steps, kernel, taps, rows, width, p, q) for p in range(3)]
        by.append((m[1] + m[0], m[1] + m[2]))
    return [[by[1][i] + by[0][i], by[1][i] + by[2][i]] for i in range(2)]


def third_own_kernel(place, active, kernel, own, level, steps):
    rows, width = active.shape[1] - 2, active.shape[2]
    for frame in range(2):
        differences(lambda at: active[frame, at], level, steps, frame, rows + 2)
    for out, taps in ((0, ((0, 2),)), (1, ((0, 1), (1, 2)))):
        result = phases(level, steps, kernel, taps, rows, width)
        for i in range(2):
            for j in range(2):
                own[out, 2 * i + j] = result[i][j]


def last_kernel(place, packed, kernel, own, decoded, level, steps, woven):
    half, width = packed.shape[1], packed.shape[2]
    tall = 2 * half
    rows = tall - 2
    follows = place[0] > 0

    for frame in range(2):
        def get(at):
            side, row = divmod(at, half)
            v = packed[frame, row, :, 192 * side : 192 * side + 192]
            return jnp.where(follows, v, jnp.zeros_like(v))

        differences(get, level, steps, frame, tall)
    for out, taps in ((0, ((0, 0), (1, 1))), (1, ((1, 0),))):
        result = phases(level, steps, kernel, taps, rows, width)
        for i in range(2):
            for j in range(2):
                own[out, 2 * i + j] += result[i][j]

        @pl.loop(0, rows)
        def _(row):
            for i in range(2):
                for j in range(2):
                    value = own[out, 2 * i + j, pl.ds(row * width, width)]
                    woven[i, 0, pl.ds(j, width, stride=2)] = value[:, 0:128]
                    woven[i, 1, pl.ds(j, width, stride=2), 0:64] = value[:, 128:192]
                decoded[out, 2 * row + i, :, 0:128] = woven[i, 0].astype(BF16)
                decoded[out, 2 * row + i, :, 128:192] = woven[i, 1, :, 0:64].astype(BF16)


def onward(value):
    count = lax.axis_size("tm")
    return lax.ppermute(value, "tm", [(i, (i + 1) % count) for i in range(count)])


def swap(value, offset):
    count = lax.axis_size("rows")
    pairs = [((2 * i + offset) % count, (2 * i + 1 + offset) % count) for i in range(count // 2)]
    return lax.ppermute(value, "rows", pairs + [(b, a) for a, b in pairs])


def body(
    latents,
    gain_first,
    kernel_first,
    gain_second,
    kernel_second,
    shortcut,
    gain_third,
    kernel_third,
):
    frames, rows, width, channels = latents.shape
    group, slab = lax.axis_index("tm"), lax.axis_index("rows")
    place = jnp.stack(
        [group, slab, jnp.int32(lax.axis_size("tm")), jnp.int32(lax.axis_size("rows"))]
    ).astype(jnp.int32)
    odd = slab % 2
    near = swap(lax.dynamic_slice_in_dim(latents, (rows - HALO) * (1 - odd), HALO, 1), 0)
    far = swap(lax.dynamic_slice_in_dim(latents, (rows - HALO) * odd, HALO, 1), 1)

    shape = jax.ShapeDtypeStruct
    wide1, wide2 = rows + 4, rows + 2
    pixels1, pixels2 = wide1 * width, wide2 * width
    folded = kernel_first.reshape(3, 3, 3 * channels, 192)
    partial, cols = call(
        first_kernel,
        (shape((2, wide1 // 2, width, 384), BF16), shape((2, wide1 + 2, width, 3 * channels), BF16)),
        [pltpu.VMEM((2, pixels1, 192), F32)],
        6 * 9 * pixels1 * channels * 192,
        8 << 20,
        40,
        place, latents, near, far, gain_first.reshape(1, -1), folded,
    )
    before = onward(partial)
    own = call(
        first_own_kernel,
        shape((2, pixels1, 192), F32),
        [],
        6 * 9 * pixels1 * channels * 192,
        8 << 20,
        40,
        place, cols, folded,
    )
    mixed = call(
        weights_kernel, shape((3, 3, 3, 192, 192), BF16), [], 1 << 24, 4 << 20, 40, place, kernel_third
    )
    partial, cols = call(
        second_kernel,
        (shape((2, wide2 // 2, width, 384), BF16), shape((3, 2, wide1, width, 192), BF16)),
        [pltpu.VMEM((2, pixels2, 192), F32)],
        6 * 9 * pixels2 * 192 * 192,
        8 << 20,
        40,
        place, own, before, gain_second.reshape(1, -1), kernel_second,
    )
    before = onward(partial)
    own = call(
        second_own_kernel,
        shape((2, pixels2, 192), F32),
        [],
        6 * 9 * pixels2 * 192 * 192,
        8 << 20,
        40,
        place, cols, kernel_second, latents, near, far, shortcut,
    )
    block_out, packed, active = call(
        third_kernel,
        (
            shape((2, rows, width, 192), BF16),
            shape((2, wide2 // 2, width, 384), BF16),
            shape((2, wide2, width, 192), BF16),
        ),
        [],
        1 << 24,
        4 << 20,
        40,
        place, own, before, gain_third.reshape(1, -1),
    )
    before = onward(packed)
    scratch = [
        pltpu.VMEM((3, 2, rows, width, 192), BF16),
        pltpu.VMEM((3, 2, rows + 1, width, 192), BF16),
    ]
    own = call(
        third_own_kernel,
        shape((2, 4, rows * width, 192), F32),
        scratch,
        6 * 9 * rows * width * 192 * 192,
        8 << 20,
        40,
        place, active, mixed,
    )
    decoded = call(
        last_kernel,
        shape((2, 2 * rows, 2 * width, 192), BF16),
        scratch + [pltpu.VMEM((2, 2, 2 * width, 128), F32)],
        6 * 9 * rows * width * 192 * 192,
        8 << 20,
        40,
        place, before, mixed, own,
    )
    return (block_out, decoded)


def solution(mesh):
    return jax.shard_map(
        body,
        mesh=mesh,
        in_specs=(P("tm", "rows", None, None), P(), P(), P(), P(), P(), P(), P()),
        out_specs=(P("tm", "rows", None, None), P("tm", "rows", None, None)),
        check_vma=False,
    )
```

time: 166 us -> 74.9 us (0.45)
  the two profiles are of different devices: /device:TPU:119 before, /device:TPU:102 now
where the time goes in v1:
time: 74.9 us; the launch traced here: 74.5 us
  Pallas kernels  34 us (45%)
  waiting for transfers between devices  18.9 us (25%)
  local copies, waits for them, and re-layouts  17.6 us (23%)
  starting transfers between devices  3.12 us (4%)
  between operations  0.77 us (1%)
    pallas_call x8, Pallas kernels, call(): pl.pallas_call(kernel, out_shape=out_shape, in_specs=[smem] + [vmem] * (l...  34 us
    ppermute x3, waiting for transfers between devices, onward(): lax.ppermute(value, 'tm', [(i, (i + 1) % count) for i in range(count)])  18.8 us
    unnamed x30, local copies, waits for them, and re-layouts  16.5 us
    ppermute x3, starting transfers between devices, onward(): lax.ppermute(value, 'tm', [(i, (i + 1) % count) for i in range(count)])  2.09 us
  transfers between devices with their start and end apart: 5, of which 3 were waited for; matrix products, arithmetic and copies ran while one was open for 13% of the time, Pallas kernels for 16%

profile of v1, /device:TPU:102, one launch (start us, length us, event | category | flops | bytes accessed | tf_op | source)
XLA Modules:
  0.0 74.5 jit_solution(11165554666050302716)
XLA Ops:
  0.7 1.1 %constant_dynamic-slice_fusion = (bf16[2,3,48,384]{3,2,1,0:T(8,128)(2,1)S(1)}, bf16[2,3,48,384]{3,2,1,0:T(8,128)(2,1)S(1)}) fusion(bf16[2,8,48,384]{3,2,1,0:T(8,128)(2,1)} %latents.3, s32[]{:T(128)S(6)} %select_n.15, s32[]{:T(128)S(6)} %select_n.14), kind=kLoop, calls=%fused_computation.1 | loop fusion | bytes 884744 | tf_op jit(solution)/shard_map/dynamic_slice | solution.py:345
  1.8 0.1 collective-permute-start
  1.9 0.9 %collective-permute-start.1 = (bf16[2,3,48,384]{3,2,1,0:T(8,128)(2,1)S(1)}, bf16[2,3,48,384]{3,2,1,0:T(8,128)(2,1)S(1)}, u32[]{:S(2)}, u32[]{:S(2)}) collective-permute-start(bf16[2,3,48,384]{3,2,1,0:T(8,128)(2,1)S(1)} %get-tuple-element.16), channel_id=1, source_target_pairs={{1,2},{3,4},{5,6},{7,8},{9,10},{11,12},{13,14},{15,16},{17,18},{19... | collective-permute-start | bytes 663560 | tf_op jit(solution)/shard_map/ppermute | solution.py:325
  2.8 0.0 copy-start.13
  2.8 0.0 copy-start.4
  2.8 8.2 %copy.10 = bf16[3,3,3,384,192]{4,3,2,1,0:T(8,128)(2,1)} copy(bf16[3,3,3,384,192]{3,4,2,1,0:T(8,128)(2,1)} %param.10) | data formatting | bytes 7962624 | tf_op args[2]
  11.0 0.0 copy-done.13
  11.0 0.1 pad_add_fusion.place
  11.1 0.0 collective-permute-done.near
  11.1 0.0 copy-start.7
  11.1 0.0 collective-permute-done.1.far
  11.1 0.0 copy-start.9
  11.1 0.0 copy-done.4
  11.1 0.0 copy-start
  11.1 2.6 %copy-done = bf16[3,3,3,384,192]{4,3,2,1,0:T(8,128)(2,1)S(1)} copy-done((bf16[3,3,3,384,192]{4,3,2,1,0:T(8,128)(2,1)S(1)}, bf16[3,3,3,384,192]{4,3,2,1,0:T(8,128)(2,1)}, u32[]{:S(2)}) %copy-start) | copy-done | bytes 3981336
  13.8 0.0 copy-start.1
  13.8 8.0 %shard_map.95 = (bf16[2,6,48,384]{3,2,1,0:T(8,128)(2,1)S(1)}, bf16[2,14,48,1152]{3,2,1,0:T(8,128)(2,1)S(1)}) custom-call(s32[4]{0:T(128)S(1)} %pad_add_fusion.place, bf16[2,8,48,384]{3,2,1,0:T(8,128)(2,1)S(1)} %copy-done.4, bf16[2,3,48,384]{3,2,1,0:T(8,128)(2,1)S(1)} %collective-permute-done.near, bf16[2,3,48,384]{3,2,1,0:T(8,128)(2,1)S(1)} %collective-permute-done.1.far, ...), custom_call_target="tpu_custom_call" | custom-call | flops 2293235712 | bytes 8388608 | tf_op jit(solution)/shard_map/pallas_call | solution.py:34
  21.8 0.0 copy-done.7
  21.8 0.0 copy-done.9
  21.8 1.7 %collective-permute-start.2 = (bf16[2,6,48,384]{3,2,1,0:T(8,128)(2,1)S(1)}, bf16[2,6,48,384]{3,2,1,0:T(8,128)(2,1)S(1)}, u32[]{:S(2)}, u32[]{:S(2)}) collective-permute-start(bf16[2,6,48,384]{3,2,1,0:T(8,128)(2,1)S(1)} %get-tuple-element.10), channel_id=1, source_target_pairs={{0,64},{64,128},{128,192},{192,0},{1,65},{65,129},{129,193},{193,1... | collective-permute-start | bytes 1327112 | tf_op jit(solution)/shard_map/ppermute | solution.py:319
  23.5 0.0 copy-done.1
  23.5 0.0 copy-start.2
  23.5 0.0 copy-start.11
  23.5 4.9 %shard_map.96.own = f32[2,576,192]{2,1,0:T(8,128)S(1)} custom-call(s32[4]{0:T(128)S(1)} %pad_add_fusion.place, bf16[2,14,48,1152]{3,2,1,0:T(8,128)(2,1)S(1)} %get-tuple-element.9.cols, bf16[3,3,1152,192]{3,2,1,0:T(8,128)(2,1)S(1)} %bitcast.6), custom_call_target="tpu_custom_call" | custom-call | flops 2293235712 | bytes 8388608 | tf_op jit(solution)/shard_map/pallas_call | solution.py:34
  28.4 6.3 %collective-permute-done.2.before = bf16[2,6,48,384]{3,2,1,0:T(8,128)(2,1)S(1)} collective-permute-done((bf16[2,6,48,384]{3,2,1,0:T(8,128)(2,1)S(1)}, bf16[2,6,48,384]{3,2,1,0:T(8,128)(2,1)S(1)}, u32[]{:S(2)}, u32[]{:S(2)}) %collective-permute-start.2) | collective-permute-done | bytes 442400 | tf_op jit(solution)/shard_map/ppermute | solution.py:319
  34.7 0.0 copy-done.2
  34.7 0.0 copy-done.11
  34.7 6.2 %shard_map.97 = (bf16[2,5,48,384]{3,2,1,0:T(8,128)(2,1)}, bf16[3,2,12,48,192]{4,3,2,1,0:T(8,128)(2,1)S(1)}) custom-call(s32[4]{0:T(128)S(1)} %pad_add_fusion.place, f32[2,576,192]{2,1,0:T(8,128)S(1)} %shard_map.96.own, bf16[2,6,48,384]{3,2,1,0:T(8,128)(2,1)S(1)} %collective-permute-done.2.before, f32[1,192]{1,0:T(1,128)S(1)} %bitcast.7, ...), custom_call_target="tpu_custom_call" | custom-call | flops 955514880 | bytes 8388608 | tf_op jit(solution)/shard_map/pallas_call | solution.py:34
  40.9 0.0 copy-start.5
  40.9 1.2 %copy-done.5 = bf16[3,2,12,48,192]{4,3,2,1,0:T(8,128)(2,1)} copy-done((bf16[3,2,12,48,192]{4,3,2,1,0:T(8,128)(2,1)}, bf16[3,2,12,48,192]{4,3,2,1,0:T(8,128)(2,1)S(1)}, u32[]{:S(2)}) %copy-start.5) | copy-done | bytes 1327128
  42.2 0.4 collective-permute-start.3
  42.6 1.0 %copy.11.shortcut = bf16[384,192]{1,0:T(8,128)(2,1)S(1)} copy(bf16[384,192]{0,1:T(8,128)(2,1)} %param.13) | data formatting | bytes 294912 | tf_op args[5]
  43.6 0.0 copy-start.6
  43.6 1.5 %copy-done.6 = bf16[3,2,12,48,192]{4,3,2,1,0:T(8,128)(2,1)S(1)} copy-done((bf16[3,2,12,48,192]{4,3,2,1,0:T(8,128)(2,1)S(1)}, bf16[3,2,12,48,192]{4,3,2,1,0:T(8,128)(2,1)}, u32[]{:S(2)}) %copy-start.6) | copy-done | bytes 1327128
  45.1 0.0 copy-start.8
  45.1 0.9 %copy-done.8 = bf16[2,3,48,384]{3,2,1,0:T(8,128)(2,1)S(1)} copy-done((bf16[2,3,48,384]{3,2,1,0:T(8,128)(2,1)S(1)}, bf16[2,3,48,384]{3,2,1,0:T(8,128)(2,1)}, u32[]{:S(2)}) %copy-start.8) | copy-done | bytes 221208
  46.1 0.0 copy-start.10
  46.1 0.9 %copy-done.10 = bf16[2,3,48,384]{3,2,1,0:T(8,128)(2,1)S(1)} copy-done((bf16[2,3,48,384]{3,2,1,0:T(8,128)(2,1)S(1)}, bf16[2,3,48,384]{3,2,1,0:T(8,128)(2,1)}, u32[]{:S(2)}) %copy-start.10) | copy-done | bytes 221208
  47.0 0.0 copy-start.12
  47.0 0.0 copy-start.3
  47.0 3.6 %shard_map.98.own = f32[2,480,192]{2,1,0:T(8,128)S(1)} custom-call(s32[4]{0:T(128)S(1)} %pad_add_fusion.place, bf16[3,2,12,48,192]{4,3,2,1,0:T(8,128)(2,1)S(1)} %copy-done.6, bf16[3,3,3,192,192]{4,3,2,1,0:T(8,128)(2,1)S(1)} %copy-done.2, bf16[2,8,48,384]{3,2,1,0:T(8,128)(2,1)S(1)} %copy-done.4, bf16[2,3,48,384]{3,2,1,0:T(8,128)(2,1)S(1)} %copy-done.8, ...), custom_call_target="tpu_custom_call" | custom-call | flops 955514880 | bytes 8388608 | tf_op jit(solution)/shard_map/pallas_call | solution.py:34
  50.6 4.2 %collective-permute-done.3.before = bf16[2,5,48,384]{3,2,1,0:T(8,128)(2,1)} collective-permute-done((bf16[2,5,48,384]{3,2,1,0:T(8,128)(2,1)}, bf16[2,5,48,384]{3,2,1,0:T(8,128)(2,1)}, u32[]{:S(2)}, u32[]{:S(2)}) %collective-permute-start.3) | collective-permute-done | bytes 368672 | tf_op jit(solution)/shard_map/ppermute | solution.py:319
  54.8 0.0 copy-done.12
  54.8 3.2 %shard_map.99 = (bf16[2,8,48,192]{3,2,1,0:T(8,128)(2,1)}, bf16[2,5,48,384]{3,2,1,0:T(8,128)(2,1)S(1)}, bf16[2,10,48,192]{3,2,1,0:T(8,128)(2,1)S(1)}) custom-call(s32[4]{0:T(128)S(1)} %pad_add_fusion.place, f32[2,480,192]{2,1,0:T(8,128)S(1)} %shard_map.98.own, bf16[2,5,48,384]{3,2,1,0:T(8,128)(2,1)} %collective-permute-done.3.before, f32[1,192]{1,0:T(1,128)S(1)} %bitcast.8), custom_call_target="tpu_custom_call" | custom-call | flops 16777216 | bytes 4194304 | tf_op jit(solution)/shard_map/pallas_call | solution.py:34
  58.0 0.0 collective-permute-start.4
  58.0 0.0 copy-done.3
  58.0 1.3 %shard_map.100.kernel = bf16[3,3,3,192,192]{4,3,2,1,0:T(8,128)(2,1)S(1)} custom-call(s32[4]{0:T(128)S(1)} %pad_add_fusion.place, bf16[3,3,3,192,192]{4,3,2,1,0:T(8,128)(2,1)S(1)} %copy-done.3), custom_call_target="tpu_custom_call" | custom-call | flops 16777216 | bytes 4194304 | tf_op jit(solution)/shard_map/pallas_call | solution.py:34
  59.2 2.3 %shard_map.101.own = f32[2,4,384,192]{3,2,1,0:T(8,128)S(1)} custom-call(s32[4]{0:T(128)S(1)} %pad_add_fusion.place, bf16[2,10,48,192]{3,2,1,0:T(8,128)(2,1)S(1)} %get-tuple-element.15.active, bf16[3,3,3,192,192]{4,3,2,1,0:T(8,128)(2,1)S(1)} %shard_map.100.kernel), custom_call_target="tpu_custom_call" | custom-call | flops 764411904 | bytes 8388608 | tf_op jit(solution)/shard_map/pallas_call | solution.py:34
  61.5 8.3 %collective-permute-done.4.packed = bf16[2,5,48,384]{3,2,1,0:T(8,128)(2,1)S(1)} collective-permute-done((bf16[2,5,48,384]{3,2,1,0:T(8,128)(2,1)S(1)}, bf16[2,5,48,384]{3,2,1,0:T(8,128)(2,1)S(1)}, u32[]{:S(2)}, u32[]{:S(2)}) %collective-permute-start.4) | collective-permute-done | bytes 368672 | tf_op jit(solution)/shard_map/ppermute | solution.py:319
  69.8 4.6 %shard_map.102 = bf16[2,16,96,192]{3,2,1,0:T(8,128)(2,1)} custom-call(s32[4]{0:T(128)S(1)} %pad_add_fusion.place, bf16[2,5,48,384]{3,2,1,0:T(8,128)(2,1)S(1)} %collective-permute-done.4.packed, bf16[3,3,3,192,192]{4,3,2,1,0:T(8,128)(2,1)S(1)} %shard_map.100.kernel, f32[2,4,384,192]{3,2,1,0:T(8,128)S(1)} %shard_map.101.own), custom_call_target="tpu_custom_call" | custom-call | flops 764411904 | bytes 8388608 | tf_op jit(solution)/shard_map/pallas_call | solution.py:34
  (1 shorter events, 0.0 us)
Async XLA Ops:
  1.8 9.3 %collective-permute-start = (bf16[2,3,48,384]{3,2,1,0:T(8,128)(2,1)S(1)}, bf16[2,3,48,384]{3,2,1,0:T(8,128)(2,1)S(1)}, u32[]{:S(2)}, u32[]{:S(2)}) collective-permute-start(bf16[2,3,48,384]{3,2,1,0:T(8,128)(2,1)S(1)} %get-tuple-element.17), channel_id=1, source_target_pairs={{0,1},{2,3},{4,5},{6,7},{8,9},{10,11},{12,13},{14,15},{16,17},{18,... | collective-permute-start | bytes 663560 | tf_op jit(solution)/shard_map/ppermute | solution.py:325
  1.9 9.2 %collective-permute-start.1 = (bf16[2,3,48,384]{3,2,1,0:T(8,128)(2,1)S(1)}, bf16[2,3,48,384]{3,2,1,0:T(8,128)(2,1)S(1)}, u32[]{:S(2)}, u32[]{:S(2)}) collective-permute-start(bf16[2,3,48,384]{3,2,1,0:T(8,128)(2,1)S(1)} %get-tuple-element.16), channel_id=1, source_target_pairs={{1,2},{3,4},{5,6},{7,8},{9,10},{11,12},{13,14},{15,16},{17,18},{19... | collective-permute-start | bytes 663560 | tf_op jit(solution)/shard_map/ppermute | solution.py:325
  2.8 8.2 %copy-start.13 = (f32[384]{0:T(512)S(1)}, f32[384]{0:T(512)}, u32[]{:S(2)}) copy-start(f32[384]{0:T(512)} %param.9) | copy-start | bytes 4612
  2.8 8.3 %copy-start.4 = (bf16[2,8,48,384]{3,2,1,0:T(8,128)(2,1)S(1)}, bf16[2,8,48,384]{3,2,1,0:T(8,128)(2,1)}, u32[]{:S(2)}) copy-start(bf16[2,8,48,384]{3,2,1,0:T(8,128)(2,1)} %latents.3) | copy-start | bytes 1769476
  11.1 10.7 %copy-start.7 = (bf16[2,3,48,384]{3,2,1,0:T(8,128)(2,1)}, bf16[2,3,48,384]{3,2,1,0:T(8,128)(2,1)S(1)}, u32[]{:S(2)}) copy-start(bf16[2,3,48,384]{3,2,1,0:T(8,128)(2,1)S(1)} %collective-permute-done.near) | copy-start | bytes 663556
  11.1 10.7 %copy-start.9 = (bf16[2,3,48,384]{3,2,1,0:T(8,128)(2,1)}, bf16[2,3,48,384]{3,2,1,0:T(8,128)(2,1)S(1)}, u32[]{:S(2)}) copy-start(bf16[2,3,48,384]{3,2,1,0:T(8,128)(2,1)S(1)} %collective-permute-done.1.far) | copy-start | bytes 663556
  11.1 2.7 %copy-start = (bf16[3,3,3,384,192]{4,3,2,1,0:T(8,128)(2,1)S(1)}, bf16[3,3,3,384,192]{4,3,2,1,0:T(8,128)(2,1)}, u32[]{:S(2)}) copy-start(bf16[3,3,3,384,192]{4,3,2,1,0:T(8,128)(2,1)} %copy.10) | copy-start | bytes 11943940
  13.8 9.7 %copy-start.1 = (bf16[3,3,3,384,192]{4,3,2,1,0:T(8,128)(2,1)S(1)}, bf16[3,3,3,384,192]{4,3,2,1,0:T(8,128)(2,1)}, u32[]{:S(2)}) copy-start(bf16[3,3,3,384,192]{4,3,2,1,0:T(8,128)(2,1)} %copy.10) | copy-start | bytes 11943940
  21.8 12.9 %collective-permute-start.2 = (bf16[2,6,48,384]{3,2,1,0:T(8,128)(2,1)S(1)}, bf16[2,6,48,384]{3,2,1,0:T(8,128)(2,1)S(1)}, u32[]{:S(2)}, u32[]{:S(2)}) collective-permute-start(bf16[2,6,48,384]{3,2,1,0:T(8,128)(2,1)S(1)} %get-tuple-element.10), channel_id=1, source_target_pairs={{0,64},{64,128},{128,192},{192,0},{1,65},{65,129},{129,193},{193,1... | collective-permute-start | bytes 1327112 | tf_op jit(solution)/shard_map/ppermute | solution.py:319
  23.5 11.2 %copy-start.2 = (bf16[3,3,3,192,192]{4,3,2,1,0:T(8,128)(2,1)S(1)}, bf16[3,3,3,192,192]{4,3,2,1,0:T(8,128)(2,1)}, u32[]{:S(2)}) copy-start(bf16[3,3,3,192,192]{4,3,2,1,0:T(8,128)(2,1)} %kernel.4) | copy-start | bytes 5971972
  23.5 11.2 %copy-start.11 = (f32[192]{0:T(256)S(1)}, f32[192]{0:T(256)}, u32[]{:S(2)}) copy-start(f32[192]{0:T(256)} %param.11) | copy-start | bytes 2308
  40.9 1.2 %copy-start.5 = (bf16[3,2,12,48,192]{4,3,2,1,0:T(8,128)(2,1)}, bf16[3,2,12,48,192]{4,3,2,1,0:T(8,128)(2,1)S(1)}, u32[]{:S(2)}) copy-start(bf16[3,2,12,48,192]{4,3,2,1,0:T(8,128)(2,1)S(1)} %get-tuple-element.11.cols) | copy-start | bytes 3981316
  42.2 12.7 %collective-permute-start.3 = (bf16[2,5,48,384]{3,2,1,0:T(8,128)(2,1)}, bf16[2,5,48,384]{3,2,1,0:T(8,128)(2,1)}, u32[]{:S(2)}, u32[]{:S(2)}) collective-permute-start(bf16[2,5,48,384]{3,2,1,0:T(8,128)(2,1)} %get-tuple-element.12), channel_id=1, source_target_pairs={{0,64},{64,128},{128,192},{192,0},{1,65},{65,129},{129,193},{193,1... | collective-permute-start | bytes 1105928 | tf_op jit(solution)/shard_map/ppermute | solution.py:319
  43.6 1.5 %copy-start.6 = (bf16[3,2,12,48,192]{4,3,2,1,0:T(8,128)(2,1)S(1)}, bf16[3,2,12,48,192]{4,3,2,1,0:T(8,128)(2,1)}, u32[]{:S(2)}) copy-start(bf16[3,2,12,48,192]{4,3,2,1,0:T(8,128)(2,1)} %copy-done.5) | copy-start | bytes 3981316
  45.1 0.9 %copy-start.8 = (bf16[2,3,48,384]{3,2,1,0:T(8,128)(2,1)S(1)}, bf16[2,3,48,384]{3,2,1,0:T(8,128)(2,1)}, u32[]{:S(2)}) copy-start(bf16[2,3,48,384]{3,2,1,0:T(8,128)(2,1)} %copy-done.7) | copy-start | bytes 663556
  46.1 0.9 %copy-start.10 = (bf16[2,3,48,384]{3,2,1,0:T(8,128)(2,1)S(1)}, bf16[2,3,48,384]{3,2,1,0:T(8,128)(2,1)}, u32[]{:S(2)}) copy-start(bf16[2,3,48,384]{3,2,1,0:T(8,128)(2,1)} %copy-done.9) | copy-start | bytes 663556
  47.0 7.8 %copy-start.12 = (f32[192]{0:T(256)S(1)}, f32[192]{0:T(256)}, u32[]{:S(2)}) copy-start(f32[192]{0:T(256)} %param.14) | copy-start | bytes 2308
  47.0 11.0 %copy-start.3 = (bf16[3,3,3,192,192]{4,3,2,1,0:T(8,128)(2,1)S(1)}, bf16[3,3,3,192,192]{4,3,2,1,0:T(8,128)(2,1)}, u32[]{:S(2)}) copy-start(bf16[3,3,3,192,192]{4,3,2,1,0:T(8,128)(2,1)} %kernel.5) | copy-start | bytes 5971972
  58.0 11.8 %collective-permute-start.4 = (bf16[2,5,48,384]{3,2,1,0:T(8,128)(2,1)S(1)}, bf16[2,5,48,384]{3,2,1,0:T(8,128)(2,1)S(1)}, u32[]{:S(2)}, u32[]{:S(2)}) collective-permute-start(bf16[2,5,48,384]{3,2,1,0:T(8,128)(2,1)S(1)} %get-tuple-element.14), channel_id=1, source_target_pairs={{0,64},{64,128},{128,192},{192,0},{1,65},{65,129},{129,193},{193,1... | collective-permute-start | bytes 1105928 | tf_op jit(solution)/shard_map/ppermute | solution.py:319

commit v2 on v0

v2 whole, which is shorter than its diff:
```python
import jax
import jax.numpy as jnp
from jax import lax
from jax.experimental import pallas as pl
from jax.experimental.pallas import tpu as pltpu
from jax.sharding import PartitionSpec as P

F32 = jnp.float32
BF16 = jnp.bfloat16
HALO = 3
LIMIT = 24


def dot(a, b):
    return jnp.dot(a, b, preferred_element_type=F32)


def dot_t(a, b):
    return lax.dot_general(a, b, (((1,), (1,)), ((), ())), preferred_element_type=F32)


def spans(channels):
    return [(at, min(128, channels - at)) for at in range(0, channels, 128)]


def scales(squares, channels):
    total = dot(squares, jnp.ones((channels, 128), BF16))
    return lax.rsqrt(total * (1.0 / channels) + 1e-06)


def activated(v, scale, gain):
    u = v * scale * gain
    return u * (0.5 + 0.5 * jnp.tanh(0.5 * u))


def column_masks(width, channels):
    column = lax.broadcasted_iota(jnp.int32, (width, channels), 0)
    return column == 0, column == width - 1


def beside(v, masks):
    width = v.shape[0]
    left = jnp.where(masks[0], 0.0, pltpu.roll(v, 1, 0))
    right = jnp.where(masks[1], 0.0, pltpu.roll(v, width - 1, 0))
    return left, right


def call(kernel, out_shape, scratch, flops, args, hbm=(), out_hbm=(), aliases=None):
    smem = pl.BlockSpec(memory_space=pltpu.SMEM)
    vmem = pl.BlockSpec(memory_space=pltpu.VMEM)
    far = pl.BlockSpec(memory_space=pltpu.HBM)
    in_specs = [smem] + [far if i in hbm else vmem for i in range(1, len(args))]
    args = [pltpu.with_memory_space_constraint(x, pltpu.HBM) if i in hbm else x for i, x in enumerate(args)]
    return pl.pallas_call(
        kernel,
        out_shape=out_shape,
        in_specs=in_specs,
        out_specs=tuple(far if i in out_hbm else vmem for i in range(len(out_shape))),
        scratch_shapes=scratch,
        input_output_aliases=aliases or {},
        compiler_params=pltpu.CompilerParams(vmem_limit_bytes=LIMIT << 20),
        cost_estimate=pl.CostEstimate(flops=flops, bytes_accessed=4 << 20, transcendentals=0),
    )(*args)


def pack_rows(ref, rows, get):
    half = rows // 2
    for row in range(half):
        upper, lower = get(row), get(row + half)
        ref[row] = upper[:, 0:128].astype(BF16)
        ref[row + half] = lower[:, 0:128].astype(BF16)
        ref[rows + row] = jnp.concatenate([upper[:, 128:192], lower[:, 128:192]], axis=1).astype(BF16)


def unpack_row(ref, row):
    half = ref.shape[0] // 3
    side, at = divmod(row, half)
    rest = ref[2 * half + at].astype(F32)
    return jnp.concatenate([ref[row].astype(F32), rest[:, 64 * side : 64 * side + 64]], axis=1)


def convolve(acc, product, kernel, terms, rows, width):
    masks = column_masks(width, 192)
    fields = [window(b) for window, a in terms for b in range(3)]
    if product is dot_t:
        fields = [jnp.concatenate(fields, axis=1)]
    for e in range(3):
        taps = [kernel[a, b, e] for window, a in terms for b in range(3)]
        if product is dot_t:
            taps = [jnp.concatenate(taps, axis=1)]
        total = None
        for field, tap in zip(fields, taps):
            term = product(field, tap)
            total = term if total is None else total + term
        for row in range(rows):
            part = slice(row * width, (row + 1) * width)
            moved = total[part]
            if e == 0:
                acc[part] = jnp.where(masks[0], 0.0, pltpu.roll(moved, 1, 0))
            elif e == 1:
                acc[part] += moved
            else:
                acc[part] += jnp.where(masks[1], 0.0, pltpu.roll(moved, width - 1, 0))


def windows(ref, rows):
    return lambda b: ref[b : b + rows].reshape(rows * ref.shape[1], ref.shape[2])


OWN = (((0, 2),), ((0, 1), (1, 2)))


def activate_rows(ref, gain, squares, scale, out):
    rows, width, channels = ref.shape
    pixels = rows * width
    v = ref[...].astype(F32)
    squares[0:pixels] = (v * v).astype(BF16).reshape(pixels, channels)
    scale[0:pixels] = scales(squares[0:pixels], channels)
    for row in range(rows):
        part = slice(row * width, (row + 1) * width)
        for at, lanes in spans(channels):
            out[row, :, at : at + lanes] = activated(
                ref[row, :, at : at + lanes].astype(F32), scale[part], gain[at : at + lanes].reshape(1, lanes)
            ).astype(BF16)


def inner_kernel(place, latents, gain, kernel, held, weights, active, sums, held_gain, squares, scale, sems):
    frames, rows, width, channels = held.shape
    copies = [
        pltpu.make_async_copy(latents.at[1], held.at[1], sems.at[0]),
        pltpu.make_async_copy(latents.at[0], held.at[0], sems.at[1]),
        pltpu.make_async_copy(kernel, weights, sems.at[2]),
        pltpu.make_async_copy(gain, held_gain, sems.at[3]),
    ]
    for copy in (copies[0], copies[3], copies[1], copies[2]):
        copy.start()
    copies[3].wait()
    for frame, copy in ((1, copies[0]), (0, copies[1])):
        copy.wait()
        activate_rows(held.at[frame], held_gain, squares, scale, active.at[frame])
    copies[2].wait()
    count = rows - 2
    convolve(sums.at[1], dot_t, weights, [(windows(active.at[1], count), 0)], count, width)
    convolve(
        sums.at[0],
        dot_t,
        weights,
        [(windows(active.at[0], count), 0), (windows(active.at[1], count), 1)],
        count,
        width,
    )


def fill_edges(place, near, far, frame, gain, active, edges, raw, squares, scale):
    odd = place[1] % 2 == 1
    inner = jnp.logical_and(place[1] > 0, place[1] < place[3] - 1)
    rows = active.shape[1]
    for row in range(HALO):
        chip = near[frame, row]
        next_chip = jnp.where(inner, far[frame, row], jnp.zeros_like(chip))
        raw[row] = jnp.where(odd, chip, next_chip)
        raw[HALO + row] = jnp.where(odd, next_chip, chip)
    activate_rows(raw.at[0:HALO], gain, squares, scale, edges.at[0, 0:HALO])
    activate_rows(raw.at[HALO : 2 * HALO], gain, squares, scale, edges.at[1, 2 : 2 + HALO])
    edges[0, HALO : HALO + 2] = active[frame, 0:2]
    edges[1, 0:2] = active[frame, rows - 2 : rows]


def edge_windows(edges):
    width, channels = edges.shape[2], edges.shape[3]
    return lambda b: edges[:, b : b + HALO].reshape(2 * HALO * width, channels)


def pack_joined(partial, sums, acc, wide, width):
    def get(row):
        if HALO <= row < wide - HALO:
            return sums[(row - HALO) * width : (row - HALO + 1) * width]
        at = row if row < HALO else row - (wide - 2 * HALO)
        return acc[at * width : (at + 1) * width]

    pack_rows(partial, wide, get)


def late_edge_kernel(
    place, near, far, gain, active, weights, sums, partial, edges, acc, raw, squares, scale
):
    fill_edges(place, near, far, 1, gain, active, edges, raw, squares, scale)
    width = active.shape[2]
    convolve(acc, dot_t, weights, [(edge_windows(edges), 0)], 2 * HALO, width)
    pack_joined(partial, sums.at[1], acc, active.shape[1] + 4, width)


def early_edge_kernel(
    place, near, far, gain, active, weights, sums, late, partial, tall, edges, acc, raw, squares, scale
):
    fill_edges(place, near, far, 0, gain, active, edges, raw, squares, scale)
    rows, width = active.shape[1], active.shape[2]
    convolve(acc, dot_t, weights, [(edge_windows(edges), 0), (edge_windows(late), 1)], 2 * HALO, width)
    pack_joined(partial, sums.at[0], acc, rows + 4, width)
    for frame, ends in ((0, edges), (1, late)):
        tall[frame, 0:HALO] = ends[0, 0:HALO]
        tall[frame, HALO : HALO + rows] = active[frame]
        tall[frame, HALO + rows :] = ends[1, 2:]


def first_own_kernel(place, active, kernel, own):
    wide, width = active.shape[1] - 2, active.shape[2]
    for out in (1, 0):
        terms = [(windows(active.at[frame], wide), a) for frame, a in OWN[out]]
        convolve(own.at[out], dot_t, kernel, terms, wide, width)


def finish(place, own, before, gain, raw, squares, scale, keep, out):
    tall, width = before.shape[0] * 2 // 3, before.shape[1]
    start = place[1] * 8 - (tall - 8) // 2
    follows = place[0] > 0
    for row in range(tall):
        part = slice(row * width, (row + 1) * width)
        earlier = jnp.where(follows, unpack_row(before, row), 0.0)
        total = (own[part] + earlier).astype(BF16)
        raw[part] = total
        keep(row, total)
        total = total.astype(F32)
        squares[part] = (total * total).astype(BF16)
    scale[...] = scales(squares[...], 192)

    def get(row):
        part = slice(row * width, (row + 1) * width)
        inside = jnp.logical_and(start + row >= 0, start + row < place[3] * 8)
        lanes = []
        for at, count in spans(192):
            v = activated(
                raw[part, at : at + count].astype(F32), scale[part, 0:count], gain[at : at + count].reshape(1, count)
            )
            if not (tall - 8) // 2 <= row < (tall + 8) // 2:
                v = jnp.where(inside, v, 0.0)
            lanes.append(v)
        v = jnp.concatenate(lanes, axis=1)
        out[row] = v.astype(BF16)
        return v

    return get


def late_second_kernel(
    place, own, before, gain, kernel, partial, active, raw, squares, scale, acc
):
    tall, width = active.shape[0], active.shape[1]
    get = finish(place, own.at[1], before, gain, raw, squares, scale, lambda row, total: None, active)
    for row in range(tall):
        get(row)
    wide = tall - 2
    convolve(acc, dot, kernel, [(windows(active, wide), 0)], wide, width)
    pack_rows(partial, wide, lambda row: acc[row * width : (row + 1) * width])


def early_second_kernel(
    place, own, before, gain, kernel, late, partial, active, raw, squares, scale, acc
):
    tall, width = active.shape[0], active.shape[1]
    get = finish(place, own.at[0], before, gain, raw, squares, scale, lambda row, total: None, active)
    for row in range(tall):
        get(row)
    wide = tall - 2
    convolve(acc, dot, kernel, [(windows(active, wide), 0), (windows(late, wide), 1)], wide, width)
    pack_rows(partial, wide, lambda row: acc[row * width : (row + 1) * width])


def second_own_kernel(place, early, late, kernel, latents, near, far, shortcut, own):
    wide, width = early.shape[0] - 2, early.shape[1]
    pixels = wide * width
    rows, channels = latents.shape[1], latents.shape[3]
    odd = place[1] % 2
    inner = wide - 1
    active = (early, late)
    for out in (1, 0):
        terms = [(windows(active[frame], wide), a) for frame, a in OWN[out]]
        convolve(own.at[out], dot, kernel, terms, wide, width)
        body = latents[out].reshape(rows * width, channels)
        own[out, width : pixels - width] += dot_t(body, shortcut[...])
        other = dot_t(near[out, jnp.where(odd == 1, HALO - 1, 0)], shortcut[...])
        own[out, pl.ds(jnp.where(odd == 1, 0, inner * width), width)] += other
        other = dot_t(far[out, jnp.where(odd == 1, 0, HALO - 1)], shortcut[...])
        own[out, pl.ds(jnp.where(odd == 1, inner * width, 0), width)] += other


def late_third_kernel(place, own, before, gain, block_out, packed, active, raw, squares, scale):
    tall = active.shape[0]

    def keep(row, total):
        if 0 < row < tall - 1:
            block_out[row - 1] = total

    pack_rows(packed, tall, finish(place, own.at[1], before, gain, raw, squares, scale, keep, active))


def early_third_kernel(place, own, before, gain, late_out, block_out, packed, active, raw, squares, scale):
    tall = active.shape[0]

    def keep(row, total):
        if 0 < row < tall - 1:
            block_out[0, row - 1] = total

    block_out[1] = late_out[...]
    pack_rows(packed, tall, finish(place, own.at[0], before, gain, raw, squares, scale, keep, active))


def weights_kernel(place, kernel, out):
    for a in range(3):
        by_row = []
        for b in range(3):
            k = [kernel[a, b, e].astype(F32) for e in range(3)]
            by_row.append((-k[0], k[0] + k[1] + k[2], k[2]))
        for q in range(3):
            out[a, 0, q] = (-by_row[0][q]).astype(BF16)
            out[a, 1, q] = (by_row[0][q] + by_row[1][q] + by_row[2][q]).astype(BF16)
            out[a, 2, q] = by_row[2][q].astype(BF16)


def differences(get, level, steps, tall, width):
    masks = column_masks(width, 192)
    last = None
    for at in range(tall):
        v = get(at).astype(F32)
        left, right = beside(v, masks)
        now = (v - left, v, right - v)
        for q in range(3):
            if 0 < at < tall - 1:
                level[q, at - 1] = now[q].astype(BF16)
            if at > 0:
                steps[q, at - 1] = (now[q] - last[q]).astype(BF16)
        last = now


def products(terms, kernel, rows, width, p, q):
    total = None
    for level, steps, a in terms:
        if p == 1:
            window = level[q]
        else:
            window = steps[q, 0:rows] if p == 0 else steps[q, 1 : rows + 1]
        term = dot(window.reshape(rows * width, 192), kernel[a, p, q])
        total = term if total is None else total + term
    return total


def phases(terms, kernel, rows, width):
    by = []
    for q in range(3):
        m = [products(terms, kernel, rows, width, p, q) for p in range(3)]
        by.append((m[1] + m[0], m[1] + m[2]))
    return [[by[1][i] + by[0][i], by[1][i] + by[2][i]] for i in range(2)]


def third_own_kernel(place, early, late, kernel, own, level, steps):
    rows, width = early.shape[0] - 2, early.shape[1]
    for frame, active in enumerate((early, late)):
        differences(lambda at: active[at], level.at[frame], steps.at[frame], rows + 2, width)
    for out, taps in enumerate(OWN):
        terms = [(level.at[frame], steps.at[frame], a) for frame, a in taps]
        result = phases(terms, kernel, rows, width)
        for i in range(2):
            for j in range(2):
                own[out, 2 * i + j] = result[i][j]


def weave(total, i, j, rows, width, woven):
    for row in range(rows):
        value = total[row * width : (row + 1) * width]
        woven[i, row, 0, pl.ds(j, width, stride=2)] = value[:, 0:128]
        woven[i, row, 1, pl.ds(j, width, stride=2), 0:64] = value[:, 128:192]


def weave_out(fine, i, rows, woven):
    for row in range(rows):
        fine[2 * row + i, :, 0:128] = woven[i, row, 0].astype(BF16)
        fine[2 * row + i, :, 128:192] = woven[i, row, 1, :, 0:64].astype(BF16)


def before_terms(place, packed, level, steps, a):
    tall, width = 2 * packed.shape[0] // 3, packed.shape[1]
    follows = place[0] > 0
    differences(lambda at: jnp.where(follows, unpack_row(packed, at), 0.0), level, steps, tall, width)
    return [(level, steps, a)]


def late_last_kernel(place, packed, kernel, own, decoded, rest, level, steps, woven, fine, sem):
    rows, width = 2 * packed.shape[0] // 3 - 2, packed.shape[1]
    terms = before_terms(place, packed, level, steps, 0)
    result = phases(terms, kernel, rows, width)
    for i in range(2):
        for j in range(2):
            weave(own[1, 2 * i + j] + result[i][j], i, j, rows, width, woven)
        weave_out(fine, i, rows, woven)
    copy = pltpu.make_async_copy(fine, decoded.at[1], sem)
    copy.start()
    result = phases([(level, steps, 1)], kernel, rows, width)
    for i in range(2):
        for j in range(2):
            rest[2 * i + j] = own[0, 2 * i + j] + result[i][j]
    copy.wait()


def early_last_kernel(place, packed, kernel, rest, half, decoded, level, steps, woven, fine, sem):
    rows, width = 2 * packed.shape[0] // 3 - 2, packed.shape[1]
    terms = before_terms(place, packed, level, steps, 0)
    result = phases(terms, kernel, rows, width)
    for i in range(2):
        for j in range(2):
            weave(rest[2 * i + j] + result[i][j], i, j, rows, width, woven)
        weave_out(fine, i, rows, woven)
    copy = pltpu.make_async_copy(fine, decoded.at[0], sem)
    copy.start()
    copy.wait()


def onward(value):
    count = lax.axis_size("tm")
    return lax.ppermute(value, "tm", [(i, (i + 1) % count) for i in range(count)])


def swap(value, offset):
    count = lax.axis_size("rows")
    pairs = [((2 * i + offset) % count, (2 * i + 1 + offset) % count) for i in range(count // 2)]
    return lax.ppermute(value, "rows", pairs + [(b, a) for a, b in pairs])


def body(
    latents,
    gain_first,
    kernel_first,
    gain_second,
    kernel_second,
    shortcut,
    gain_third,
    kernel_third,
):
    frames, rows, width, channels = latents.shape
    group, slab = lax.axis_index("tm"), lax.axis_index("rows")
    place = jnp.stack(
        [group, slab, jnp.int32(lax.axis_size("tm")), jnp.int32(lax.axis_size("rows"))]
    ).astype(jnp.int32)
    shape = jax.ShapeDtypeStruct
    odd = slab % 2
    near = lax.dynamic_slice_in_dim(latents, (rows - HALO) * (1 - odd), HALO, 1)
    far = lax.dynamic_slice_in_dim(latents, (rows - HALO) * odd, HALO, 1)
    near, far = swap(near, 0), swap(far, 1)

    wide1, wide2 = rows + 4, rows + 2
    pixels, pixels1, pixels2 = rows * width, wide1 * width, wide2 * width
    flops1, flops2, flops3 = (18 * n * 192 for n in (pixels1 * channels, pixels2 * 192, pixels * 192))
    dma = pltpu.SemaphoreType.DMA

    def work(tall, channels):
        return [pltpu.VMEM((tall * width, channels), BF16), pltpu.VMEM((tall * width, 128), F32)]

    held, weights, active, sums, gain_first = call(
        inner_kernel,
        (
            shape(latents.shape, BF16),
            shape((3, 3, 3, 192, channels), BF16),
            shape(latents.shape, BF16),
            shape((2, (rows - 2) * width, 192), F32),
            shape((channels,), F32),
        ),
        work(rows, channels) + [dma((4,))],
        2 * flops1,
        (place, latents, gain_first, jnp.swapaxes(kernel_first, 3, 4)),
        hbm=(1, 2, 3),
    )
    edge_work = [
        pltpu.VMEM((2 * HALO * width, 192), F32),
        pltpu.VMEM((2 * HALO, width, channels), BF16),
    ] + work(HALO, channels)
    ends = shape((2, HALO + 2, width, channels), BF16)
    packed1 = shape((wide1 * 3 // 2, width, 128), BF16)
    partial, late = call(
        late_edge_kernel,
        (packed1, ends),
        edge_work,
        flops1 // 2,
        (place, near, far, gain_first, active, weights, sums),
    )
    before_late = onward(partial)
    partial, tall = call(
        early_edge_kernel,
        (packed1, shape((2, wide1 + 2, width, channels), BF16)),
        [pltpu.VMEM(ends.shape, BF16)] + edge_work,
        flops1,
        (place, near, far, gain_first, active, weights, sums, late),
    )
    before_early = onward(partial)
    (own,) = call(
        first_own_kernel, (shape((2, pixels1, 192), F32),), [], 3 * flops1, (place, tall, weights)
    )
    (mixed,) = call(
        weights_kernel, (shape((3, 3, 3, 192, 192), BF16),), [], 1 << 24, (place, kernel_third)
    )
    second_work = (
        [pltpu.VMEM((pixels1, 192), BF16)] + work(wide1, 192) + [pltpu.VMEM((pixels2, 192), F32)]
    )
    packed2 = shape((wide2 * 3 // 2, width, 128), BF16)
    field = shape((wide1, width, 192), BF16)
    partial, late = call(
        late_second_kernel,
        (packed2, field),
        second_work,
        flops2,
        (place, own, before_late, gain_second, kernel_second),
    )
    before_late = onward(partial)
    partial, early = call(
        early_second_kernel,
        (packed2, field),
        second_work,
        2 * flops2,
        (place, own, before_early, gain_second, kernel_second, late),
    )
    before_early = onward(partial)
    (own,) = call(
        second_own_kernel,
        (shape((2, pixels2, 192), F32),),
        [],
        3 * flops2,
        (place, early, late, kernel_second, held, near, far, shortcut.T),
    )
    third_work = [pltpu.VMEM((pixels2, 192), BF16)] + work(wide2, 192)
    field = shape((wide2, width, 192), BF16)
    late_out, packed, late = call(
        late_third_kernel,
        (shape((rows, width, 192), BF16), packed2, field),
        third_work,
        1 << 24,
        (place, own, before_late, gain_third),
    )
    before_late = onward(packed)
    block_out, packed, early = call(
        early_third_kernel,
        (shape((2, rows, width, 192), BF16), packed2, field),
        third_work,
        1 << 24,
        (place, own, before_early, gain_third, late_out),
    )
    before_early = onward(packed)
    (own,) = call(
        third_own_kernel,
        (shape((2, 4, pixels, 192), F32),),
        [pltpu.VMEM((2, 3, rows, width, 192), BF16), pltpu.VMEM((2, 3, rows + 1, width, 192), BF16)],
        3 * flops3,
        (place, early, late, mixed),
    )
    last_work = [
        pltpu.VMEM((3, rows, width, 192), BF16),
        pltpu.VMEM((3, rows + 1, width, 192), BF16),
        pltpu.VMEM((2, rows, 2, 2 * width, 128), F32),
        pltpu.VMEM((2 * rows, 2 * width, 192), BF16),
        dma,
    ]
    fine = shape((2, 2 * rows, 2 * width, 192), BF16)
    decoded, rest = call(
        late_last_kernel,
        (fine, shape((4, pixels, 192), F32)),
        last_work,
        2 * flops3,
        (place, before_late, mixed, own),
        out_hbm=(0,),
    )
    (decoded,) = call(
        early_last_kernel,
        (fine,),
        last_work,
        flops3,
        (place, before_early, mixed, rest, decoded),
        hbm=(4,),
        out_hbm=(0,),
        aliases={4: 0},
    )
    return (block_out, decoded)


def solution(mesh):
    return jax.shard_map(
        body,
        mesh=mesh,
        in_specs=(P("tm", "rows", None, None), P(), P(), P(), P(), P(), P(), P()),
        out_specs=(P("tm", "rows", None, None), P("tm", "rows", None, None)),
        check_vma=False,
    )
```

time: 166 us -> 51.6 us (0.31)
  the two profiles are of different devices: /device:TPU:119 before, /device:TPU:24 now
where the time goes in v2:
time: 51.6 us; the launch traced here: 51.5 us
  Pallas kernels  31.1 us (60%)
  starting transfers between devices  17.6 us (34%)
  local copies, waits for them, and re-layouts  1.12 us (2%)
  between operations  0.96 us (2%)
  waiting for transfers between devices  0.61 us (1%)
    pallas_call x13, Pallas kernels, call(): pl.pallas_call(kernel, out_shape=out_shape, in_specs=in_specs, out_specs=...  31.1 us
    ppermute x6, starting transfers between devices, onward(): lax.ppermute(value, 'tm', [(i, (i + 1) % count) for i in range(count)])  9.39 us
    ppermute x2, starting transfers between devices, swap(): return lax.ppermute(value, 'rows', pairs + [(b, a) for a, b in pairs])  8.24 us
    dynamic_slice x1, local copies, waits for them, and re-layouts, body(): far = lax.dynamic_slice_in_dim(latents, (rows - HALO) * odd, HALO, 1)  1.1 us
  transfers between devices with their start and end apart: 8, of which 1 were waited for; matrix products, arithmetic and copies ran while one was open for 0% of the time, Pallas kernels for 52%

profile of v2, /device:TPU:24, one launch (start us, length us, event | category | flops | bytes accessed | tf_op | source)
XLA Modules:
  0.0 51.5 jit_solution(10688525398294699620)
XLA Ops:
  0.7 1.1 %constant_dynamic-slice_fusion = (bf16[2,3,48,384]{3,2,1,0:T(8,128)(2,1)S(1)}, bf16[2,3,48,384]{3,2,1,0:T(8,128)(2,1)S(1)}) fusion(bf16[2,8,48,384]{3,2,1,0:T(8,128)(2,1)} %latents.1, s32[]{:T(128)S(6)} %select_n.15, s32[]{:T(128)S(6)} %select_n.14), kind=kLoop, calls=%fused_computation.1 | loop fusion | bytes 884744 | tf_op jit(solution)/shard_map/dynamic_slice | solution.py:446
  1.8 0.1 collective-permute-start
  1.9 8.2 %collective-permute-start.1 = (bf16[2,3,48,384]{3,2,1,0:T(8,128)(2,1)S(1)}, bf16[2,3,48,384]{3,2,1,0:T(8,128)(2,1)S(1)}, u32[]{:S(2)}, u32[]{:S(2)}) collective-permute-start(bf16[2,3,48,384]{3,2,1,0:T(8,128)(2,1)S(1)} %get-tuple-element.44), channel_id=1, source_target_pairs={{1,2},{3,4},{5,6},{7,8},{9,10},{11,12},{13,14},{15,16},{17,18},{19... | collective-permute-start | bytes 663560 | tf_op jit(solution)/shard_map/ppermute | solution.py:425
  10.0 0.1 pad_add_fusion.place
  10.1 4.9 %shard_map.95 = (bf16[2,8,48,384]{3,2,1,0:T(8,128)(2,1)S(1)}, bf16[3,3,3,192,384]{4,3,2,1,0:T(8,128)(2,1)S(1)}, bf16[2,8,48,384]{3,2,1,0:T(8,128)(2,1)S(1)}, f32[2,288,192]{2,1,0:T(8,128)S(1)}, f32[384]{0:T(512)S(1)}) custom-call(s32[4]{0:T(128)S(1)} %pad_add_fusion.place, bf16[2,8,48,384]{3,2,1,0:T(8,128)(2,1)} %latents.1, f32[384]{0:T(512)} %gain.5, ...), custom_call_target="tpu_custom_call" | custom-call | flops 1528823808 | bytes 4194304 | tf_op jit(solution)/shard_map/pallas_call | solution.py:54
  15.0 0.0 collective-permute-done.near
  15.0 0.0 collective-permute-done.1.far
  15.0 1.7 %shard_map.96 = (bf16[18,48,128]{2,1,0:T(8,128)(2,1)S(1)}, bf16[2,5,48,384]{3,2,1,0:T(8,128)(2,1)S(1)}) custom-call(s32[4]{0:T(128)S(1)} %pad_add_fusion.place, bf16[2,3,48,384]{3,2,1,0:T(8,128)(2,1)S(1)} %collective-permute-done.near, bf16[2,3,48,384]{3,2,1,0:T(8,128)(2,1)S(1)} %collective-permute-done.1.far, f32[384]{0:T(512)S(1)} %get-tuple-element.23.gain, ...), custom_call_target="tpu_custom_call" | custom-call | flops 382205952 | bytes 4194304 | tf_op jit(solution)/shard_map/pallas_call | solution.py:54
  16.7 0.3 collective-permute-start.3
  17.0 2.2 %shard_map.97 = (bf16[18,48,128]{2,1,0:T(8,128)(2,1)S(1)}, bf16[2,14,48,384]{3,2,1,0:T(8,128)(2,1)S(1)}) custom-call(s32[4]{0:T(128)S(1)} %pad_add_fusion.place, bf16[2,3,48,384]{3,2,1,0:T(8,128)(2,1)S(1)} %collective-permute-done.near, bf16[2,3,48,384]{3,2,1,0:T(8,128)(2,1)S(1)} %collective-permute-done.1.far, f32[384]{0:T(512)S(1)} %get-tuple-element.23.gain, ...), custom_call_target="tpu_custom_call" | custom-call | flops 764411904 | bytes 4194304 | tf_op jit(solution)/shard_map/pallas_call | solution.py:54
  19.2 1.7 %collective-permute-start.2 = (bf16[18,48,128]{2,1,0:T(8,128)(2,1)S(1)}, bf16[18,48,128]{2,1,0:T(8,128)(2,1)S(1)}, u32[]{:S(2)}, u32[]{:S(2)}) collective-permute-start(bf16[18,48,128]{2,1,0:T(8,128)(2,1)S(1)} %get-tuple-element.29), channel_id=1, source_target_pairs={{0,64},{64,128},{128,192},{192,0},{1,65},{65,129},{129,193},{193,1... | collective-permute-start | bytes 663560 | tf_op jit(solution)/shard_map/ppermute | solution.py:419
  20.8 0.0 copy-start
  20.8 0.0 copy-start.3
  20.8 4.0 %shard_map.98.own = f32[2,576,192]{2,1,0:T(8,128)S(1)} custom-call(s32[4]{0:T(128)S(1)} %pad_add_fusion.place, bf16[2,14,48,384]{3,2,1,0:T(8,128)(2,1)S(1)} %get-tuple-element.28.active, bf16[3,3,3,192,384]{4,3,2,1,0:T(8,128)(2,1)S(1)} %get-tuple-element.25.weights.kernel), custom_call_target="tpu_custom_call" | custom-call | flops 2293235712 | bytes 4194304 | tf_op jit(solution)/shard_map/pallas_call | solution.py:54
  24.9 0.0 collective-permute-done.3.before
  24.9 0.0 copy-done
  24.9 0.0 copy-done.3
  24.9 1.7 %shard_map.99 = (bf16[15,48,128]{2,1,0:T(8,128)(2,1)S(1)}, bf16[12,48,192]{2,1,0:T(8,128)(2,1)S(1)}) custom-call(s32[4]{0:T(128)S(1)} %pad_add_fusion.place, f32[2,576,192]{2,1,0:T(8,128)S(1)} %shard_map.98.own, bf16[18,48,128]{2,1,0:T(8,128)(2,1)S(1)} %collective-permute-done.3.before, f32[192]{0:T(256)S(1)} %copy-done.3, ...), custom_call_target="tpu_custom_call" | custom-call | flops 318504960 | bytes 4194304 | tf_op jit(solution)/shard_map/pallas_call | solution.py:54
  26.6 0.0 copy-start.2
  26.6 1.6 %collective-permute-start.5 = (bf16[15,48,128]{2,1,0:T(8,128)(2,1)S(1)}, bf16[15,48,128]{2,1,0:T(8,128)(2,1)S(1)}, u32[]{:S(2)}, u32[]{:S(2)}) collective-permute-start(bf16[15,48,128]{2,1,0:T(8,128)(2,1)S(1)} %get-tuple-element.35), channel_id=1, source_target_pairs={{0,64},{64,128},{128,192},{192,0},{1,65},{65,129},{129,193},{193,1... | collective-permute-start | bytes 552968 | tf_op jit(solution)/shard_map/ppermute | solution.py:419
  28.3 0.0 collective-permute-done.2.before
  28.3 2.3 %shard_map.100 = (bf16[15,48,128]{2,1,0:T(8,128)(2,1)S(1)}, bf16[12,48,192]{2,1,0:T(8,128)(2,1)S(1)}) custom-call(s32[4]{0:T(128)S(1)} %pad_add_fusion.place, f32[2,576,192]{2,1,0:T(8,128)S(1)} %shard_map.98.own, bf16[18,48,128]{2,1,0:T(8,128)(2,1)S(1)} %collective-permute-done.2.before, f32[192]{0:T(256)S(1)} %copy-done.3, ...), custom_call_target="tpu_custom_call" | custom-call | flops 637009920 | bytes 4194304 | tf_op jit(solution)/shard_map/pallas_call | solution.py:54
  30.6 2.1 %collective-permute-start.4 = (bf16[15,48,128]{2,1,0:T(8,128)(2,1)S(1)}, bf16[15,48,128]{2,1,0:T(8,128)(2,1)S(1)}, u32[]{:S(2)}, u32[]{:S(2)}) collective-permute-start(bf16[15,48,128]{2,1,0:T(8,128)(2,1)S(1)} %get-tuple-element.34), channel_id=1, source_target_pairs={{0,64},{64,128},{128,192},{192,0},{1,65},{65,129},{129,193},{193,1... | collective-permute-start | bytes 552968 | tf_op jit(solution)/shard_map/ppermute | solution.py:419
  32.7 0.0 copy-done.2
  32.7 0.0 copy-start.4
  32.7 0.0 copy-start.1
  32.7 3.0 %shard_map.101.own = f32[2,480,192]{2,1,0:T(8,128)S(1)} custom-call(s32[4]{0:T(128)S(1)} %pad_add_fusion.place, bf16[12,48,192]{2,1,0:T(8,128)(2,1)S(1)} %get-tuple-element.32.early, bf16[12,48,192]{2,1,0:T(8,128)(2,1)S(1)} %get-tuple-element.31.late, bf16[3,3,3,192,192]{4,3,2,1,0:T(8,128)(2,1)S(1)} %copy-done, ...), custom_call_target="tpu_custom_call" | custom-call | flops 955514880 | bytes 4194304 | tf_op jit(solution)/shard_map/pallas_call | solution.py:54
  35.7 0.0 collective-permute-done.5.before
  35.7 0.0 copy-done.4
  35.7 1.0 %shard_map.102 = (bf16[8,48,192]{2,1,0:T(8,128)(2,1)S(1)}, bf16[15,48,128]{2,1,0:T(8,128)(2,1)S(1)}, bf16[10,48,192]{2,1,0:T(8,128)(2,1)S(1)}) custom-call(s32[4]{0:T(128)S(1)} %pad_add_fusion.place, f32[2,480,192]{2,1,0:T(8,128)S(1)} %shard_map.101.own, bf16[15,48,128]{2,1,0:T(8,128)(2,1)S(1)} %collective-permute-done.5.before, f32[192]{0:T(256)S(1)} %copy-done.4), custom_call_target="tpu_custom_call" | custom-call | flops 16777216 | bytes 4194304 | tf_op jit(solution)/shard_map/pallas_call | solution.py:54
  36.7 0.9 %collective-permute-start.7 = (bf16[15,48,128]{2,1,0:T(8,128)(2,1)S(1)}, bf16[15,48,128]{2,1,0:T(8,128)(2,1)S(1)}, u32[]{:S(2)}, u32[]{:S(2)}) collective-permute-start(bf16[15,48,128]{2,1,0:T(8,128)(2,1)S(1)} %get-tuple-element.39), channel_id=1, source_target_pairs={{0,64},{64,128},{128,192},{192,0},{1,65},{65,129},{129,193},{193,1... | collective-permute-start | bytes 552968 | tf_op jit(solution)/shard_map/ppermute | solution.py:419
  37.6 0.6 %collective-permute-done.4.before = bf16[15,48,128]{2,1,0:T(8,128)(2,1)S(1)} collective-permute-done((bf16[15,48,128]{2,1,0:T(8,128)(2,1)S(1)}, bf16[15,48,128]{2,1,0:T(8,128)(2,1)S(1)}, u32[]{:S(2)}, u32[]{:S(2)}) %collective-permute-start.4) | collective-permute-done | bytes 184352 | tf_op jit(solution)/shard_map/ppermute | solution.py:419
  38.2 1.7 %shard_map.103 = (bf16[2,8,48,192]{3,2,1,0:T(8,128)(2,1)}, bf16[15,48,128]{2,1,0:T(8,128)(2,1)S(1)}, bf16[10,48,192]{2,1,0:T(8,128)(2,1)S(1)}) custom-call(s32[4]{0:T(128)S(1)} %pad_add_fusion.place, f32[2,480,192]{2,1,0:T(8,128)S(1)} %shard_map.101.own, bf16[15,48,128]{2,1,0:T(8,128)(2,1)S(1)} %collective-permute-done.4.before, f32[192]{0:T(256)S(1)} %copy-done.4, ...), custom_call_target="tpu_custom_call" | custom-call | flops 16777216 | bytes 4194304 | tf_op jit(solution)/shard_map/pallas_call | solution.py:54
  39.8 2.8 %collective-permute-start.6 = (bf16[15,48,128]{2,1,0:T(8,128)(2,1)S(1)}, bf16[15,48,128]{2,1,0:T(8,128)(2,1)S(1)}, u32[]{:S(2)}, u32[]{:S(2)}) collective-permute-start(bf16[15,48,128]{2,1,0:T(8,128)(2,1)S(1)} %get-tuple-element.38), channel_id=1, source_target_pairs={{0,64},{64,128},{128,192},{192,0},{1,65},{65,129},{129,193},{193,1... | collective-permute-start | bytes 552968 | tf_op jit(solution)/shard_map/ppermute | solution.py:419
  42.6 0.0 copy-done.1
  42.6 1.3 %shard_map.104.kernel = bf16[3,3,3,192,192]{4,3,2,1,0:T(8,128)(2,1)S(1)} custom-call(s32[4]{0:T(128)S(1)} %pad_add_fusion.place, bf16[3,3,3,192,192]{4,3,2,1,0:T(8,128)(2,1)S(1)} %copy-done.1), custom_call_target="tpu_custom_call" | custom-call | flops 16777216 | bytes 4194304 | tf_op jit(solution)/shard_map/pallas_call | solution.py:54
  43.9 2.3 %shard_map.105.own = f32[2,4,384,192]{3,2,1,0:T(8,128)S(1)} custom-call(s32[4]{0:T(128)S(1)} %pad_add_fusion.place, bf16[10,48,192]{2,1,0:T(8,128)(2,1)S(1)} %get-tuple-element.40.early, bf16[10,48,192]{2,1,0:T(8,128)(2,1)S(1)} %get-tuple-element.41.late, bf16[3,3,3,192,192]{4,3,2,1,0:T(8,128)(2,1)S(1)} %shard_map.104.kernel), custom_call_target="tpu_custom_call" | custom-call | flops 764411904 | bytes 4194304 | tf_op jit(solution)/shard_map/pallas_call | solution.py:54
  46.3 0.0 collective-permute-done.7.packed
  46.3 2.6 %shard_map.106 = (bf16[2,16,96,192]{3,2,1,0:T(8,128)(2,1)}, f32[4,384,192]{2,1,0:T(8,128)S(1)}) custom-call(s32[4]{0:T(128)S(1)} %pad_add_fusion.place, bf16[15,48,128]{2,1,0:T(8,128)(2,1)S(1)} %collective-permute-done.7.packed, bf16[3,3,3,192,192]{4,3,2,1,0:T(8,128)(2,1)S(1)} %shard_map.104.kernel, f32[2,4,384,192]{3,2,1,0:T(8,128)S(1)} %shard_map.105.own), custom_call_target="tpu_custom_call" | custom-call | flops 509607936 | bytes 4194304 | tf_op jit(solution)/shard_map/pallas_call | solution.py:54
  48.8 0.0 collective-permute-done.6.packed
  48.8 2.5 %shard_map.107 = bf16[2,16,96,192]{3,2,1,0:T(8,128)(2,1)} custom-call(s32[4]{0:T(128)S(1)} %pad_add_fusion.place, bf16[15,48,128]{2,1,0:T(8,128)(2,1)S(1)} %collective-permute-done.6.packed, bf16[3,3,3,192,192]{4,3,2,1,0:T(8,128)(2,1)S(1)} %shard_map.104.kernel, f32[4,384,192]{2,1,0:T(8,128)S(1)} %get-tuple-element.42.rest, ...), custom_call_target="tpu_custom_call", output_to_operand_aliasing={{}: (4, {})} | custom-call | flops 254803968 | bytes 4194304 | tf_op jit(solution)/shard_map/pallas_call | solution.py:54
Async XLA Ops:
  1.8 13.2 %collective-permute-start = (bf16[2,3,48,384]{3,2,1,0:T(8,128)(2,1)S(1)}, bf16[2,3,48,384]{3,2,1,0:T(8,128)(2,1)S(1)}, u32[]{:S(2)}, u32[]{:S(2)}) collective-permute-start(bf16[2,3,48,384]{3,2,1,0:T(8,128)(2,1)S(1)} %get-tuple-element.45), channel_id=1, source_target_pairs={{0,1},{2,3},{4,5},{6,7},{8,9},{10,11},{12,13},{14,15},{16,17},{18,... | collective-permute-start | bytes 663560 | tf_op jit(solution)/shard_map/ppermute | solution.py:425
  1.9 13.1 %collective-permute-start.1 = (bf16[2,3,48,384]{3,2,1,0:T(8,128)(2,1)S(1)}, bf16[2,3,48,384]{3,2,1,0:T(8,128)(2,1)S(1)}, u32[]{:S(2)}, u32[]{:S(2)}) collective-permute-start(bf16[2,3,48,384]{3,2,1,0:T(8,128)(2,1)S(1)} %get-tuple-element.44), channel_id=1, source_target_pairs={{1,2},{3,4},{5,6},{7,8},{9,10},{11,12},{13,14},{15,16},{17,18},{19... | collective-permute-start | bytes 663560 | tf_op jit(solution)/shard_map/ppermute | solution.py:425
  16.7 8.2 %collective-permute-start.3 = (bf16[18,48,128]{2,1,0:T(8,128)(2,1)S(1)}, bf16[18,48,128]{2,1,0:T(8,128)(2,1)S(1)}, u32[]{:S(2)}, u32[]{:S(2)}) collective-permute-start(bf16[18,48,128]{2,1,0:T(8,128)(2,1)S(1)} %get-tuple-element.30), channel_id=1, source_target_pairs={{0,64},{64,128},{128,192},{192,0},{1,65},{65,129},{129,193},{193,1... | collective-permute-start | bytes 663560 | tf_op jit(solution)/shard_map/ppermute | solution.py:419
  19.2 9.1 %collective-permute-start.2 = (bf16[18,48,128]{2,1,0:T(8,128)(2,1)S(1)}, bf16[18,48,128]{2,1,0:T(8,128)(2,1)S(1)}, u32[]{:S(2)}, u32[]{:S(2)}) collective-permute-start(bf16[18,48,128]{2,1,0:T(8,128)(2,1)S(1)} %get-tuple-element.29), channel_id=1, source_target_pairs={{0,64},{64,128},{128,192},{192,0},{1,65},{65,129},{129,193},{193,1... | collective-permute-start | bytes 663560 | tf_op jit(solution)/shard_map/ppermute | solution.py:419
  20.8 4.0 %copy-start = (bf16[3,3,3,192,192]{4,3,2,1,0:T(8,128)(2,1)S(1)}, bf16[3,3,3,192,192]{4,3,2,1,0:T(8,128)(2,1)}, u32[]{:S(2)}) copy-start(bf16[3,3,3,192,192]{4,3,2,1,0:T(8,128)(2,1)} %kernel.6) | copy-start | bytes 5971972
  20.8 4.1 %copy-start.3 = (f32[192]{0:T(256)S(1)}, f32[192]{0:T(256)}, u32[]{:S(2)}) copy-start(f32[192]{0:T(256)} %gain.7) | copy-start | bytes 2308
  26.6 6.1 %copy-start.2 = (bf16[384,192]{0,1:T(8,128)(2,1)S(1)}, bf16[384,192]{0,1:T(8,128)(2,1)}, u32[]{:S(2)}) copy-start(bf16[384,192]{0,1:T(8,128)(2,1)} %param.13) | copy-start | bytes 442372
  26.6 9.0 %collective-permute-start.5 = (bf16[15,48,128]{2,1,0:T(8,128)(2,1)S(1)}, bf16[15,48,128]{2,1,0:T(8,128)(2,1)S(1)}, u32[]{:S(2)}, u32[]{:S(2)}) collective-permute-start(bf16[15,48,128]{2,1,0:T(8,128)(2,1)S(1)} %get-tuple-element.35), channel_id=1, source_target_pairs={{0,64},{64,128},{128,192},{192,0},{1,65},{65,129},{129,193},{193,1... | collective-permute-start | bytes 552968 | tf_op jit(solution)/shard_map/ppermute | solution.py:419
  30.6 7.6 %collective-permute-start.4 = (bf16[15,48,128]{2,1,0:T(8,128)(2,1)S(1)}, bf16[15,48,128]{2,1,0:T(8,128)(2,1)S(1)}, u32[]{:S(2)}, u32[]{:S(2)}) collective-permute-start(bf16[15,48,128]{2,1,0:T(8,128)(2,1)S(1)} %get-tuple-element.34), channel_id=1, source_target_pairs={{0,64},{64,128},{128,192},{192,0},{1,65},{65,129},{129,193},{193,1... | collective-permute-start | bytes 552968 | tf_op jit(solution)/shard_map/ppermute | solution.py:419
  32.7 3.0 %copy-start.4 = (f32[192]{0:T(256)S(1)}, f32[192]{0:T(256)}, u32[]{:S(2)}) copy-start(f32[192]{0:T(256)} %gain.9) | copy-start | bytes 2308
  32.7 9.9 %copy-start.1 = (bf16[3,3,3,192,192]{4,3,2,1,0:T(8,128)(2,1)S(1)}, bf16[3,3,3,192,192]{4,3,2,1,0:T(8,128)(2,1)}, u32[]{:S(2)}) copy-start(bf16[3,3,3,192,192]{4,3,2,1,0:T(8,128)(2,1)} %kernel.7) | copy-start | bytes 5971972
  36.7 9.6 %collective-permute-start.7 = (bf16[15,48,128]{2,1,0:T(8,128)(2,1)S(1)}, bf16[15,48,128]{2,1,0:T(8,128)(2,1)S(1)}, u32[]{:S(2)}, u32[]{:S(2)}) collective-permute-start(bf16[15,48,128]{2,1,0:T(8,128)(2,1)S(1)} %get-tuple-element.39), channel_id=1, source_target_pairs={{0,64},{64,128},{128,192},{192,0},{1,65},{65,129},{129,193},{193,1... | collective-permute-start | bytes 552968 | tf_op jit(solution)/shard_map/ppermute | solution.py:419
  39.8 9.0 %collective-permute-start.6 = (bf16[15,48,128]{2,1,0:T(8,128)(2,1)S(1)}, bf16[15,48,128]{2,1,0:T(8,128)(2,1)S(1)}, u32[]{:S(2)}, u32[]{:S(2)}) collective-permute-start(bf16[15,48,128]{2,1,0:T(8,128)(2,1)S(1)} %get-tuple-element.38), channel_id=1, source_target_pairs={{0,64},{64,128},{128,192},{192,0},{1,65},{65,129},{129,193},{193,1... | collective-permute-start | bytes 552968 | tf_op jit(solution)/shard_map/ppermute | solution.py:419

commit v3 on v2

v3 whole, which is shorter than its diff:
```python
import jax
import jax.numpy as jnp
from jax import lax
from jax.experimental import pallas as pl
from jax.experimental.pallas import tpu as pltpu
from jax.sharding import PartitionSpec as P

F32 = jnp.float32
BF16 = jnp.bfloat16
HALO = 3
LIMIT = 24


def dot(a, b):
    return jnp.dot(a, b, preferred_element_type=F32)


def dot_t(a, b):
    return lax.dot_general(a, b, (((1,), (1,)), ((), ())), preferred_element_type=F32)


def spans(channels):
    return [(at, min(128, channels - at)) for at in range(0, channels, 128)]


def scales(squares, channels):
    total = dot(squares, jnp.ones((channels, 128), BF16))
    return lax.rsqrt(total * (1.0 / channels) + 1e-06)


def activated(v, scale, gain):
    u = v * scale * gain
    return u * (0.5 + 0.5 * jnp.tanh(0.5 * u))


def column_masks(width, channels):
    column = lax.broadcasted_iota(jnp.int32, (width, channels), 0)
    return column == 0, column == width - 1


def beside(v, masks):
    width = v.shape[0]
    left = jnp.where(masks[0], 0.0, pltpu.roll(v, 1, 0))
    right = jnp.where(masks[1], 0.0, pltpu.roll(v, width - 1, 0))
    return left, right


def call(kernel, out_shape, scratch, flops, args, hbm=(), out_hbm=(), aliases=None):
    vmem = pl.BlockSpec(memory_space=pltpu.VMEM)
    far = pl.BlockSpec(memory_space=pltpu.HBM)
    args = [pltpu.with_memory_space_constraint(x, pltpu.HBM) if i in hbm else x for i, x in enumerate(args)]

    def placed(*refs):
        kernel([f(axis) for f in (lax.axis_index, lax.axis_size) for axis in ("tm", "rows")], *refs)

    return pl.pallas_call(
        placed,
        out_shape=out_shape,
        in_specs=[far if i in hbm else vmem for i in range(len(args))],
        out_specs=tuple(far if i in out_hbm else vmem for i in range(len(out_shape))),
        scratch_shapes=scratch,
        input_output_aliases=aliases or {},
        compiler_params=pltpu.CompilerParams(vmem_limit_bytes=LIMIT << 20),
        cost_estimate=pl.CostEstimate(flops=flops, bytes_accessed=4 << 20, transcendentals=0),
    )(*args)


def pack_rows(ref, rows, get):
    for row in range(0, rows, 2):
        upper, lower = get(row), get(row + 1)
        ref[row] = upper[:, 0:128].astype(BF16)
        ref[row + 1] = lower[:, 0:128].astype(BF16)
        ref[rows + row // 2] = jnp.concatenate([upper[:, 128:192], lower[:, 128:192]], axis=1).astype(BF16)


def unpack_row(ref, row):
    rows = ref.shape[0] * 2 // 3
    rest = ref[rows + row // 2].astype(F32)
    side = 64 * (row % 2)
    return jnp.concatenate([ref[row].astype(F32), rest[:, side : side + 64]], axis=1)


def fill_field(field, rows, first, rest):
    width = field.shape[2]
    masks = column_masks(width, 128)
    for row in range(rows):
        for at, part in ((0, first(row)), (128, rest(row))):
            left, right = beside(part, masks)
            for shift, value in enumerate((left, part, right)):
                field[shift, row, :, at : at + 128] = value.astype(BF16)


def packed_parts(ref, follows=None):
    rows = ref.shape[0] * 2 // 3

    def guard(value):
        value = value.astype(F32)
        return value if follows is None else jnp.where(follows, value, 0.0)

    def first(row):
        return guard(ref[row])

    def rest(row):
        at = rows + row // 2
        if row % 2 == 0:
            return guard(ref[at])
        upper = ref[at].astype(F32)[:, 64:128]
        lower = jnp.zeros_like(upper) if row == rows - 1 else ref[at + 1].astype(F32)[:, 0:64]
        return guard(jnp.concatenate([upper, lower], axis=1))

    return rows, first, rest


def row_parts(rows, get):
    made = {}

    def row_of(row):
        if row not in made:
            made[row] = get(row)
        return made[row]

    def rest(row):
        upper = row_of(row)[:, 128:192]
        lower = row_of(row + 1)[:, 128:192] if row < rows - 1 else jnp.zeros_like(upper)
        return jnp.concatenate([upper, lower], axis=1)

    return rows, lambda row: row_of(row)[:, 0:128], rest


def two_rows(field, shift, row, rows):
    pixels = rows * field.shape[2]
    return [
        field[shift, row : row + rows].reshape(pixels, 256),
        field[shift, row + 1 : row + 1 + rows, :, 0:128].reshape(pixels, 128),
    ]


def two_rows_weights(upper, lower):
    return [upper, lower[128:192], lower[0:128]]


def convolve_field(kernel, terms, rows):
    lanes, weights = [], []
    for field, a in terms:
        for e in range(3):
            lanes += two_rows(field, e, 0, rows)
            weights += two_rows_weights(kernel[a, 0, e], kernel[a, 1, e])
            lanes.append(field[e, 2 : 2 + rows].reshape(rows * field.shape[2], 256))
            weights += [kernel[a, 2, e], jnp.zeros((64, 192), BF16)]
    return dot(jnp.concatenate(lanes, axis=1), jnp.concatenate(weights, axis=0))


def convolve(acc, product, kernel, terms, rows, width):
    masks = column_masks(width, 192)
    fields = [window(b) for window, a in terms for b in range(3)]
    if product is dot_t:
        fields = [jnp.concatenate(fields, axis=1)]
    for e in range(3):
        taps = [kernel[a, b, e] for window, a in terms for b in range(3)]
        if product is dot_t:
            taps = [jnp.concatenate(taps, axis=1)]
        total = None
        for field, tap in zip(fields, taps):
            term = product(field, tap)
            total = term if total is None else total + term
        for row in range(rows):
            part = slice(row * width, (row + 1) * width)
            moved = total[part]
            if e == 0:
                acc[part] = jnp.where(masks[0], 0.0, pltpu.roll(moved, 1, 0))
            elif e == 1:
                acc[part] += moved
            else:
                acc[part] += jnp.where(masks[1], 0.0, pltpu.roll(moved, width - 1, 0))


def windows(ref, rows):
    return lambda b: ref[b : b + rows].reshape(rows * ref.shape[1], ref.shape[2])


OWN = (((0, 2),), ((0, 1), (1, 2)))


def activate_rows(ref, gain, squares, scale, out):
    rows, width, channels = ref.shape
    pixels = rows * width
    v = ref[...].astype(F32)
    squares[0:pixels] = (v * v).astype(BF16).reshape(pixels, channels)
    scale[0:pixels] = scales(squares[0:pixels], channels)
    for row in range(rows):
        part = slice(row * width, (row + 1) * width)
        for at, lanes in spans(channels):
            out[row, :, at : at + lanes] = activated(
                ref[row, :, at : at + lanes].astype(F32), scale[part], gain[at : at + lanes].reshape(1, lanes)
            ).astype(BF16)


def inner_kernel(place, latents, gain, kernel, held, weights, active, sums, held_gain, squares, scale, sems):
    frames, rows, width, channels = held.shape
    copies = [
        pltpu.make_async_copy(latents.at[1], held.at[1], sems.at[0]),
        pltpu.make_async_copy(latents.at[0], held.at[0], sems.at[1]),
        pltpu.make_async_copy(kernel, weights, sems.at[2]),
        pltpu.make_async_copy(gain, held_gain, sems.at[3]),
    ]
    for copy in (copies[0], copies[3], copies[1], copies[2]):
        copy.start()
    copies[3].wait()
    for frame, copy in ((1, copies[0]), (0, copies[1])):
        copy.wait()
        activate_rows(held.at[frame], held_gain, squares, scale, active.at[frame])
    copies[2].wait()
    count = rows - 2
    convolve(sums, dot_t, weights, [(windows(active.at[1], count), 0)], count, width)


def fill_edges(place, near, far, frame, gain, active, edges, raw, squares, scale):
    odd = place[1] % 2 == 1
    inner = jnp.logical_and(place[1] > 0, place[1] < place[3] - 1)
    rows = active.shape[1]
    for row in range(HALO):
        chip = near[frame, row]
        next_chip = jnp.where(inner, far[frame, row], jnp.zeros_like(chip))
        raw[row] = jnp.where(odd, chip, next_chip)
        raw[HALO + row] = jnp.where(odd, next_chip, chip)
    activate_rows(raw.at[0:HALO], gain, squares, scale, edges.at[0, 0:HALO])
    activate_rows(raw.at[HALO : 2 * HALO], gain, squares, scale, edges.at[1, 2 : 2 + HALO])
    edges[0, HALO : HALO + 2] = active[frame, 0:2]
    edges[1, 0:2] = active[frame, rows - 2 : rows]


def edge_windows(edges):
    width, channels = edges.shape[2], edges.shape[3]
    return lambda b: edges[:, b : b + HALO].reshape(2 * HALO * width, channels)


def pack_joined(partial, sums, acc, wide, width):
    def get(row):
        if HALO <= row < wide - HALO:
            return sums[(row - HALO) * width : (row - HALO + 1) * width]
        at = row if row < HALO else row - (wide - 2 * HALO)
        return acc[at * width : (at + 1) * width]

    pack_rows(partial, wide, get)


def late_edge_kernel(
    place, near, far, gain, active, weights, sums, partial, edges, acc, raw, squares, scale
):
    fill_edges(place, near, far, 1, gain, active, edges, raw, squares, scale)
    width = active.shape[2]
    convolve(acc, dot_t, weights, [(edge_windows(edges), 0)], 2 * HALO, width)
    pack_joined(partial, sums, acc, active.shape[1] + 4, width)


def early_edge_kernel(
    place, near, far, gain, active, weights, late, partial, tall, edges, acc, raw, squares, scale
):
    fill_edges(place, near, far, 0, gain, active, edges, raw, squares, scale)
    rows, width = active.shape[1], active.shape[2]
    for frame, ends in ((0, edges), (1, late)):
        tall[frame, 0:HALO] = ends[0, 0:HALO]
        tall[frame, HALO : HALO + rows] = active[frame]
        tall[frame, HALO + rows :] = ends[1, 2:]
    wide = rows + 4
    convolve(
        acc, dot_t, weights, [(windows(tall.at[0], wide), 0), (windows(tall.at[1], wide), 1)], wide, width
    )
    pack_rows(partial, wide, lambda row: acc[row * width : (row + 1) * width])


def first_own_kernel(place, active, kernel, third, own, mixed):
    wide, width = active.shape[1] - 2, active.shape[2]
    for out in (1, 0):
        terms = [(windows(active.at[frame], wide), a) for frame, a in OWN[out]]
        convolve(own.at[out], dot_t, kernel, terms, wide, width)
    mix_weights(third, mixed)


def finish(place, own, before, gain, raw, squares, scale, keep):
    tall, width = before.shape[0] * 2 // 3, before.shape[1]
    start = place[1] * 8 - (tall - 8) // 2
    follows = place[0] > 0
    for row in range(tall):
        part = slice(row * width, (row + 1) * width)
        earlier = jnp.where(follows, unpack_row(before, row), 0.0)
        total = (own[part] + earlier).astype(BF16)
        raw[part] = total
        keep(row, total)
        total = total.astype(F32)
        squares[part] = (total * total).astype(BF16)
    scale[...] = scales(squares[...], 192)

    def get(row):
        part = slice(row * width, (row + 1) * width)
        inside = jnp.logical_and(start + row >= 0, start + row < place[3] * 8)
        lanes = []
        for at, count in spans(192):
            v = activated(
                raw[part, at : at + count].astype(F32), scale[part, 0:count], gain[at : at + count].reshape(1, count)
            )
            if not (tall - 8) // 2 <= row < (tall + 8) // 2:
                v = jnp.where(inside, v, 0.0)
            lanes.append(v)
        return jnp.concatenate(lanes, axis=1)

    return get


def second(place, own, before, gain, kernel, terms, partial, field, raw, squares, scale):
    rows = field.shape[1]
    width, wide = field.shape[2], rows - 2
    get = finish(place, own, before, gain, raw, squares, scale, lambda row, total: None)
    fill_field(field, *row_parts(rows, get))
    total = convolve_field(kernel, terms, wide)
    pack_rows(partial, wide, lambda row: total[row * width : (row + 1) * width])


def late_second_kernel(place, own, before, gain, kernel, partial, field, raw, squares, scale):
    terms = [(field, 0)]
    second(place, own.at[1], before, gain, kernel, terms, partial, field, raw, squares, scale)


def early_second_kernel(place, own, before, gain, kernel, late, partial, field, raw, squares, scale):
    terms = [(field, 0), (late, 1)]
    second(place, own.at[0], before, gain, kernel, terms, partial, field, raw, squares, scale)


def second_own_kernel(place, early, late, kernel, latents, near, far, shortcut, own):
    wide, width = early.shape[1] - 2, early.shape[2]
    pixels = wide * width
    rows, channels = latents.shape[1], latents.shape[3]
    odd = place[1] % 2
    inner = wide - 1
    fields = (early, late)
    for out in (1, 0):
        own[out] = convolve_field(kernel, [(fields[frame], a) for frame, a in OWN[out]], wide)
        body = latents[out].reshape(rows * width, channels)
        own[out, width : pixels - width] += dot_t(body, shortcut[...])
        other = dot_t(near[out, jnp.where(odd == 1, HALO - 1, 0)], shortcut[...])
        own[out, pl.ds(jnp.where(odd == 1, 0, inner * width), width)] += other
        other = dot_t(far[out, jnp.where(odd == 1, 0, HALO - 1)], shortcut[...])
        own[out, pl.ds(jnp.where(odd == 1, inner * width, 0), width)] += other


def third(place, own, before, gain, block, packed, raw, squares, scale):
    tall = packed.shape[0] * 2 // 3

    def keep(row, total):
        if 0 < row < tall - 1:
            block[row - 1] = total

    pack_rows(packed, tall, finish(place, own, before, gain, raw, squares, scale, keep))


def late_third_kernel(place, own, before, gain, block, packed, raw, squares, scale):
    third(place, own.at[1], before, gain, block, packed, raw, squares, scale)


def early_third_kernel(place, own, before, gain, block, packed, raw, squares, scale):
    third(place, own.at[0], before, gain, block, packed, raw, squares, scale)


def mix_weights(kernel, out):
    def halves(taps, parity):
        if parity == 0:
            return taps[0], taps[1] + taps[2]
        return taps[0] + taps[1], taps[2]

    for a in range(3):
        for i in range(2):
            rows = [halves([kernel[a, b, e].astype(F32) for b in range(3)], i) for e in range(3)]
            for j in range(2):
                upper = halves([rows[e][0] for e in range(3)], j)
                lower = halves([rows[e][1] for e in range(3)], j)
                for column in range(2):
                    at = 384 * column
                    for part in two_rows_weights(upper[column].astype(BF16), lower[column].astype(BF16)):
                        out[a, 2 * i + j, at : at + part.shape[0]] = part
                        at += part.shape[0]


def phase(terms, kernel, i, j, rows):
    lanes, weights = [], []
    for field, a in terms:
        for shift in (j, j + 1):
            lanes += two_rows(field, shift, i, rows)
        weights.append(kernel[a, 2 * i + j])
    return dot(jnp.concatenate(lanes, axis=1), jnp.concatenate(weights, axis=0))


def third_own_kernel(place, early, late, kernel, early_out, late_out, own, block_out, fields, sems):
    copies = [
        pltpu.make_async_copy(block, block_out.at[frame], sems.at[frame])
        for frame, block in enumerate((early_out, late_out))
    ]
    for copy in copies:
        copy.start()
    for frame, packed in enumerate((early, late)):
        fill_field(fields.at[frame], *packed_parts(packed))
    rows = early_out.shape[0]
    for out in (1, 0):
        terms = [(fields.at[frame], a) for frame, a in OWN[out]]
        for i in range(2):
            for j in range(2):
                own[out, 2 * i + j] = phase(terms, kernel, i, j, rows)
    for copy in copies:
        copy.wait()


def weave(total, j, rows, width, woven):
    for row in range(rows):
        value = total[row * width : (row + 1) * width]
        woven[row, 0, pl.ds(j, width, stride=2)] = value[:, 0:128]
        woven[row, 1, pl.ds(j, width, stride=2), 0:64] = value[:, 128:192]


def write_out(own, field, kernel, a, rows, width, woven, fine, out, sems):
    copies = []
    for i in range(2):
        for j in range(2):
            total = own[2 * i + j] + phase([(field, a)], kernel, i, j, rows)
            weave(total, j, rows, width, woven.at[i])
        for row in range(rows):
            fine[i, row, :, 0:128] = woven[i, row, 0].astype(BF16)
            fine[i, row, :, 128:192] = woven[i, row, 1, :, 0:64].astype(BF16)
        copies.append(pltpu.make_async_copy(fine.at[i], out.at[:, i], sems.at[i]))
        copies[-1].start()
    return copies


def late_last_kernel(place, packed, kernel, own, decoded, rest, field, woven, fine, sems):
    rows, width = packed.shape[0] * 2 // 3 - 2, packed.shape[1]
    fill_field(field, *packed_parts(packed, place[0] > 0))
    copies = write_out(own.at[1], field, kernel, 0, rows, width, woven, fine, decoded.at[1], sems)
    for i in range(2):
        for j in range(2):
            rest[2 * i + j] = own[0, 2 * i + j] + phase([(field, 1)], kernel, i, j, rows)
    for copy in copies:
        copy.wait()


def early_last_kernel(place, packed, kernel, rest, late, decoded, field, woven, fine, sems):
    rows, width = packed.shape[0] * 2 // 3 - 2, packed.shape[1]
    fill_field(field, *packed_parts(packed, place[0] > 0))
    for copy in write_out(rest, field, kernel, 0, rows, width, woven, fine, decoded.at[0], sems):
        copy.wait()


def onward(value):
    count = lax.axis_size("tm")
    return lax.ppermute(value, "tm", [(i, (i + 1) % count) for i in range(count)])


def swap(value, offset):
    count = lax.axis_size("rows")
    pairs = [(i, i + 1) for i in range(offset, count - 1, 2)]
    alone = set(range(count)) - {i for pair in pairs for i in pair}
    return lax.ppermute(
        value, "rows", pairs + [(b, a) for a, b in pairs] + [(i, i) for i in sorted(alone)]
    )


def body(
    latents,
    gain_first,
    kernel_first,
    gain_second,
    kernel_second,
    shortcut,
    gain_third,
    kernel_third,
):
    frames, rows, width, channels = latents.shape
    shape = jax.ShapeDtypeStruct
    odd = lax.axis_index("rows") % 2
    near = lax.dynamic_slice_in_dim(latents, (rows - HALO) * (1 - odd), HALO, 1)
    far = lax.dynamic_slice_in_dim(latents, (rows - HALO) * odd, HALO, 1)
    near, far = swap(near, 0), swap(far, 1)

    wide1, wide2 = rows + 4, rows + 2
    pixels, pixels1, pixels2 = rows * width, wide1 * width, wide2 * width
    flops1, flops2, flops3 = (18 * n * 192 for n in (pixels1 * channels, pixels2 * 192, pixels * 192))
    dma = pltpu.SemaphoreType.DMA

    def work(tall, channels):
        return [pltpu.VMEM((tall * width, channels), BF16), pltpu.VMEM((tall * width, 128), F32)]

    held, weights, active, sums, gain_first = call(
        inner_kernel,
        (
            shape(latents.shape, BF16),
            shape((3, 3, 3, 192, channels), BF16),
            shape(latents.shape, BF16),
            shape(((rows - 2) * width, 192), F32),
            shape((channels,), F32),
        ),
        work(rows, channels) + [dma((4,))],
        2 * flops1,
        (latents, gain_first, jnp.swapaxes(kernel_first, 3, 4)),
        hbm=(0, 1, 2),
    )
    edge_work = [pltpu.VMEM((2 * HALO, width, channels), BF16)] + work(HALO, channels)
    ends = shape((2, HALO + 2, width, channels), BF16)
    packed1 = shape((wide1 * 3 // 2, width, 128), BF16)
    partial, late = call(
        late_edge_kernel,
        (packed1, ends),
        [pltpu.VMEM((2 * HALO * width, 192), F32)] + edge_work,
        flops1 // 2,
        (near, far, gain_first, active, weights, sums),
    )
    before_late = onward(partial)
    partial, tall = call(
        early_edge_kernel,
        (packed1, shape((2, wide1 + 2, width, channels), BF16)),
        [pltpu.VMEM(ends.shape, BF16), pltpu.VMEM((pixels1, 192), F32)] + edge_work,
        2 * flops1,
        (near, far, gain_first, active, weights, late),
    )
    before_early = onward(partial)
    own, mixed = call(
        first_own_kernel,
        (shape((2, pixels1, 192), F32), shape((3, 4, 768, 192), BF16)),
        [],
        3 * flops1,
        (tall, weights, kernel_third),
    )
    second_work = [pltpu.VMEM((pixels1, 192), BF16)] + work(wide1, 192)
    packed2 = shape((wide2 * 3 // 2, width, 128), BF16)
    field = shape((3, wide1, width, 256), BF16)
    partial, late = call(
        late_second_kernel,
        (packed2, field),
        second_work,
        flops2,
        (own, before_late, gain_second, kernel_second),
    )
    before_late = onward(partial)
    partial, early = call(
        early_second_kernel,
        (packed2, field),
        second_work,
        2 * flops2,
        (own, before_early, gain_second, kernel_second, late),
    )
    before_early = onward(partial)
    (own,) = call(
        second_own_kernel,
        (shape((2, pixels2, 192), F32),),
        [],
        3 * flops2,
        (early, late, kernel_second, held, near, far, shortcut.T),
    )
    third_work = [pltpu.VMEM((pixels2, 192), BF16)] + work(wide2, 192)
    block = shape((rows, width, 192), BF16)
    late_out, late = call(
        late_third_kernel,
        (block, packed2),
        third_work,
        1 << 24,
        (own, before_late, gain_third),
    )
    before_late = onward(late)
    early_out, early = call(
        early_third_kernel,
        (block, packed2),
        third_work,
        1 << 24,
        (own, before_early, gain_third),
    )
    before_early = onward(early)
    own, block_out = call(
        third_own_kernel,
        (shape((2, 4, pixels, 192), F32), shape((2, rows, width, 192), BF16)),
        [pltpu.VMEM((2, 3, wide2, width, 256), BF16), dma((2,))],
        3 * flops3,
        (early, late, mixed, early_out, late_out),
        out_hbm=(1,),
    )
    last_work = [
        pltpu.VMEM((3, wide2, width, 256), BF16),
        pltpu.VMEM((2, rows, 2, 2 * width, 128), F32),
        pltpu.VMEM((2, rows, 2 * width, 192), BF16),
        dma((2,)),
    ]
    fine = shape((2, rows, 2, 2 * width, 192), BF16)
    decoded, rest = call(
        late_last_kernel,
        (fine, shape((4, pixels, 192), F32)),
        last_work,
        2 * flops3,
        (before_late, mixed, own),
        out_hbm=(0,),
    )
    (decoded,) = call(
        early_last_kernel,
        (fine,),
        last_work,
        flops3,
        (before_early, mixed, rest, decoded),
        hbm=(3,),
        out_hbm=(0,),
        aliases={3: 0},
    )
    decoded = decoded.reshape(2, 2 * rows, 2 * width, 192)
    return (block_out, decoded)


def solution(mesh):
    return jax.shard_map(
        body,
        mesh=mesh,
        in_specs=(P("tm", "rows", None, None), P(), P(), P(), P(), P(), P(), P()),
        out_specs=(P("tm", "rows", None, None), P("tm", "rows", None, None)),
        check_vma=False,
    )
```

time: 51.6 us -> 47.1 us (0.913)
  the two profiles are of different devices: /device:TPU:24 before, /device:TPU:128 now
where the time goes in v3:
time: 47.1 us; the launch traced here: 46.7 us
  Pallas kernels  23.9 us (51%)
  waiting for transfers between devices  11.7 us (25%)
  starting transfers between devices  9.06 us (19%)
  local copies, waits for them, and re-layouts  1.12 us (2%)
  between operations  0.92 us (2%)
    pallas_call x12, Pallas kernels, call(): pl.pallas_call(placed, out_shape=out_shape, in_specs=[far if i in hbm els...  23.9 us
    ppermute x6, waiting for transfers between devices, onward(): lax.ppermute(value, 'tm', [(i, (i + 1) % count) for i in range(count)])  8.16 us
    ppermute x6, starting transfers between devices, onward(): lax.ppermute(value, 'tm', [(i, (i + 1) % count) for i in range(count)])  5.32 us
    ppermute x2, starting transfers between devices, swap(): lax.ppermute(value, 'rows', pairs + [(b, a) for a, b in pairs] + [(i, i)...  3.74 us
    ppermute x2, waiting for transfers between devices, swap(): lax.ppermute(value, 'rows', pairs + [(b, a) for a, b in pairs] + [(i, i)...  3.56 us
    dynamic_slice x1, local copies, waits for them, and re-layouts, body(): far = lax.dynamic_slice_in_dim(latents, (rows - HALO) * odd, HALO, 1)  1.1 us
  transfers between devices with their start and end apart: 8, of which 4 were waited for; matrix products, arithmetic and copies ran while one was open for 0% of the time, Pallas kernels for 45%

profile of v3, /device:TPU:128, one launch (start us, length us, event | category | flops | bytes accessed | tf_op | source)
XLA Modules:
  0.0 46.7 jit_solution(2153254234751917941)
XLA Ops:
  0.6 1.1 %constant_dynamic-slice_fusion = (bf16[2,3,48,384]{3,2,1,0:T(8,128)(2,1)S(1)}, bf16[2,3,48,384]{3,2,1,0:T(8,128)(2,1)S(1)}) fusion(bf16[2,8,48,384]{3,2,1,0:T(8,128)(2,1)} %refs_0_.1, s32[]{:T(128)S(6)} %select_n.15, s32[]{:T(128)S(6)} %select_n.14), kind=kLoop, calls=%fused_computation | loop fusion | bytes 884744 | tf_op jit(solution)/shard_map/dynamic_slice | solution.py:478
  1.8 3.7 %collective-permute-start.1 = (bf16[2,3,48,384]{3,2,1,0:T(8,128)(2,1)S(1)}, bf16[2,3,48,384]{3,2,1,0:T(8,128)(2,1)S(1)}, u32[]{:S(2)}, u32[]{:S(2)}) collective-permute-start(bf16[2,3,48,384]{3,2,1,0:T(8,128)(2,1)S(1)} %get-tuple-element.48), channel_id=1, source_target_pairs={{1,2},{3,4},{5,6},{7,8},{9,10},{11,12},{13,14},{15,16},{17,18},{19... | collective-permute-start | bytes 663560 | tf_op jit(solution)/shard_map/ppermute | solution.py:459
  5.4 0.1 collective-permute-start
  5.5 3.2 %shard_map.95 = (bf16[2,8,48,384]{3,2,1,0:T(8,128)(2,1)S(1)}, bf16[3,3,3,192,384]{4,3,2,1,0:T(8,128)(2,1)S(1)}, bf16[2,8,48,384]{3,2,1,0:T(8,128)(2,1)S(1)}, f32[288,192]{1,0:T(8,128)S(1)}, f32[384]{0:T(512)S(1)}) custom-call(bf16[2,8,48,384]{3,2,1,0:T(8,128)(2,1)} %refs_0_.1, f32[384]{0:T(512)} %refs_1_.1, bf16[3,3,3,192,384]{4,3,2,1,0:T(8,128)(2,1)} %bitcast.5), custom_call_target="tpu_custom_call" | custom-call | flops 1528823808 | bytes 4194304 | tf_op jit(solution)/shard_map/pallas_call | solution.py:56
  8.8 3.6 %collective-permute-done.1.refs_1_.refs_5_ = bf16[2,3,48,384]{3,2,1,0:T(8,128)(2,1)S(1)} collective-permute-done((bf16[2,3,48,384]{3,2,1,0:T(8,128)(2,1)S(1)}, bf16[2,3,48,384]{3,2,1,0:T(8,128)(2,1)S(1)}, u32[]{:S(2)}, u32[]{:S(2)}) %collective-permute-start.1) | collective-permute-done | bytes 221216 | tf_op jit(solution)/shard_map/ppermute | solution.py:459
  12.3 0.0 collective-permute-done.refs_0_.refs_4_
  12.3 1.1 %shard_map.96 = (bf16[18,48,128]{2,1,0:T(8,128)(2,1)S(1)}, bf16[2,5,48,384]{3,2,1,0:T(8,128)(2,1)S(1)}) custom-call(bf16[2,3,48,384]{3,2,1,0:T(8,128)(2,1)S(1)} %collective-permute-done.refs_0_.refs_4_, bf16[2,3,48,384]{3,2,1,0:T(8,128)(2,1)S(1)} %collective-permute-done.1.refs_1_.refs_5_, f32[384]{0:T(512)S(1)} %get-tuple-element.25.refs_2_, ...), custom_call_target="tpu_custom_call" | custom-call | flops 382205952 | bytes 4194304 | tf_op jit(solution)/shard_map/pallas_call | solution.py:56
  13.5 1.6 %collective-permute-start.3 = (bf16[18,48,128]{2,1,0:T(8,128)(2,1)S(1)}, bf16[18,48,128]{2,1,0:T(8,128)(2,1)S(1)}, u32[]{:S(2)}, u32[]{:S(2)}) collective-permute-start(bf16[18,48,128]{2,1,0:T(8,128)(2,1)S(1)} %get-tuple-element.33), channel_id=1, source_target_pairs={{0,64},{64,128},{128,192},{192,0},{1,65},{65,129},{129,193},{193,1... | collective-permute-start | bytes 663560 | tf_op jit(solution)/shard_map/ppermute | solution.py:452
  15.1 0.0 copy-start.4
  15.1 2.6 %shard_map.97 = (bf16[18,48,128]{2,1,0:T(8,128)(2,1)S(1)}, bf16[2,14,48,384]{3,2,1,0:T(8,128)(2,1)S(1)}) custom-call(bf16[2,3,48,384]{3,2,1,0:T(8,128)(2,1)S(1)} %collective-permute-done.refs_0_.refs_4_, bf16[2,3,48,384]{3,2,1,0:T(8,128)(2,1)S(1)} %collective-permute-done.1.refs_1_.refs_5_, f32[384]{0:T(512)S(1)} %get-tuple-element.25.refs_2_, ...), custom_call_target="tpu_custom_call" | custom-call | flops 1528823808 | bytes 4194304 | tf_op jit(solution)/shard_map/pallas_call | solution.py:56
  17.7 1.6 %collective-permute-start.2 = (bf16[18,48,128]{2,1,0:T(8,128)(2,1)S(1)}, bf16[18,48,128]{2,1,0:T(8,128)(2,1)S(1)}, u32[]{:S(2)}, u32[]{:S(2)}) collective-permute-start(bf16[18,48,128]{2,1,0:T(8,128)(2,1)S(1)} %get-tuple-element.32), channel_id=1, source_target_pairs={{0,64},{64,128},{128,192},{192,0},{1,65},{65,129},{129,193},{193,1... | collective-permute-start | bytes 663560 | tf_op jit(solution)/shard_map/ppermute | solution.py:452
  19.4 0.0 copy-done.4
  19.4 0.0 copy-start
  19.4 0.0 copy-start.3
  19.4 4.7 %shard_map.98 = (f32[2,576,192]{2,1,0:T(8,128)S(1)}, bf16[3,4,768,192]{3,2,1,0:T(8,128)(2,1)S(1)}) custom-call(bf16[2,14,48,384]{3,2,1,0:T(8,128)(2,1)S(1)} %get-tuple-element.30.refs_0_, bf16[3,3,3,192,384]{4,3,2,1,0:T(8,128)(2,1)S(1)} %get-tuple-element.27.refs_4_.refs_1_, bf16[3,3,3,192,192]{4,3,2,1,0:T(8,128)(2,1)S(1)} %copy-done.4), custom_call_target="tpu_custom_call" | custom-call | flops 2293235712 | bytes 4194304 | tf_op jit(solution)/shard_map/pallas_call | solution.py:56
  24.1 0.0 collective-permute-done.3.refs_1_
  24.1 0.0 copy-done
  24.1 0.0 copy-done.3
  24.1 1.3 %shard_map.99 = (bf16[15,48,128]{2,1,0:T(8,128)(2,1)S(1)}, bf16[3,12,48,256]{3,2,1,0:T(8,128)(2,1)S(1)}) custom-call(f32[2,576,192]{2,1,0:T(8,128)S(1)} %get-tuple-element.31.refs_0_, bf16[18,48,128]{2,1,0:T(8,128)(2,1)S(1)} %collective-permute-done.3.refs_1_, f32[192]{0:T(256)S(1)} %copy-done.3, bf16[3,3,3,192,192]{4,3,2,1,0:T(8,128)(2,1)S(1)} %copy-done), custom_call_target="tpu_custom_call" | custom-call | flops 318504960 | bytes 4194304 | tf_op jit(solution)/shard_map/pallas_call | solution.py:56
  25.4 0.0 copy-start.1
  25.4 1.5 %collective-permute-start.5 = (bf16[15,48,128]{2,1,0:T(8,128)(2,1)S(1)}, bf16[15,48,128]{2,1,0:T(8,128)(2,1)S(1)}, u32[]{:S(2)}, u32[]{:S(2)}) collective-permute-start(bf16[15,48,128]{2,1,0:T(8,128)(2,1)S(1)} %get-tuple-element.39), channel_id=1, source_target_pairs={{0,64},{64,128},{128,192},{192,0},{1,65},{65,129},{129,193},{193,1... | collective-permute-start | bytes 552968 | tf_op jit(solution)/shard_map/ppermute | solution.py:452
  26.9 0.0 collective-permute-done.2.refs_1_
  26.9 1.8 %shard_map.100 = (bf16[15,48,128]{2,1,0:T(8,128)(2,1)S(1)}, bf16[3,12,48,256]{3,2,1,0:T(8,128)(2,1)S(1)}) custom-call(f32[2,576,192]{2,1,0:T(8,128)S(1)} %get-tuple-element.31.refs_0_, bf16[18,48,128]{2,1,0:T(8,128)(2,1)S(1)} %collective-permute-done.2.refs_1_, f32[192]{0:T(256)S(1)} %copy-done.3, bf16[3,3,3,192,192]{4,3,2,1,0:T(8,128)(2,1)S(1)} %copy-done, ...), custom_call_target="tpu_custom_call" | custom-call | flops 637009920 | bytes 4194304 | tf_op jit(solution)/shard_map/pallas_call | solution.py:56
  28.7 0.3 collective-permute-start.4
  29.0 0.0 copy-done.1
  29.0 0.0 copy-start.2
  29.0 2.1 %shard_map.101.refs_0_ = f32[2,480,192]{2,1,0:T(8,128)S(1)} custom-call(bf16[3,12,48,256]{3,2,1,0:T(8,128)(2,1)S(1)} %get-tuple-element.35.refs_0_, bf16[3,12,48,256]{3,2,1,0:T(8,128)(2,1)S(1)} %get-tuple-element.34.refs_4_.refs_1_, bf16[3,3,3,192,192]{4,3,2,1,0:T(8,128)(2,1)S(1)} %copy-done, bf16[2,8,48,384]{3,2,1,0:T(8,128)(2,1)S(1)} %get-tuple-element.36.refs_3_, ...), custom_call_target="tpu_custom_call" | custom-call | flops 955514880 | bytes 4194304 | tf_op jit(solution)/shard_map/pallas_call | solution.py:56
  31.1 2.2 %collective-permute-done.5.refs_1_ = bf16[15,48,128]{2,1,0:T(8,128)(2,1)S(1)} collective-permute-done((bf16[15,48,128]{2,1,0:T(8,128)(2,1)S(1)}, bf16[15,48,128]{2,1,0:T(8,128)(2,1)S(1)}, u32[]{:S(2)}, u32[]{:S(2)}) %collective-permute-start.5) | collective-permute-done | bytes 184352 | tf_op jit(solution)/shard_map/ppermute | solution.py:452
  33.3 0.0 copy-done.2
  33.3 0.4 shard_map.103
  33.7 0.1 collective-permute-start.7
  33.8 3.7 %collective-permute-done.4.refs_1_ = bf16[15,48,128]{2,1,0:T(8,128)(2,1)S(1)} collective-permute-done((bf16[15,48,128]{2,1,0:T(8,128)(2,1)S(1)}, bf16[15,48,128]{2,1,0:T(8,128)(2,1)S(1)}, u32[]{:S(2)}, u32[]{:S(2)}) %collective-permute-start.4) | collective-permute-done | bytes 184352 | tf_op jit(solution)/shard_map/ppermute | solution.py:452
  37.5 0.4 shard_map.102
  38.0 0.1 collective-permute-start.6
  38.0 2.7 %shard_map.104 = (f32[2,4,384,192]{3,2,1,0:T(8,128)S(1)}, bf16[2,8,48,192]{3,2,1,0:T(8,128)(2,1)}) custom-call(bf16[15,48,128]{2,1,0:T(8,128)(2,1)S(1)} %get-tuple-element.38.refs_0_, bf16[15,48,128]{2,1,0:T(8,128)(2,1)S(1)} %get-tuple-element.40.refs_1_, bf16[3,4,768,192]{3,2,1,0:T(8,128)(2,1)S(1)} %get-tuple-element.41.refs_2_.refs_1_, ...), custom_call_target="tpu_custom_call" | custom-call | flops 764411904 | bytes 4194304 | tf_op jit(solution)/shard_map/pallas_call | solution.py:56
  40.7 0.0 collective-permute-done.7.refs_0_
  40.7 1.8 %shard_map.105 = (bf16[2,8,2,96,192]{4,3,2,1,0:T(8,128)(2,1)}, f32[4,384,192]{2,1,0:T(8,128)S(1)}) custom-call(bf16[15,48,128]{2,1,0:T(8,128)(2,1)S(1)} %collective-permute-done.7.refs_0_, bf16[3,4,768,192]{3,2,1,0:T(8,128)(2,1)S(1)} %get-tuple-element.41.refs_2_.refs_1_, f32[2,4,384,192]{3,2,1,0:T(8,128)S(1)} %get-tuple-element.45.refs_2_), custom_call_target="tpu_custom_call" | custom-call | flops 509607936 | bytes 4194304 | tf_op jit(solution)/shard_map/pallas_call | solution.py:56
  42.5 2.3 %collective-permute-done.6.refs_0_ = bf16[15,48,128]{2,1,0:T(8,128)(2,1)S(1)} collective-permute-done((bf16[15,48,128]{2,1,0:T(8,128)(2,1)S(1)}, bf16[15,48,128]{2,1,0:T(8,128)(2,1)S(1)}, u32[]{:S(2)}, u32[]{:S(2)}) %collective-permute-start.6) | collective-permute-done | bytes 184352 | tf_op jit(solution)/shard_map/ppermute | solution.py:452
  44.8 1.7 %shard_map.106 = bf16[2,8,2,96,192]{4,3,2,1,0:T(8,128)(2,1)} custom-call(bf16[15,48,128]{2,1,0:T(8,128)(2,1)S(1)} %collective-permute-done.6.refs_0_, bf16[3,4,768,192]{3,2,1,0:T(8,128)(2,1)S(1)} %get-tuple-element.41.refs_2_.refs_1_, f32[4,384,192]{2,1,0:T(8,128)S(1)} %get-tuple-element.46.refs_2_, ...), custom_call_target="tpu_custom_call", output_to_operand_aliasing={{}: (3, {})} | custom-call | flops 254803968 | bytes 4194304 | tf_op jit(solution)/shard_map/pallas_call | solution.py:56
Async XLA Ops:
  1.8 10.6 %collective-permute-start.1 = (bf16[2,3,48,384]{3,2,1,0:T(8,128)(2,1)S(1)}, bf16[2,3,48,384]{3,2,1,0:T(8,128)(2,1)S(1)}, u32[]{:S(2)}, u32[]{:S(2)}) collective-permute-start(bf16[2,3,48,384]{3,2,1,0:T(8,128)(2,1)S(1)} %get-tuple-element.48), channel_id=1, source_target_pairs={{1,2},{3,4},{5,6},{7,8},{9,10},{11,12},{13,14},{15,16},{17,18},{19... | collective-permute-start | bytes 663560 | tf_op jit(solution)/shard_map/ppermute | solution.py:459
  5.4 6.9 %collective-permute-start = (bf16[2,3,48,384]{3,2,1,0:T(8,128)(2,1)S(1)}, bf16[2,3,48,384]{3,2,1,0:T(8,128)(2,1)S(1)}, u32[]{:S(2)}, u32[]{:S(2)}) collective-permute-start(bf16[2,3,48,384]{3,2,1,0:T(8,128)(2,1)S(1)} %get-tuple-element.49), channel_id=1, source_target_pairs={{0,1},{2,3},{4,5},{6,7},{8,9},{10,11},{12,13},{14,15},{16,17},{18,... | collective-permute-start | bytes 663560 | tf_op jit(solution)/shard_map/ppermute | solution.py:459
  13.5 10.6 %collective-permute-start.3 = (bf16[18,48,128]{2,1,0:T(8,128)(2,1)S(1)}, bf16[18,48,128]{2,1,0:T(8,128)(2,1)S(1)}, u32[]{:S(2)}, u32[]{:S(2)}) collective-permute-start(bf16[18,48,128]{2,1,0:T(8,128)(2,1)S(1)} %get-tuple-element.33), channel_id=1, source_target_pairs={{0,64},{64,128},{128,192},{192,0},{1,65},{65,129},{129,193},{193,1... | collective-permute-start | bytes 663560 | tf_op jit(solution)/shard_map/ppermute | solution.py:452
  15.1 4.3 %copy-start.4 = (bf16[3,3,3,192,192]{4,3,2,1,0:T(8,128)(2,1)S(1)}, bf16[3,3,3,192,192]{4,3,2,1,0:T(8,128)(2,1)}, u32[]{:S(2)}) copy-start(bf16[3,3,3,192,192]{4,3,2,1,0:T(8,128)(2,1)} %refs_2_.6) | copy-start | bytes 5971972
  17.7 9.2 %collective-permute-start.2 = (bf16[18,48,128]{2,1,0:T(8,128)(2,1)S(1)}, bf16[18,48,128]{2,1,0:T(8,128)(2,1)S(1)}, u32[]{:S(2)}, u32[]{:S(2)}) collective-permute-start(bf16[18,48,128]{2,1,0:T(8,128)(2,1)S(1)} %get-tuple-element.32), channel_id=1, source_target_pairs={{0,64},{64,128},{128,192},{192,0},{1,65},{65,129},{129,193},{193,1... | collective-permute-start | bytes 663560 | tf_op jit(solution)/shard_map/ppermute | solution.py:452
  19.4 4.7 %copy-start = (bf16[3,3,3,192,192]{4,3,2,1,0:T(8,128)(2,1)S(1)}, bf16[3,3,3,192,192]{4,3,2,1,0:T(8,128)(2,1)}, u32[]{:S(2)}) copy-start(bf16[3,3,3,192,192]{4,3,2,1,0:T(8,128)(2,1)} %refs_2_.9) | copy-start | bytes 5971972
  19.4 4.8 %copy-start.3 = (f32[192]{0:T(256)S(1)}, f32[192]{0:T(256)}, u32[]{:S(2)}) copy-start(f32[192]{0:T(256)} %refs_2_.8) | copy-start | bytes 2308
  25.4 3.6 %copy-start.1 = (bf16[384,192]{0,1:T(8,128)(2,1)S(1)}, bf16[384,192]{0,1:T(8,128)(2,1)}, u32[]{:S(2)}) copy-start(bf16[384,192]{0,1:T(8,128)(2,1)} %param.13) | copy-start | bytes 442372
  25.4 7.9 %collective-permute-start.5 = (bf16[15,48,128]{2,1,0:T(8,128)(2,1)S(1)}, bf16[15,48,128]{2,1,0:T(8,128)(2,1)S(1)}, u32[]{:S(2)}, u32[]{:S(2)}) collective-permute-start(bf16[15,48,128]{2,1,0:T(8,128)(2,1)S(1)} %get-tuple-element.39), channel_id=1, source_target_pairs={{0,64},{64,128},{128,192},{192,0},{1,65},{65,129},{129,193},{193,1... | collective-permute-start | bytes 552968 | tf_op jit(solution)/shard_map/ppermute | solution.py:452
  28.7 8.8 %collective-permute-start.4 = (bf16[15,48,128]{2,1,0:T(8,128)(2,1)S(1)}, bf16[15,48,128]{2,1,0:T(8,128)(2,1)S(1)}, u32[]{:S(2)}, u32[]{:S(2)}) collective-permute-start(bf16[15,48,128]{2,1,0:T(8,128)(2,1)S(1)} %get-tuple-element.37), channel_id=1, source_target_pairs={{0,64},{64,128},{128,192},{192,0},{1,65},{65,129},{129,193},{193,1... | collective-permute-start | bytes 552968 | tf_op jit(solution)/shard_map/ppermute | solution.py:452
  29.0 4.3 %copy-start.2 = (f32[192]{0:T(256)S(1)}, f32[192]{0:T(256)}, u32[]{:S(2)}) copy-start(f32[192]{0:T(256)} %refs_2_.11) | copy-start | bytes 2308
  33.7 7.0 %collective-permute-start.7 = (bf16[15,48,128]{2,1,0:T(8,128)(2,1)S(1)}, bf16[15,48,128]{2,1,0:T(8,128)(2,1)S(1)}, u32[]{:S(2)}, u32[]{:S(2)}) collective-permute-start(bf16[15,48,128]{2,1,0:T(8,128)(2,1)S(1)} %get-tuple-element.40.refs_1_), channel_id=1, source_target_pairs={{0,64},{64,128},{128,192},{192,0},{1,65},{65,129},{129,193},{193,1... | collective-permute-start | bytes 552968 | tf_op jit(solution)/shard_map/ppermute | solution.py:452
  38.0 6.8 %collective-permute-start.6 = (bf16[15,48,128]{2,1,0:T(8,128)(2,1)S(1)}, bf16[15,48,128]{2,1,0:T(8,128)(2,1)S(1)}, u32[]{:S(2)}, u32[]{:S(2)}) collective-permute-start(bf16[15,48,128]{2,1,0:T(8,128)(2,1)S(1)} %get-tuple-element.38.refs_0_), channel_id=1, source_target_pairs={{0,64},{64,128},{128,192},{192,0},{1,65},{65,129},{129,193},{193,1... | collective-permute-start | bytes 552968 | tf_op jit(solution)/shard_map/ppermute | solution.py:452

commit v4 on v3

--- a/solution.py
+++ b/solution.py
@@ -45,24 +45,27 @@
     return left, right
 
 
-def call(kernel, out_shape, scratch, flops, args, hbm=(), out_hbm=(), aliases=None):
+def call(kernel, out_shape, scratch, flops, args, hbm=(), out_hbm=(), aliases=None, after=()):
     vmem = pl.BlockSpec(memory_space=pltpu.VMEM)
     far = pl.BlockSpec(memory_space=pltpu.HBM)
     args = [pltpu.with_memory_space_constraint(x, pltpu.HBM) if i in hbm else x for i, x in enumerate(args)]
 
+    count = len(args)
+
     def placed(*refs):
-        kernel([f(axis) for f in (lax.axis_index, lax.axis_size) for axis in ("tm", "rows")], *refs)
+        place = [f(axis) for f in (lax.axis_index, lax.axis_size) for axis in ("tm", "rows")]
+        kernel(place, *refs[:count], *refs[count + len(after) :])
 
     return pl.pallas_call(
         placed,
         out_shape=out_shape,
-        in_specs=[far if i in hbm else vmem for i in range(len(args))],
+        in_specs=[far if i in hbm else vmem for i in range(count)] + [pl.BlockSpec(memory_space=pl.ANY)] * len(after),
         out_specs=tuple(far if i in out_hbm else vmem for i in range(len(out_shape))),
         scratch_shapes=scratch,
         input_output_aliases=aliases or {},
         compiler_params=pltpu.CompilerParams(vmem_limit_bytes=LIMIT << 20),
         cost_estimate=pl.CostEstimate(flops=flops, bytes_accessed=4 << 20, transcendentals=0),
-    )(*args)
+    )(*args, *after)
 
 
 def pack_rows(ref, rows, get):
@@ -195,23 +198,35 @@
             ).astype(BF16)
 
 
-def inner_kernel(place, latents, gain, kernel, held, weights, active, sums, held_gain, squares, scale, sems):
+def rim_kernel(place, latents, gain, held, held_gain, near, far, sems):
+    rows = held.shape[1]
+    copies = [pltpu.make_async_copy(latents.at[frame], held.at[frame], sems.at[frame]) for frame in range(2)]
+    copies.append(pltpu.make_async_copy(gain, held_gain, sems.at[2]))
+    for copy in copies:
+        copy.start()
+    odd = place[1] % 2
+    for frame in range(2):
+        copies[frame].wait()
+        far[frame] = held[frame, pl.ds((rows - HALO) * odd, HALO)]
+        near[frame] = held[frame, pl.ds((rows - HALO) * (1 - odd), HALO)]
+    copies[2].wait()
+
+
+def inner_kernel(place, held, gain, weights, active, packed, squares, scale, sums):
     frames, rows, width, channels = held.shape
-    copies = [
-        pltpu.make_async_copy(latents.at[1], held.at[1], sems.at[0]),
-        pltpu.make_async_copy(latents.at[0], held.at[0], sems.at[1]),
-        pltpu.make_async_copy(kernel, weights, sems.at[2]),
-        pltpu.make_async_copy(gain, held_gain, sems.at[3]),
-    ]
-    for copy in (copies[0], copies[3], copies[1], copies[2]):
-        copy.start()
-    copies[3].wait()
-    for frame, copy in ((1, copies[0]), (0, copies[1])):
-        copy.wait()
-        activate_rows(held.at[frame], held_gain, squares, scale, active.at[frame])
-    copies[2].wait()
+    for frame in range(frames):
+        activate_rows(held.at[frame], gain, squares, scale, active.at[frame])
     count = rows - 2
-    convolve(sums, dot_t, weights, [(windows(active.at[1], count), 0)], count, width)
+    for out, taps in ((1, ((1, 0),)), (0, ((0, 0), (1, 1)))):
+        terms = [(windows(active.at[frame], count), a) for frame, a in taps]
+        convolve(sums.at[out], dot_t, weights, terms, count, width)
+        pack_rows(packed.at[out], count, lambda row: sums[out, row * width : (row + 1) * width])
+
+
+def late_inner_own_kernel(place, active, weights, own):
+    count, width = active.shape[1] - 2, active.shape[2]
+    terms = [(windows(active.at[frame], count), a) for frame, a in OWN[1]]
+    convolve(own, dot_t, weights, terms, count, width)
 
 
 def fill_edges(place, near, far, frame, gain, active, edges, raw, squares, scale):
@@ -234,57 +249,46 @@
     return lambda b: edges[:, b : b + HALO].reshape(2 * HALO * width, channels)
 
 
-def pack_joined(partial, sums, acc, wide, width):
-    def get(row):
-        if HALO <= row < wide - HALO:
-            return sums[(row - HALO) * width : (row - HALO + 1) * width]
-        at = row if row < HALO else row - (wide - 2 * HALO)
-        return acc[at * width : (at + 1) * width]
-
-    pack_rows(partial, wide, get)
-
-
-def late_edge_kernel(
-    place, near, far, gain, active, weights, sums, partial, edges, acc, raw, squares, scale
-):
+def pack_edges(partial, acc, width):
+    pack_rows(partial, 2 * HALO, lambda row: acc[row * width : (row + 1) * width])
+
+
+def late_edge_kernel(place, near, far, gain, active, weights, partial, edges, acc, raw, squares, scale):
     fill_edges(place, near, far, 1, gain, active, edges, raw, squares, scale)
     width = active.shape[2]
     convolve(acc, dot_t, weights, [(edge_windows(edges), 0)], 2 * HALO, width)
-    pack_joined(partial, sums, acc, active.shape[1] + 4, width)
+    pack_edges(partial, acc, width)
 
 
 def early_edge_kernel(
-    place, near, far, gain, active, weights, late, partial, tall, edges, acc, raw, squares, scale
+    place, near, far, gain, active, weights, late, partial, edges, acc, raw, squares, scale
 ):
     fill_edges(place, near, far, 0, gain, active, edges, raw, squares, scale)
-    rows, width = active.shape[1], active.shape[2]
-    for frame, ends in ((0, edges), (1, late)):
-        tall[frame, 0:HALO] = ends[0, 0:HALO]
-        tall[frame, HALO : HALO + rows] = active[frame]
-        tall[frame, HALO + rows :] = ends[1, 2:]
-    wide = rows + 4
-    convolve(
-        acc, dot_t, weights, [(windows(tall.at[0], wide), 0), (windows(tall.at[1], wide), 1)], wide, width
-    )
-    pack_rows(partial, wide, lambda row: acc[row * width : (row + 1) * width])
-
-
-def first_own_kernel(place, active, kernel, third, own, mixed):
-    wide, width = active.shape[1] - 2, active.shape[2]
-    for out in (1, 0):
-        terms = [(windows(active.at[frame], wide), a) for frame, a in OWN[out]]
-        convolve(own.at[out], dot_t, kernel, terms, wide, width)
-    mix_weights(third, mixed)
+    width = active.shape[2]
+    convolve(acc, dot_t, weights, [(edge_windows(edges), 0), (edge_windows(late), 1)], 2 * HALO, width)
+    pack_edges(partial, acc, width)
+
+
+def late_edge_own_kernel(place, early, late, weights, own):
+    terms = [(edge_windows((early, late)[frame]), a) for frame, a in OWN[1]]
+    convolve(own, dot_t, weights, terms, 2 * HALO, early.shape[2])
+
+
+def early_own_kernel(place, active, early, weights, inner, edges):
+    count, width = active.shape[1] - 2, active.shape[2]
+    (frame, a), = OWN[0]
+    convolve(inner, dot_t, weights, [(windows(active.at[frame], count), a)], count, width)
+    convolve(edges, dot_t, weights, [(edge_windows(early), a)], 2 * HALO, width)
 
 
 def finish(place, own, before, gain, raw, squares, scale, keep):
-    tall, width = before.shape[0] * 2 // 3, before.shape[1]
+    before, tall, width = before
     start = place[1] * 8 - (tall - 8) // 2
     follows = place[0] > 0
     for row in range(tall):
         part = slice(row * width, (row + 1) * width)
-        earlier = jnp.where(follows, unpack_row(before, row), 0.0)
-        total = (own[part] + earlier).astype(BF16)
+        earlier = jnp.where(follows, before(row), 0.0)
+        total = (own(row) + earlier).astype(BF16)
         raw[part] = total
         keep(row, total)
         total = total.astype(F32)
@@ -316,14 +320,49 @@
     pack_rows(partial, wide, lambda row: total[row * width : (row + 1) * width])
 
 
-def late_second_kernel(place, own, before, gain, kernel, partial, field, raw, squares, scale):
-    terms = [(field, 0)]
-    second(place, own.at[1], before, gain, kernel, terms, partial, field, raw, squares, scale)
-
-
-def early_second_kernel(place, own, before, gain, kernel, late, partial, field, raw, squares, scale):
-    terms = [(field, 0), (late, 1)]
-    second(place, own.at[0], before, gain, kernel, terms, partial, field, raw, squares, scale)
+def joined(inner, edges):
+    count = inner.shape[0] * 2 // 3
+
+    def get(row):
+        if HALO <= row < HALO + count:
+            return unpack_row(inner, row - HALO)
+        return unpack_row(edges, row if row < HALO else row - count)
+
+    return get, count + 2 * HALO, inner.shape[1]
+
+
+def whole(packed):
+    return lambda row: unpack_row(packed, row), packed.shape[0] * 2 // 3, packed.shape[1]
+
+
+def joined_own(inner, edges, width):
+    count = inner.shape[0] // width
+
+    def get(row):
+        ref, at = (inner, row - HALO) if HALO <= row < HALO + count else (edges, row if row < HALO else row - count)
+        return ref[at * width : (at + 1) * width]
+
+    return get
+
+
+def rows_of(own, width):
+    return lambda row: own[row * width : (row + 1) * width]
+
+
+def late_second_kernel(
+    place, own_inner, own_edges, inner, edges, gain, kernel, partial, field, raw, squares, scale
+):
+    before = joined(inner.at[1], edges)
+    own = joined_own(own_inner, own_edges, field.shape[2])
+    second(place, own, before, gain, kernel, [(field, 0)], partial, field, raw, squares, scale)
+
+
+def early_second_kernel(
+    place, own_inner, own_edges, inner, edges, gain, kernel, late, partial, field, raw, squares, scale
+):
+    before = joined(inner.at[0], edges)
+    own = joined_own(own_inner, own_edges, field.shape[2])
+    second(place, own, before, gain, kernel, [(field, 0), (late, 1)], partial, field, raw, squares, scale)
 
 
 def second_own_kernel(place, early, late, kernel, latents, near, far, shortcut, own):
@@ -350,7 +389,8 @@
         if 0 < row < tall - 1:
             block[row - 1] = total
 
-    pack_rows(packed, tall, finish(place, own, before, gain, raw, squares, scale, keep))
+    own = rows_of(own, packed.shape[1])
+    pack_rows(packed, tall, finish(place, own, whole(before), gain, raw, squares, scale, keep))
 
 
 def late_third_kernel(place, own, before, gain, block, packed, raw, squares, scale):
@@ -361,7 +401,7 @@
     third(place, own.at[0], before, gain, block, packed, raw, squares, scale)
 
 
-def mix_weights(kernel, out):
+def weights_kernel(place, kernel, out):
     def halves(taps, parity):
         if parity == 0:
             return taps[0], taps[1] + taps[2]
@@ -473,6 +513,7 @@
 ):
     frames, rows, width, channels = latents.shape
     shape = jax.ShapeDtypeStruct
+    shape = jax.ShapeDtypeStruct
     odd = lax.axis_index("rows") % 2
     near = lax.dynamic_slice_in_dim(latents, (rows - HALO) * (1 - odd), HALO, 1)
     far = lax.dynamic_slice_in_dim(latents, (rows - HALO) * odd, HALO, 1)
@@ -486,46 +527,57 @@
     def work(tall, channels):
         return [pltpu.VMEM((tall * width, channels), BF16), pltpu.VMEM((tall * width, 128), F32)]
 
-    held, weights, active, sums, gain_first = call(
+    rim = shape((frames, HALO, width, channels), BF16)
+    held, gain_first, near, far = call(
+        rim_kernel,
+        (shape(latents.shape, BF16), shape((channels,), F32), rim, rim),
+        [dma((3,))],
+        1 << 34,
+        (latents, gain_first),
+        hbm=(0, 1),
+    )
+    far, near = swap(far, 1), swap(near, 0)
+    inner_rows = rows - 2
+    inner_pixels = inner_rows * width
+    across = jnp.swapaxes(kernel_first, 3, 4)
+    active, inner = call(
         inner_kernel,
         (
             shape(latents.shape, BF16),
-            shape((3, 3, 3, 192, channels), BF16),
-            shape(latents.shape, BF16),
-            shape(((rows - 2) * width, 192), F32),
-            shape((channels,), F32),
+            shape((2, inner_rows * 3 // 2, width, 128), BF16),
         ),
-        work(rows, channels) + [dma((4,))],
+        work(rows, channels) + [pltpu.VMEM((2, inner_pixels, 192), F32)],
         2 * flops1,
-        (latents, gain_first, jnp.swapaxes(kernel_first, 3, 4)),
-        hbm=(0, 1, 2),
-    )
-    edge_work = [pltpu.VMEM((2 * HALO, width, channels), BF16)] + work(HALO, channels)
+        (held, gain_first, across),
+    )
+    inner = onward(inner)
+    (late_inner,) = call(
+        late_inner_own_kernel, (shape((inner_pixels, 192), F32),), [], flops1, (active, across)
+    )
+    edge_sums = shape((2 * HALO * width, 192), F32)
+    edge_work = [pltpu.VMEM(edge_sums.shape, F32), pltpu.VMEM((2 * HALO, width, channels), BF16)]
+    edge_work += work(HALO, channels)
     ends = shape((2, HALO + 2, width, channels), BF16)
-    packed1 = shape((wide1 * 3 // 2, width, 128), BF16)
+    packed1 = shape((HALO * 3, width, 128), BF16)
     partial, late = call(
         late_edge_kernel,
         (packed1, ends),
-        [pltpu.VMEM((2 * HALO * width, 192), F32)] + edge_work,
+        edge_work,
         flops1 // 2,
-        (near, far, gain_first, active, weights, sums),
-    )
-    before_late = onward(partial)
-    partial, tall = call(
+        (near, far, gain_first, active, across),
+        after=(late_inner,),
+    )
+    late_edges = onward(partial)
+    partial, early = call(
         early_edge_kernel,
-        (packed1, shape((2, wide1 + 2, width, channels), BF16)),
-        [pltpu.VMEM(ends.shape, BF16), pltpu.VMEM((pixels1, 192), F32)] + edge_work,
-        2 * flops1,
-        (near, far, gain_first, active, weights, late),
-    )
-    before_early = onward(partial)
-    own, mixed = call(
-        first_own_kernel,
-        (shape((2, pixels1, 192), F32), shape((3, 4, 768, 192), BF16)),
-        [],
-        3 * flops1,
-        (tall, weights, kernel_third),
-    )
+        (packed1, ends),
+        edge_work,
+        flops1,
+        (near, far, gain_first, active, across, late),
+        after=(partial,),
+    )
+    early_edges = onward(partial)
+    (late_rest,) = call(late_edge_own_kernel, (edge_sums,), [], flops1, (early, late, across))
     second_work = [pltpu.VMEM((pixels1, 192), BF16)] + work(wide1, 192)
     packed2 = shape((wide2 * 3 // 2, width, 128), BF16)
     field = shape((3, wide1, width, 256), BF16)
@@ -534,15 +586,23 @@
         (packed2, field),
         second_work,
         flops2,
-        (own, before_late, gain_second, kernel_second),
+        (late_inner, late_rest, inner, late_edges, gain_second, kernel_second),
     )
     before_late = onward(partial)
+    early_inner, early_rest = call(
+        early_own_kernel,
+        (shape((inner_pixels, 192), F32), edge_sums),
+        [],
+        flops1,
+        (active, early, across),
+        after=(partial,),
+    )
     partial, early = call(
         early_second_kernel,
         (packed2, field),
         second_work,
         2 * flops2,
-        (own, before_early, gain_second, kernel_second, late),
+        (early_inner, early_rest, inner, early_edges, gain_second, kernel_second, late),
     )
     before_early = onward(partial)
     (own,) = call(
@@ -551,6 +611,9 @@
         [],
         3 * flops2,
         (early, late, kernel_second, held, near, far, shortcut.T),
+    )
+    (mixed,) = call(
+        weights_kernel, (shape((3, 4, 768, 192), BF16),), [], 1 << 24, (kernel_third,), after=(own,)
     )
     third_work = [pltpu.VMEM((pixels2, 192), BF16)] + work(wide2, 192)
     block = shape((rows, width, 192), BF16)

time: 47.1 us -> 44 us (0.934)
  waiting for transfers between devices: 11.7 us -> 8.16 us
  starting transfers between devices: 9.06 us -> 11.2 us
  local copies, waits for them, and re-layouts: 1.12 us -> 0.03 us
  Pallas kernels: 23.9 us -> 23.4 us
    ppermute x2, waiting for transfers between devices: 3.56 us -> 0.98 us  [swap(): lax.ppermute(value, 'rows', pairs + [(b, a) for a, b in pairs] + [(i, i)...]
    ppermute x6 -> x7, starting transfers between devices: 5.32 us -> 6.81 us  [onward(): lax.ppermute(value, 'tm', [(i, (i + 1) % count) for i in range(count)])]
    dynamic_slice x1 -> x0, local copies, waits for them, and re-layouts: 1.1 us -> none  [body(): far = lax.dynamic_slice_in_dim(latents, (rows - HALO) * odd, HALO, 1)]
    ppermute x6 -> x7, waiting for transfers between devices: 8.16 us -> 7.18 us  [onward(): lax.ppermute(value, 'tm', [(i, (i + 1) % count) for i in range(count)])]
    ppermute x2, starting transfers between devices: 3.74 us -> 4.39 us  [swap(): lax.ppermute(value, 'rows', pairs + [(b, a) for a, b in pairs] + [(i, i)...]
    pallas_call x12 -> x16, Pallas kernels: 23.9 us -> 23.4 us  [call(): pl.pallas_call(placed, out_shape=out_shape, in_specs=[far if i in hbm els...]
  transfers between devices with their start and end apart: 8 -> 9, of which waited for: 4 -> 5; matrix products, arithmetic and copies ran while one was open for 0% -> 0% of each run, Pallas kernels for 45% -> 47%
where the time goes in v4:
time: 44 us; the launch traced here: 43.7 us
  Pallas kernels  23.4 us (53%)
  starting transfers between devices  11.2 us (25%)
  waiting for transfers between devices  8.16 us (19%)
  between operations  0.95 us (2%)
    pallas_call x16, Pallas kernels, call(): pl.pallas_call(placed, out_shape=out_shape, in_specs=[far if i in hbm els...  23.4 us
    ppermute x7, waiting for transfers between devices, onward(): lax.ppermute(value, 'tm', [(i, (i + 1) % count) for i in range(count)])  7.18 us
    ppermute x7, starting transfers between devices, onward(): lax.ppermute(value, 'tm', [(i, (i + 1) % count) for i in range(count)])  6.81 us
    ppermute x2, starting transfers between devices, swap(): lax.ppermute(value, 'rows', pairs + [(b, a) for a, b in pairs] + [(i, i)...  4.39 us
    ppermute x2, waiting for transfers between devices, swap(): lax.ppermute(value, 'rows', pairs + [(b, a) for a, b in pairs] + [(i, i)...  0.98 us
  transfers between devices with their start and end apart: 9, of which 5 were waited for; matrix products, arithmetic and copies ran while one was open for 0% of the time, Pallas kernels for 47%

profile of v4, /device:TPU:128, one launch (start us, length us, event | category | flops | bytes accessed | tf_op | source)
XLA Modules:
  0.0 43.7 jit_solution(12358125260478667442)
XLA Ops:
  0.6 0.0 copy-start
  0.6 1.2 %shard_map.95 = (bf16[2,8,48,384]{3,2,1,0:T(8,128)(2,1)S(1)}, f32[384]{0:T(512)S(1)}, bf16[2,3,48,384]{3,2,1,0:T(8,128)(2,1)S(1)}, bf16[2,3,48,384]{3,2,1,0:T(8,128)(2,1)S(1)}) custom-call(bf16[2,8,48,384]{3,2,1,0:T(8,128)(2,1)} %refs_0_.2, f32[384]{0:T(512)} %refs_1_.1), custom_call_target="tpu_custom_call" | custom-call | flops 17179869184 | bytes 4194304 | tf_op jit(solution)/shard_map/pallas_call | solution.py:59
  1.9 0.1 collective-permute-start
  2.0 4.3 %collective-permute-start.1 = (bf16[2,3,48,384]{3,2,1,0:T(8,128)(2,1)S(1)}, bf16[2,3,48,384]{3,2,1,0:T(8,128)(2,1)S(1)}, u32[]{:S(2)}, u32[]{:S(2)}) collective-permute-start(bf16[2,3,48,384]{3,2,1,0:T(8,128)(2,1)S(1)} %get-tuple-element.30), channel_id=1, source_target_pairs={{1,2},{3,4},{5,6},{7,8},{9,10},{11,12},{13,14},{15,16},{17,18},{19... | collective-permute-start | bytes 663560 | tf_op jit(solution)/shard_map/ppermute | solution.py:499
  6.3 0.0 copy-done
  6.3 2.5 %shard_map.96 = (bf16[2,8,48,384]{3,2,1,0:T(8,128)(2,1)S(1)}, bf16[2,9,48,128]{3,2,1,0:T(8,128)(2,1)S(1)}) custom-call(bf16[2,8,48,384]{3,2,1,0:T(8,128)(2,1)S(1)} %get-tuple-element.26.refs_0_.refs_3_, f32[384]{0:T(512)S(1)} %get-tuple-element.27.refs_1_.refs_2_, bf16[3,3,3,192,384]{4,3,2,1,0:T(8,128)(2,1)S(1)} %bitcast.3), custom_call_target="tpu_custom_call" | custom-call | flops 1528823808 | bytes 4194304 | tf_op jit(solution)/shard_map/pallas_call | solution.py:59
  8.8 1.6 %collective-permute-start.2 = (bf16[2,9,48,128]{3,2,1,0:T(8,128)(2,1)S(1)}, bf16[2,9,48,128]{3,2,1,0:T(8,128)(2,1)S(1)}, u32[]{:S(2)}, u32[]{:S(2)}) collective-permute-start(bf16[2,9,48,128]{3,2,1,0:T(8,128)(2,1)S(1)} %get-tuple-element.34), channel_id=1, source_target_pairs={{0,64},{64,128},{128,192},{192,0},{1,65},{65,129},{129,193},{193,1... | collective-permute-start | bytes 663560 | tf_op jit(solution)/shard_map/ppermute | solution.py:492
  10.5 1.2 %shard_map.97.refs_5_.refs_0_ = f32[288,192]{1,0:T(8,128)S(1)} custom-call(bf16[2,8,48,384]{3,2,1,0:T(8,128)(2,1)S(1)} %get-tuple-element.28.refs_0_.refs_3_, bf16[3,3,3,192,384]{4,3,2,1,0:T(8,128)(2,1)S(1)} %bitcast.4), custom_call_target="tpu_custom_call" | custom-call | flops 764411904 | bytes 4194304 | tf_op jit(solution)/shard_map/pallas_call | solution.py:59
  11.7 0.0 collective-permute-done.refs_0_.refs_4_
  11.7 1.0 %collective-permute-done.1.refs_1_.refs_5_ = bf16[2,3,48,384]{3,2,1,0:T(8,128)(2,1)S(1)} collective-permute-done((bf16[2,3,48,384]{3,2,1,0:T(8,128)(2,1)S(1)}, bf16[2,3,48,384]{3,2,1,0:T(8,128)(2,1)S(1)}, u32[]{:S(2)}, u32[]{:S(2)}) %collective-permute-start.1) | collective-permute-done | bytes 221216 | tf_op jit(solution)/shard_map/ppermute | solution.py:499
  12.7 1.1 %shard_map.98 = (bf16[9,48,128]{2,1,0:T(8,128)(2,1)S(1)}, bf16[2,5,48,384]{3,2,1,0:T(8,128)(2,1)S(1)}) custom-call(bf16[2,3,48,384]{3,2,1,0:T(8,128)(2,1)S(1)} %collective-permute-done.refs_0_.refs_4_, bf16[2,3,48,384]{3,2,1,0:T(8,128)(2,1)S(1)} %collective-permute-done.1.refs_1_.refs_5_, f32[384]{0:T(512)S(1)} %get-tuple-element.27.refs_1_.refs_2_, ...), custom_call_target="tpu_custom_call" | custom-call | flops 382205952 | bytes 4194304 | tf_op jit(solution)/shard_map/pallas_call | solution.py:59
  13.8 1.6 %collective-permute-start.3 = (bf16[9,48,128]{2,1,0:T(8,128)(2,1)S(1)}, bf16[9,48,128]{2,1,0:T(8,128)(2,1)S(1)}, u32[]{:S(2)}, u32[]{:S(2)}) collective-permute-start(bf16[9,48,128]{2,1,0:T(8,128)(2,1)S(1)} %get-tuple-element.32.refs_6_), channel_id=1, source_target_pairs={{0,64},{64,128},{128,192},{192,0},{1,65},{65,129},{129,193},{193,1... | collective-permute-start | bytes 331784 | tf_op jit(solution)/shard_map/ppermute | solution.py:492
  15.5 1.6 %shard_map.99 = (bf16[9,48,128]{2,1,0:T(8,128)(2,1)S(1)}, bf16[2,5,48,384]{3,2,1,0:T(8,128)(2,1)S(1)}) custom-call(bf16[2,3,48,384]{3,2,1,0:T(8,128)(2,1)S(1)} %collective-permute-done.refs_0_.refs_4_, bf16[2,3,48,384]{3,2,1,0:T(8,128)(2,1)S(1)} %collective-permute-done.1.refs_1_.refs_5_, f32[384]{0:T(512)S(1)} %get-tuple-element.27.refs_1_.refs_2_, ...), custom_call_target="tpu_custom_call" | custom-call | flops 764411904 | bytes 4194304 | tf_op jit(solution)/shard_map/pallas_call | solution.py:59
  17.1 0.0 copy-start.1
  17.1 0.0 copy-start.5
  17.1 1.7 %collective-permute-start.4 = (bf16[9,48,128]{2,1,0:T(8,128)(2,1)S(1)}, bf16[9,48,128]{2,1,0:T(8,128)(2,1)S(1)}, u32[]{:S(2)}, u32[]{:S(2)}) collective-permute-start(bf16[9,48,128]{2,1,0:T(8,128)(2,1)S(1)} %get-tuple-element.38), channel_id=1, source_target_pairs={{0,64},{64,128},{128,192},{192,0},{1,65},{65,129},{129,193},{193,1... | collective-permute-start | bytes 331784 | tf_op jit(solution)/shard_map/ppermute | solution.py:492
  18.8 1.2 %shard_map.100.refs_1_ = f32[288,192]{1,0:T(8,128)S(1)} custom-call(bf16[2,5,48,384]{3,2,1,0:T(8,128)(2,1)S(1)} %get-tuple-element.33.refs_0_.refs_1_, bf16[2,5,48,384]{3,2,1,0:T(8,128)(2,1)S(1)} %get-tuple-element.31.refs_5_.refs_1_, bf16[3,3,3,192,384]{4,3,2,1,0:T(8,128)(2,1)S(1)} %bitcast.7), custom_call_target="tpu_custom_call" | custom-call | flops 764411904 | bytes 4194304 | tf_op jit(solution)/shard_map/pallas_call | solution.py:59
  20.0 0.0 collective-permute-done.2.refs_2_
  20.0 0.9 %collective-permute-done.3.refs_3_ = bf16[9,48,128]{2,1,0:T(8,128)(2,1)S(1)} collective-permute-done((bf16[9,48,128]{2,1,0:T(8,128)(2,1)S(1)}, bf16[9,48,128]{2,1,0:T(8,128)(2,1)S(1)}, u32[]{:S(2)}, u32[]{:S(2)}) %collective-permute-start.3) | collective-permute-done | bytes 110624 | tf_op jit(solution)/shard_map/ppermute | solution.py:492
  20.9 0.0 copy-done.1
  20.9 0.0 copy-done.5
  20.9 1.2 %shard_map.101 = (bf16[15,48,128]{2,1,0:T(8,128)(2,1)S(1)}, bf16[3,12,48,256]{3,2,1,0:T(8,128)(2,1)S(1)}) custom-call(f32[288,192]{1,0:T(8,128)S(1)} %shard_map.97.refs_5_.refs_0_, f32[288,192]{1,0:T(8,128)S(1)} %shard_map.100.refs_1_, bf16[2,9,48,128]{3,2,1,0:T(8,128)(2,1)S(1)} %collective-permute-done.2.refs_2_, ...), custom_call_target="tpu_custom_call" | custom-call | flops 318504960 | bytes 4194304 | tf_op jit(solution)/shard_map/pallas_call | solution.py:59
  22.2 0.6 %collective-permute-start.6 = (bf16[15,48,128]{2,1,0:T(8,128)(2,1)S(1)}, bf16[15,48,128]{2,1,0:T(8,128)(2,1)S(1)}, u32[]{:S(2)}, u32[]{:S(2)}) collective-permute-start(bf16[15,48,128]{2,1,0:T(8,128)(2,1)S(1)} %get-tuple-element.35.refs_3_), channel_id=1, source_target_pairs={{0,64},{64,128},{128,192},{192,0},{1,65},{65,129},{129,193},{193,1... | collective-permute-start | bytes 552968 | tf_op jit(solution)/shard_map/ppermute | solution.py:492
  22.8 1.4 %shard_map.102 = (f32[288,192]{1,0:T(8,128)S(1)}, f32[288,192]{1,0:T(8,128)S(1)}) custom-call(bf16[2,8,48,384]{3,2,1,0:T(8,128)(2,1)S(1)} %get-tuple-element.28.refs_0_.refs_3_, bf16[2,5,48,384]{3,2,1,0:T(8,128)(2,1)S(1)} %get-tuple-element.33.refs_0_.refs_1_, bf16[3,3,3,192,384]{4,3,2,1,0:T(8,128)(2,1)S(1)} %bitcast.8, ...), custom_call_target="tpu_custom_call" | custom-call | flops 764411904 | bytes 4194304 | tf_op jit(solution)/shard_map/pallas_call | solution.py:59
  24.2 0.0 copy-start.3
  24.2 0.0 collective-permute-done.4.refs_3_
  24.2 1.8 %shard_map.103 = (bf16[15,48,128]{2,1,0:T(8,128)(2,1)S(1)}, bf16[3,12,48,256]{3,2,1,0:T(8,128)(2,1)S(1)}) custom-call(f32[288,192]{1,0:T(8,128)S(1)} %get-tuple-element.36.refs_0_, f32[288,192]{1,0:T(8,128)S(1)} %get-tuple-element.37.refs_1_, bf16[2,9,48,128]{3,2,1,0:T(8,128)(2,1)S(1)} %collective-permute-done.2.refs_2_, ...), custom_call_target="tpu_custom_call" | custom-call | flops 637009920 | bytes 4194304 | tf_op jit(solution)/shard_map/pallas_call | solution.py:59
  26.0 1.0 %collective-permute-start.5 = (bf16[15,48,128]{2,1,0:T(8,128)(2,1)S(1)}, bf16[15,48,128]{2,1,0:T(8,128)(2,1)S(1)}, u32[]{:S(2)}, u32[]{:S(2)}) collective-permute-start(bf16[15,48,128]{2,1,0:T(8,128)(2,1)S(1)} %get-tuple-element.41), channel_id=1, source_target_pairs={{0,64},{64,128},{128,192},{192,0},{1,65},{65,129},{129,193},{193,1... | collective-permute-start | bytes 552968 | tf_op jit(solution)/shard_map/ppermute | solution.py:492
  27.0 0.0 copy-done.3
  27.0 0.0 copy-start.4
  27.0 0.0 copy-start.2
  27.0 2.1 %shard_map.104.refs_0_.refs_1_ = f32[2,480,192]{2,1,0:T(8,128)S(1)} custom-call(bf16[3,12,48,256]{3,2,1,0:T(8,128)(2,1)S(1)} %get-tuple-element.40.refs_0_, bf16[3,12,48,256]{3,2,1,0:T(8,128)(2,1)S(1)} %get-tuple-element.39.refs_6_.refs_1_, bf16[3,3,3,192,192]{4,3,2,1,0:T(8,128)(2,1)S(1)} %copy-done.1, ...), custom_call_target="tpu_custom_call" | custom-call | flops 955514880 | bytes 4194304 | tf_op jit(solution)/shard_map/pallas_call | solution.py:59
  29.2 1.5 %collective-permute-done.6.refs_1_ = bf16[15,48,128]{2,1,0:T(8,128)(2,1)S(1)} collective-permute-done((bf16[15,48,128]{2,1,0:T(8,128)(2,1)S(1)}, bf16[15,48,128]{2,1,0:T(8,128)(2,1)S(1)}, u32[]{:S(2)}, u32[]{:S(2)}) %collective-permute-start.6) | collective-permute-done | bytes 184352 | tf_op jit(solution)/shard_map/ppermute | solution.py:492
  30.6 0.0 copy-done.4
  30.6 0.4 shard_map.106
  31.0 0.1 collective-permute-start.8
  31.1 3.5 %collective-permute-done.5.refs_1_ = bf16[15,48,128]{2,1,0:T(8,128)(2,1)S(1)} collective-permute-done((bf16[15,48,128]{2,1,0:T(8,128)(2,1)S(1)}, bf16[15,48,128]{2,1,0:T(8,128)(2,1)S(1)}, u32[]{:S(2)}, u32[]{:S(2)}) %collective-permute-start.5) | collective-permute-done | bytes 184352 | tf_op jit(solution)/shard_map/ppermute | solution.py:492
  34.6 0.4 shard_map.105
  35.0 0.1 collective-permute-start.7
  35.1 0.0 copy-done.2
  35.1 0.9 %shard_map.107.refs_2_.refs_1_ = bf16[3,4,768,192]{3,2,1,0:T(8,128)(2,1)S(1)} custom-call(bf16[3,3,3,192,192]{4,3,2,1,0:T(8,128)(2,1)S(1)} %copy-done.2, f32[2,480,192]{2,1,0:T(8,128)S(1)} %shard_map.104.refs_0_.refs_1_), custom_call_target="tpu_custom_call" | custom-call | flops 16777216 | bytes 4194304 | tf_op jit(solution)/shard_map/pallas_call | solution.py:59
  36.0 2.7 %shard_map.108 = (f32[2,4,384,192]{3,2,1,0:T(8,128)S(1)}, bf16[2,8,48,192]{3,2,1,0:T(8,128)(2,1)}) custom-call(bf16[15,48,128]{2,1,0:T(8,128)(2,1)S(1)} %get-tuple-element.42.refs_0_, bf16[15,48,128]{2,1,0:T(8,128)(2,1)S(1)} %get-tuple-element.43.refs_1_, bf16[3,4,768,192]{3,2,1,0:T(8,128)(2,1)S(1)} %shard_map.107.refs_2_.refs_1_, ...), custom_call_target="tpu_custom_call" | custom-call | flops 764411904 | bytes 4194304 | tf_op jit(solution)/shard_map/pallas_call | solution.py:59
  38.7 0.0 collective-permute-done.8.refs_0_
  38.7 1.8 %shard_map.109 = (bf16[2,8,2,96,192]{4,3,2,1,0:T(8,128)(2,1)}, f32[4,384,192]{2,1,0:T(8,128)S(1)}) custom-call(bf16[15,48,128]{2,1,0:T(8,128)(2,1)S(1)} %collective-permute-done.8.refs_0_, bf16[3,4,768,192]{3,2,1,0:T(8,128)(2,1)S(1)} %shard_map.107.refs_2_.refs_1_, f32[2,4,384,192]{3,2,1,0:T(8,128)S(1)} %get-tuple-element.47.refs_2_), custom_call_target="tpu_custom_call" | custom-call | flops 509607936 | bytes 4194304 | tf_op jit(solution)/shard_map/pallas_call | solution.py:59
  40.5 1.3 %collective-permute-done.7.refs_0_ = bf16[15,48,128]{2,1,0:T(8,128)(2,1)S(1)} collective-permute-done((bf16[15,48,128]{2,1,0:T(8,128)(2,1)S(1)}, bf16[15,48,128]{2,1,0:T(8,128)(2,1)S(1)}, u32[]{:S(2)}, u32[]{:S(2)}) %collective-permute-start.7) | collective-permute-done | bytes 184352 | tf_op jit(solution)/shard_map/ppermute | solution.py:492
  41.8 1.7 %shard_map.110 = bf16[2,8,2,96,192]{4,3,2,1,0:T(8,128)(2,1)} custom-call(bf16[15,48,128]{2,1,0:T(8,128)(2,1)S(1)} %collective-permute-done.7.refs_0_, bf16[3,4,768,192]{3,2,1,0:T(8,128)(2,1)S(1)} %shard_map.107.refs_2_.refs_1_, f32[4,384,192]{2,1,0:T(8,128)S(1)} %get-tuple-element.48.refs_2_, ...), custom_call_target="tpu_custom_call", output_to_operand_aliasing={{}: (3, {})} | custom-call | flops 254803968 | bytes 4194304 | tf_op jit(solution)/shard_map/pallas_call | solution.py:59
Async XLA Ops:
  0.6 5.7 %copy-start = (bf16[3,3,3,384,192]{3,4,2,1,0:T(8,128)(2,1)S(1)}, bf16[3,3,3,384,192]{3,4,2,1,0:T(8,128)(2,1)}, u32[]{:S(2)}) copy-start(bf16[3,3,3,384,192]{3,4,2,1,0:T(8,128)(2,1)} %param.10) | copy-start | bytes 11943940
  1.9 9.8 %collective-permute-start = (bf16[2,3,48,384]{3,2,1,0:T(8,128)(2,1)S(1)}, bf16[2,3,48,384]{3,2,1,0:T(8,128)(2,1)S(1)}, u32[]{:S(2)}, u32[]{:S(2)}) collective-permute-start(bf16[2,3,48,384]{3,2,1,0:T(8,128)(2,1)S(1)} %get-tuple-element.29), channel_id=1, source_target_pairs={{0,1},{2,3},{4,5},{6,7},{8,9},{10,11},{12,13},{14,15},{16,17},{18,... | collective-permute-start | bytes 663560 | tf_op jit(solution)/shard_map/ppermute | solution.py:499
  2.0 10.7 %collective-permute-start.1 = (bf16[2,3,48,384]{3,2,1,0:T(8,128)(2,1)S(1)}, bf16[2,3,48,384]{3,2,1,0:T(8,128)(2,1)S(1)}, u32[]{:S(2)}, u32[]{:S(2)}) collective-permute-start(bf16[2,3,48,384]{3,2,1,0:T(8,128)(2,1)S(1)} %get-tuple-element.30), channel_id=1, source_target_pairs={{1,2},{3,4},{5,6},{7,8},{9,10},{11,12},{13,14},{15,16},{17,18},{19... | collective-permute-start | bytes 663560 | tf_op jit(solution)/shard_map/ppermute | solution.py:499
  8.8 11.2 %collective-permute-start.2 = (bf16[2,9,48,128]{3,2,1,0:T(8,128)(2,1)S(1)}, bf16[2,9,48,128]{3,2,1,0:T(8,128)(2,1)S(1)}, u32[]{:S(2)}, u32[]{:S(2)}) collective-permute-start(bf16[2,9,48,128]{3,2,1,0:T(8,128)(2,1)S(1)} %get-tuple-element.34), channel_id=1, source_target_pairs={{0,64},{64,128},{128,192},{192,0},{1,65},{65,129},{129,193},{193,1... | collective-permute-start | bytes 663560 | tf_op jit(solution)/shard_map/ppermute | solution.py:492
  13.8 7.1 %collective-permute-start.3 = (bf16[9,48,128]{2,1,0:T(8,128)(2,1)S(1)}, bf16[9,48,128]{2,1,0:T(8,128)(2,1)S(1)}, u32[]{:S(2)}, u32[]{:S(2)}) collective-permute-start(bf16[9,48,128]{2,1,0:T(8,128)(2,1)S(1)} %get-tuple-element.32.refs_6_), channel_id=1, source_target_pairs={{0,64},{64,128},{128,192},{192,0},{1,65},{65,129},{129,193},{193,1... | collective-permute-start | bytes 331784 | tf_op jit(solution)/shard_map/ppermute | solution.py:492
  17.1 3.8 %copy-start.1 = (bf16[3,3,3,192,192]{4,3,2,1,0:T(8,128)(2,1)S(1)}, bf16[3,3,3,192,192]{4,3,2,1,0:T(8,128)(2,1)}, u32[]{:S(2)}) copy-start(bf16[3,3,3,192,192]{4,3,2,1,0:T(8,128)(2,1)} %refs_2_.3) | copy-start | bytes 5971972
  17.1 3.8 %copy-start.5 = (f32[192]{0:T(256)S(1)}, f32[192]{0:T(256)}, u32[]{:S(2)}) copy-start(f32[192]{0:T(256)} %refs_4_.3) | copy-start | bytes 2308
  17.1 7.1 %collective-permute-start.4 = (bf16[9,48,128]{2,1,0:T(8,128)(2,1)S(1)}, bf16[9,48,128]{2,1,0:T(8,128)(2,1)S(1)}, u32[]{:S(2)}, u32[]{:S(2)}) collective-permute-start(bf16[9,48,128]{2,1,0:T(8,128)(2,1)S(1)} %get-tuple-element.38), channel_id=1, source_target_pairs={{0,64},{64,128},{128,192},{192,0},{1,65},{65,129},{129,193},{193,1... | collective-permute-start | bytes 331784 | tf_op jit(solution)/shard_map/ppermute | solution.py:492
  22.2 8.4 %collective-permute-start.6 = (bf16[15,48,128]{2,1,0:T(8,128)(2,1)S(1)}, bf16[15,48,128]{2,1,0:T(8,128)(2,1)S(1)}, u32[]{:S(2)}, u32[]{:S(2)}) collective-permute-start(bf16[15,48,128]{2,1,0:T(8,128)(2,1)S(1)} %get-tuple-element.35.refs_3_), channel_id=1, source_target_pairs={{0,64},{64,128},{128,192},{192,0},{1,65},{65,129},{129,193},{193,1... | collective-permute-start | bytes 552968 | tf_op jit(solution)/shard_map/ppermute | solution.py:492
  24.2 2.8 %copy-start.3 = (bf16[384,192]{0,1:T(8,128)(2,1)S(1)}, bf16[384,192]{0,1:T(8,128)(2,1)}, u32[]{:S(2)}) copy-start(bf16[384,192]{0,1:T(8,128)(2,1)} %param.13) | copy-start | bytes 442372
  26.0 8.6 %collective-permute-start.5 = (bf16[15,48,128]{2,1,0:T(8,128)(2,1)S(1)}, bf16[15,48,128]{2,1,0:T(8,128)(2,1)S(1)}, u32[]{:S(2)}, u32[]{:S(2)}) collective-permute-start(bf16[15,48,128]{2,1,0:T(8,128)(2,1)S(1)} %get-tuple-element.41), channel_id=1, source_target_pairs={{0,64},{64,128},{128,192},{192,0},{1,65},{65,129},{129,193},{193,1... | collective-permute-start | bytes 552968 | tf_op jit(solution)/shard_map/ppermute | solution.py:492
  27.0 3.6 %copy-start.4 = (f32[192]{0:T(256)S(1)}, f32[192]{0:T(256)}, u32[]{:S(2)}) copy-start(f32[192]{0:T(256)} %refs_2_.5) | copy-start | bytes 2308
  27.0 8.1 %copy-start.2 = (bf16[3,3,3,192,192]{4,3,2,1,0:T(8,128)(2,1)S(1)}, bf16[3,3,3,192,192]{4,3,2,1,0:T(8,128)(2,1)}, u32[]{:S(2)}) copy-start(bf16[3,3,3,192,192]{4,3,2,1,0:T(8,128)(2,1)} %refs_0_.3) | copy-start | bytes 5971972
  31.0 7.6 %collective-permute-start.8 = (bf16[15,48,128]{2,1,0:T(8,128)(2,1)S(1)}, bf16[15,48,128]{2,1,0:T(8,128)(2,1)S(1)}, u32[]{:S(2)}, u32[]{:S(2)}) collective-permute-start(bf16[15,48,128]{2,1,0:T(8,128)(2,1)S(1)} %get-tuple-element.43.refs_1_), channel_id=1, source_target_pairs={{0,64},{64,128},{128,192},{192,0},{1,65},{65,129},{129,193},{193,1... | collective-permute-start | bytes 552968 | tf_op jit(solution)/shard_map/ppermute | solution.py:492
  35.0 6.8 %collective-permute-start.7 = (bf16[15,48,128]{2,1,0:T(8,128)(2,1)S(1)}, bf16[15,48,128]{2,1,0:T(8,128)(2,1)S(1)}, u32[]{:S(2)}, u32[]{:S(2)}) collective-permute-start(bf16[15,48,128]{2,1,0:T(8,128)(2,1)S(1)} %get-tuple-element.42.refs_0_), channel_id=1, source_target_pairs={{0,64},{64,128},{128,192},{192,0},{1,65},{65,129},{129,193},{193,1... | collective-permute-start | bytes 552968 | tf_op jit(solution)/shard_map/ppermute | solution.py:492

commit v5 on v4

--- a/solution.py
+++ b/solution.py
@@ -493,11 +493,13 @@
 
 
 def swap(value, offset):
-    count = lax.axis_size("rows")
-    pairs = [(i, i + 1) for i in range(offset, count - 1, 2)]
-    alone = set(range(count)) - {i for pair in pairs for i in pair}
+    groups, slabs = lax.axis_size("tm"), lax.axis_size("rows")
+    pairs = [(g * slabs + i, g * slabs + i + 1) for g in range(groups) for i in range(offset, slabs - 1, 2)]
+    if offset:
+        pairs += [(g * slabs + i, (g + 1) * slabs + i) for g in range(0, groups - 1, 2) for i in (0, slabs - 1)]
+    alone = set(range(groups * slabs)) - {i for pair in pairs for i in pair}
     return lax.ppermute(
-        value, "rows", pairs + [(b, a) for a, b in pairs] + [(i, i) for i in sorted(alone)]
+        value, ("tm", "rows"), pairs + [(b, a) for a, b in pairs] + [(i, i) for i in sorted(alone)]
     )
 
 
@@ -581,22 +583,23 @@
     second_work = [pltpu.VMEM((pixels1, 192), BF16)] + work(wide1, 192)
     packed2 = shape((wide2 * 3 // 2, width, 128), BF16)
     field = shape((3, wide1, width, 256), BF16)
+    early_inner, early_rest = call(
+        early_own_kernel,
+        (shape((inner_pixels, 192), F32), edge_sums),
+        [],
+        flops1,
+        (active, early, across),
+        after=(late_rest,),
+    )
     partial, late = call(
         late_second_kernel,
         (packed2, field),
         second_work,
         flops2,
         (late_inner, late_rest, inner, late_edges, gain_second, kernel_second),
+        after=(early_rest,),
     )
     before_late = onward(partial)
-    early_inner, early_rest = call(
-        early_own_kernel,
-        (shape((inner_pixels, 192), F32), edge_sums),
-        [],
-        flops1,
-        (active, early, across),
-        after=(partial,),
-    )
     partial, early = call(
         early_second_kernel,
         (packed2, field),
@@ -631,6 +634,7 @@
         third_work,
         1 << 24,
         (own, before_early, gain_third),
+        after=(mixed,),
     )
     before_early = onward(early)
     own, block_out = call(

time: 44 us -> 42.3 us (0.961)
  starting transfers between devices: 11.2 us -> 9.4 us
    ppermute x2, starting transfers between devices: 4.39 us -> 2.5 us  [swap(): lax.ppermute(value, ('tm', 'rows'), pairs + [(b, a) for a, b in pairs] +...]
  transfers between devices with their start and end apart: 9 -> 9, of which waited for: 5 -> 5; matrix products, arithmetic and copies ran while one was open for 0% -> 0% of each run, Pallas kernels for 47% -> 48%
where the time goes in v5:
time: 42.3 us; the launch traced here: 42.2 us
  Pallas kernels  23.4 us (55%)
  starting transfers between devices  9.4 us (22%)
  waiting for transfers between devices  8.17 us (19%)
  between operations  0.95 us (2%)
    pallas_call x16, Pallas kernels, call(): pl.pallas_call(placed, out_shape=out_shape, in_specs=[far if i in hbm els...  23.4 us
    ppermute x7, waiting for transfers between devices, onward(): lax.ppermute(value, 'tm', [(i, (i + 1) % count) for i in range(count)])  7.22 us
    ppermute x7, starting transfers between devices, onward(): lax.ppermute(value, 'tm', [(i, (i + 1) % count) for i in range(count)])  6.9 us
    ppermute x2, starting transfers between devices, swap(): lax.ppermute(value, ('tm', 'rows'), pairs + [(b, a) for a, b in pairs] +...  2.5 us
    ppermute x2, waiting for transfers between devices, swap(): lax.ppermute(value, ('tm', 'rows'), pairs + [(b, a) for a, b in pairs] +...  0.95 us
  transfers between devices with their start and end apart: 9, of which 5 were waited for; matrix products, arithmetic and copies ran while one was open for 0% of the time, Pallas kernels for 48%

profile of v5, /device:TPU:128, one launch (start us, length us, event | category | flops | bytes accessed | tf_op | source)
XLA Modules:
  0.0 42.2 jit_solution(11323964466441883216)
XLA Ops:
  0.6 0.0 copy-start
  0.6 1.2 %shard_map.95 = (bf16[2,8,48,384]{3,2,1,0:T(8,128)(2,1)S(1)}, f32[384]{0:T(512)S(1)}, bf16[2,3,48,384]{3,2,1,0:T(8,128)(2,1)S(1)}, bf16[2,3,48,384]{3,2,1,0:T(8,128)(2,1)S(1)}) custom-call(bf16[2,8,48,384]{3,2,1,0:T(8,128)(2,1)} %refs_0_.2, f32[384]{0:T(512)} %refs_1_.1), custom_call_target="tpu_custom_call" | custom-call | flops 17179869184 | bytes 4194304 | tf_op jit(solution)/shard_map/pallas_call | solution.py:59
  1.9 0.1 collective-permute-start
  2.0 2.4 %collective-permute-start.1 = (bf16[2,3,48,384]{3,2,1,0:T(8,128)(2,1)S(1)}, bf16[2,3,48,384]{3,2,1,0:T(8,128)(2,1)S(1)}, u32[]{:S(2)}, u32[]{:S(2)}) collective-permute-start(bf16[2,3,48,384]{3,2,1,0:T(8,128)(2,1)S(1)} %get-tuple-element.30), channel_id=1, source_target_pairs={{1,2},{3,4},{5,6},{7,8},{9,10},{11,12},{13,14},{15,16},{17,18},{19... | collective-permute-start | bytes 663560 | tf_op jit(solution)/shard_map/ppermute | solution.py:501
  4.4 0.0 copy-done
  4.4 2.5 %shard_map.96 = (bf16[2,8,48,384]{3,2,1,0:T(8,128)(2,1)S(1)}, bf16[2,9,48,128]{3,2,1,0:T(8,128)(2,1)S(1)}) custom-call(bf16[2,8,48,384]{3,2,1,0:T(8,128)(2,1)S(1)} %get-tuple-element.26.refs_0_.refs_3_, f32[384]{0:T(512)S(1)} %get-tuple-element.27.refs_1_.refs_2_, bf16[3,3,3,192,384]{4,3,2,1,0:T(8,128)(2,1)S(1)} %bitcast.3), custom_call_target="tpu_custom_call" | custom-call | flops 1528823808 | bytes 4194304 | tf_op jit(solution)/shard_map/pallas_call | solution.py:59
  6.9 1.6 %collective-permute-start.2 = (bf16[2,9,48,128]{3,2,1,0:T(8,128)(2,1)S(1)}, bf16[2,9,48,128]{3,2,1,0:T(8,128)(2,1)S(1)}, u32[]{:S(2)}, u32[]{:S(2)}) collective-permute-start(bf16[2,9,48,128]{3,2,1,0:T(8,128)(2,1)S(1)} %get-tuple-element.36), channel_id=1, source_target_pairs={{0,64},{64,128},{128,192},{192,0},{1,65},{65,129},{129,193},{193,1... | collective-permute-start | bytes 663560 | tf_op jit(solution)/shard_map/ppermute | solution.py:492
  8.6 1.2 %shard_map.97.refs_5_.refs_0_ = f32[288,192]{1,0:T(8,128)S(1)} custom-call(bf16[2,8,48,384]{3,2,1,0:T(8,128)(2,1)S(1)} %get-tuple-element.28.refs_0_.refs_3_, bf16[3,3,3,192,384]{4,3,2,1,0:T(8,128)(2,1)S(1)} %bitcast.4), custom_call_target="tpu_custom_call" | custom-call | flops 764411904 | bytes 4194304 | tf_op jit(solution)/shard_map/pallas_call | solution.py:59
  9.8 0.0 collective-permute-done.refs_0_.refs_4_
  9.8 0.9 %collective-permute-done.1.refs_1_.refs_5_ = bf16[2,3,48,384]{3,2,1,0:T(8,128)(2,1)S(1)} collective-permute-done((bf16[2,3,48,384]{3,2,1,0:T(8,128)(2,1)S(1)}, bf16[2,3,48,384]{3,2,1,0:T(8,128)(2,1)S(1)}, u32[]{:S(2)}, u32[]{:S(2)}) %collective-permute-start.1) | collective-permute-done | bytes 221216 | tf_op jit(solution)/shard_map/ppermute | solution.py:501
  10.8 1.1 %shard_map.98 = (bf16[9,48,128]{2,1,0:T(8,128)(2,1)S(1)}, bf16[2,5,48,384]{3,2,1,0:T(8,128)(2,1)S(1)}) custom-call(bf16[2,3,48,384]{3,2,1,0:T(8,128)(2,1)S(1)} %collective-permute-done.refs_0_.refs_4_, bf16[2,3,48,384]{3,2,1,0:T(8,128)(2,1)S(1)} %collective-permute-done.1.refs_1_.refs_5_, f32[384]{0:T(512)S(1)} %get-tuple-element.27.refs_1_.refs_2_, ...), custom_call_target="tpu_custom_call" | custom-call | flops 382205952 | bytes 4194304 | tf_op jit(solution)/shard_map/pallas_call | solution.py:59
  11.9 1.6 %collective-permute-start.4 = (bf16[9,48,128]{2,1,0:T(8,128)(2,1)S(1)}, bf16[9,48,128]{2,1,0:T(8,128)(2,1)S(1)}, u32[]{:S(2)}, u32[]{:S(2)}) collective-permute-start(bf16[9,48,128]{2,1,0:T(8,128)(2,1)S(1)} %get-tuple-element.32.refs_6_), channel_id=1, source_target_pairs={{0,64},{64,128},{128,192},{192,0},{1,65},{65,129},{129,193},{193,1... | collective-permute-start | bytes 331784 | tf_op jit(solution)/shard_map/ppermute | solution.py:492
  13.5 1.6 %shard_map.99 = (bf16[9,48,128]{2,1,0:T(8,128)(2,1)S(1)}, bf16[2,5,48,384]{3,2,1,0:T(8,128)(2,1)S(1)}) custom-call(bf16[2,3,48,384]{3,2,1,0:T(8,128)(2,1)S(1)} %collective-permute-done.refs_0_.refs_4_, bf16[2,3,48,384]{3,2,1,0:T(8,128)(2,1)S(1)} %collective-permute-done.1.refs_1_.refs_5_, f32[384]{0:T(512)S(1)} %get-tuple-element.27.refs_1_.refs_2_, ...), custom_call_target="tpu_custom_call" | custom-call | flops 764411904 | bytes 4194304 | tf_op jit(solution)/shard_map/pallas_call | solution.py:59
  15.2 1.6 %collective-permute-start.3 = (bf16[9,48,128]{2,1,0:T(8,128)(2,1)S(1)}, bf16[9,48,128]{2,1,0:T(8,128)(2,1)S(1)}, u32[]{:S(2)}, u32[]{:S(2)}) collective-permute-start(bf16[9,48,128]{2,1,0:T(8,128)(2,1)S(1)} %get-tuple-element.37), channel_id=1, source_target_pairs={{0,64},{64,128},{128,192},{192,0},{1,65},{65,129},{129,193},{193,1... | collective-permute-start | bytes 331784 | tf_op jit(solution)/shard_map/ppermute | solution.py:492
  16.8 1.2 %shard_map.100.refs_3_.refs_1_ = f32[288,192]{1,0:T(8,128)S(1)} custom-call(bf16[2,5,48,384]{3,2,1,0:T(8,128)(2,1)S(1)} %get-tuple-element.33.refs_0_.refs_1_, bf16[2,5,48,384]{3,2,1,0:T(8,128)(2,1)S(1)} %get-tuple-element.31.refs_5_.refs_1_, bf16[3,3,3,192,384]{4,3,2,1,0:T(8,128)(2,1)S(1)} %bitcast.7), custom_call_target="tpu_custom_call" | custom-call | flops 764411904 | bytes 4194304 | tf_op jit(solution)/shard_map/pallas_call | solution.py:59
  18.0 0.0 copy-start.1
  18.0 0.0 copy-start.4
  18.0 1.4 %shard_map.101 = (f32[288,192]{1,0:T(8,128)S(1)}, f32[288,192]{1,0:T(8,128)S(1)}) custom-call(bf16[2,8,48,384]{3,2,1,0:T(8,128)(2,1)S(1)} %get-tuple-element.28.refs_0_.refs_3_, bf16[2,5,48,384]{3,2,1,0:T(8,128)(2,1)S(1)} %get-tuple-element.33.refs_0_.refs_1_, bf16[3,3,3,192,384]{4,3,2,1,0:T(8,128)(2,1)S(1)} %bitcast.8, ...), custom_call_target="tpu_custom_call" | custom-call | flops 764411904 | bytes 4194304 | tf_op jit(solution)/shard_map/pallas_call | solution.py:59
  19.4 0.0 collective-permute-done.2.refs_2_
  19.4 0.0 collective-permute-done.4.refs_3_
  19.5 0.3 copy-done.1
  19.8 0.0 copy-done.4
  19.8 1.2 %shard_map.102 = (bf16[15,48,128]{2,1,0:T(8,128)(2,1)S(1)}, bf16[3,12,48,256]{3,2,1,0:T(8,128)(2,1)S(1)}) custom-call(f32[288,192]{1,0:T(8,128)S(1)} %shard_map.97.refs_5_.refs_0_, f32[288,192]{1,0:T(8,128)S(1)} %shard_map.100.refs_3_.refs_1_, bf16[2,9,48,128]{3,2,1,0:T(8,128)(2,1)S(1)} %collective-permute-done.2.refs_2_, ...), custom_call_target="tpu_custom_call" | custom-call | flops 318504960 | bytes 4194304 | tf_op jit(solution)/shard_map/pallas_call | solution.py:59
  21.0 0.0 copy-start.3
  21.0 1.5 %collective-permute-start.6 = (bf16[15,48,128]{2,1,0:T(8,128)(2,1)S(1)}, bf16[15,48,128]{2,1,0:T(8,128)(2,1)S(1)}, u32[]{:S(2)}, u32[]{:S(2)}) collective-permute-start(bf16[15,48,128]{2,1,0:T(8,128)(2,1)S(1)} %get-tuple-element.42), channel_id=1, source_target_pairs={{0,64},{64,128},{128,192},{192,0},{1,65},{65,129},{129,193},{193,1... | collective-permute-start | bytes 552968 | tf_op jit(solution)/shard_map/ppermute | solution.py:492
  22.6 0.0 collective-permute-done.3.refs_3_
  22.6 1.8 %shard_map.103 = (bf16[15,48,128]{2,1,0:T(8,128)(2,1)S(1)}, bf16[3,12,48,256]{3,2,1,0:T(8,128)(2,1)S(1)}) custom-call(f32[288,192]{1,0:T(8,128)S(1)} %get-tuple-element.34.refs_0_, f32[288,192]{1,0:T(8,128)S(1)} %get-tuple-element.35.refs_6_.refs_1_, bf16[2,9,48,128]{3,2,1,0:T(8,128)(2,1)S(1)} %collective-permute-done.2.refs_2_, ...), custom_call_target="tpu_custom_call" | custom-call | flops 637009920 | bytes 4194304 | tf_op jit(solution)/shard_map/pallas_call | solution.py:59
  24.3 0.3 collective-permute-start.5
  24.6 0.0 copy-done.3
  24.6 0.0 copy-start.5
  24.6 0.0 copy-start.2
  24.6 2.1 %shard_map.104.refs_1_.refs_0_ = f32[2,480,192]{2,1,0:T(8,128)S(1)} custom-call(bf16[3,12,48,256]{3,2,1,0:T(8,128)(2,1)S(1)} %get-tuple-element.39.refs_0_, bf16[3,12,48,256]{3,2,1,0:T(8,128)(2,1)S(1)} %get-tuple-element.38.refs_6_.refs_1_, bf16[3,3,3,192,192]{4,3,2,1,0:T(8,128)(2,1)S(1)} %copy-done.1, ...), custom_call_target="tpu_custom_call" | custom-call | flops 955514880 | bytes 4194304 | tf_op jit(solution)/shard_map/pallas_call | solution.py:59
  26.7 2.2 %collective-permute-done.6.refs_1_ = bf16[15,48,128]{2,1,0:T(8,128)(2,1)S(1)} collective-permute-done((bf16[15,48,128]{2,1,0:T(8,128)(2,1)S(1)}, bf16[15,48,128]{2,1,0:T(8,128)(2,1)S(1)}, u32[]{:S(2)}, u32[]{:S(2)}) %collective-permute-start.6) | collective-permute-done | bytes 184352 | tf_op jit(solution)/shard_map/ppermute | solution.py:492
  28.9 0.0 copy-done.5
  28.9 0.4 %shard_map.107 = (bf16[8,48,192]{2,1,0:T(8,128)(2,1)S(1)}, bf16[15,48,128]{2,1,0:T(8,128)(2,1)S(1)}) custom-call(f32[2,480,192]{2,1,0:T(8,128)S(1)} %shard_map.104.refs_1_.refs_0_, bf16[15,48,128]{2,1,0:T(8,128)(2,1)S(1)} %collective-permute-done.6.refs_1_, f32[192]{0:T(256)S(1)} %copy-done.5), custom_call_target="tpu_custom_call" | custom-call | flops 16777216 | bytes 4194304 | tf_op jit(solution)/shard_map/pallas_call | solution.py:59
  29.4 0.1 collective-permute-start.8
  29.5 0.0 copy-done.2
  29.5 0.9 %shard_map.105.refs_3_.refs_2_.refs_1_ = bf16[3,4,768,192]{3,2,1,0:T(8,128)(2,1)S(1)} custom-call(bf16[3,3,3,192,192]{4,3,2,1,0:T(8,128)(2,1)S(1)} %copy-done.2, f32[2,480,192]{2,1,0:T(8,128)S(1)} %shard_map.104.refs_1_.refs_0_), custom_call_target="tpu_custom_call" | custom-call | flops 16777216 | bytes 4194304 | tf_op jit(solution)/shard_map/pallas_call | solution.py:59
  30.4 2.7 %collective-permute-done.5.refs_1_ = bf16[15,48,128]{2,1,0:T(8,128)(2,1)S(1)} collective-permute-done((bf16[15,48,128]{2,1,0:T(8,128)(2,1)S(1)}, bf16[15,48,128]{2,1,0:T(8,128)(2,1)S(1)}, u32[]{:S(2)}, u32[]{:S(2)}) %collective-permute-start.5) | collective-permute-done | bytes 184352 | tf_op jit(solution)/shard_map/ppermute | solution.py:492
  33.1 0.4 %shard_map.106 = (bf16[8,48,192]{2,1,0:T(8,128)(2,1)S(1)}, bf16[15,48,128]{2,1,0:T(8,128)(2,1)S(1)}) custom-call(f32[2,480,192]{2,1,0:T(8,128)S(1)} %shard_map.104.refs_1_.refs_0_, bf16[15,48,128]{2,1,0:T(8,128)(2,1)S(1)} %collective-permute-done.5.refs_1_, f32[192]{0:T(256)S(1)} %copy-done.5, bf16[3,4,768,192]{3,2,1,0:T(8,128)(2,1)S(1)} %shard_map.105.refs_3_.refs_2_.refs_1_), custom_call_target="tpu_custom_call" | custom-call | flops 16777216 | bytes 4194304 | tf_op jit(solution)/shard_map/pallas_call | solution.py:59
  33.5 0.1 collective-permute-start.7
  33.6 2.7 %shard_map.108 = (f32[2,4,384,192]{3,2,1,0:T(8,128)S(1)}, bf16[2,8,48,192]{3,2,1,0:T(8,128)(2,1)}) custom-call(bf16[15,48,128]{2,1,0:T(8,128)(2,1)S(1)} %get-tuple-element.41.refs_0_, bf16[15,48,128]{2,1,0:T(8,128)(2,1)S(1)} %get-tuple-element.43.refs_1_, bf16[3,4,768,192]{3,2,1,0:T(8,128)(2,1)S(1)} %shard_map.105.refs_3_.refs_2_.refs_1_, ...), custom_call_target="tpu_custom_call" | custom-call | flops 764411904 | bytes 4194304 | tf_op jit(solution)/shard_map/pallas_call | solution.py:59
  36.3 0.4 collective-permute-done.8.refs_0_
  36.6 1.8 %shard_map.109 = (bf16[2,8,2,96,192]{4,3,2,1,0:T(8,128)(2,1)}, f32[4,384,192]{2,1,0:T(8,128)S(1)}) custom-call(bf16[15,48,128]{2,1,0:T(8,128)(2,1)S(1)} %collective-permute-done.8.refs_0_, bf16[3,4,768,192]{3,2,1,0:T(8,128)(2,1)S(1)} %shard_map.105.refs_3_.refs_2_.refs_1_, f32[2,4,384,192]{3,2,1,0:T(8,128)S(1)} %get-tuple-element.47.refs_2_), custom_call_target="tpu_custom_call" | custom-call | flops 509607936 | bytes 4194304 | tf_op jit(solution)/shard_map/pallas_call | solution.py:59
  38.4 1.9 %collective-permute-done.7.refs_0_ = bf16[15,48,128]{2,1,0:T(8,128)(2,1)S(1)} collective-permute-done((bf16[15,48,128]{2,1,0:T(8,128)(2,1)S(1)}, bf16[15,48,128]{2,1,0:T(8,128)(2,1)S(1)}, u32[]{:S(2)}, u32[]{:S(2)}) %collective-permute-start.7) | collective-permute-done | bytes 184352 | tf_op jit(solution)/shard_map/ppermute | solution.py:492
  40.3 1.7 %shard_map.110 = bf16[2,8,2,96,192]{4,3,2,1,0:T(8,128)(2,1)} custom-call(bf16[15,48,128]{2,1,0:T(8,128)(2,1)S(1)} %collective-permute-done.7.refs_0_, bf16[3,4,768,192]{3,2,1,0:T(8,128)(2,1)S(1)} %shard_map.105.refs_3_.refs_2_.refs_1_, f32[4,384,192]{2,1,0:T(8,128)S(1)} %get-tuple-element.48.refs_2_, ...), custom_call_target="tpu_custom_call", output_to_operand_aliasing={{}: (3, {})} | custom-call | flops 254803968 | bytes 4194304 | tf_op jit(solution)/shard_map/pallas_call | solution.py:59
Async XLA Ops:
  0.6 3.8 %copy-start = (bf16[3,3,3,384,192]{3,4,2,1,0:T(8,128)(2,1)S(1)}, bf16[3,3,3,384,192]{3,4,2,1,0:T(8,128)(2,1)}, u32[]{:S(2)}) copy-start(bf16[3,3,3,384,192]{3,4,2,1,0:T(8,128)(2,1)} %param.10) | copy-start | bytes 11943940
  1.9 7.9 %collective-permute-start = (bf16[2,3,48,384]{3,2,1,0:T(8,128)(2,1)S(1)}, bf16[2,3,48,384]{3,2,1,0:T(8,128)(2,1)S(1)}, u32[]{:S(2)}, u32[]{:S(2)}) collective-permute-start(bf16[2,3,48,384]{3,2,1,0:T(8,128)(2,1)S(1)} %get-tuple-element.29), channel_id=1, source_target_pairs={{0,1},{2,3},{4,5},{6,7},{8,9},{10,11},{12,13},{14,15},{16,17},{18,... | collective-permute-start | bytes 663560 | tf_op jit(solution)/shard_map/ppermute | solution.py:501
  2.0 8.8 %collective-permute-start.1 = (bf16[2,3,48,384]{3,2,1,0:T(8,128)(2,1)S(1)}, bf16[2,3,48,384]{3,2,1,0:T(8,128)(2,1)S(1)}, u32[]{:S(2)}, u32[]{:S(2)}) collective-permute-start(bf16[2,3,48,384]{3,2,1,0:T(8,128)(2,1)S(1)} %get-tuple-element.30), channel_id=1, source_target_pairs={{1,2},{3,4},{5,6},{7,8},{9,10},{11,12},{13,14},{15,16},{17,18},{19... | collective-permute-start | bytes 663560 | tf_op jit(solution)/shard_map/ppermute | solution.py:501
  6.9 12.5 %collective-permute-start.2 = (bf16[2,9,48,128]{3,2,1,0:T(8,128)(2,1)S(1)}, bf16[2,9,48,128]{3,2,1,0:T(8,128)(2,1)S(1)}, u32[]{:S(2)}, u32[]{:S(2)}) collective-permute-start(bf16[2,9,48,128]{3,2,1,0:T(8,128)(2,1)S(1)} %get-tuple-element.36), channel_id=1, source_target_pairs={{0,64},{64,128},{128,192},{192,0},{1,65},{65,129},{129,193},{193,1... | collective-permute-start | bytes 663560 | tf_op jit(solution)/shard_map/ppermute | solution.py:492
  11.9 7.5 %collective-permute-start.4 = (bf16[9,48,128]{2,1,0:T(8,128)(2,1)S(1)}, bf16[9,48,128]{2,1,0:T(8,128)(2,1)S(1)}, u32[]{:S(2)}, u32[]{:S(2)}) collective-permute-start(bf16[9,48,128]{2,1,0:T(8,128)(2,1)S(1)} %get-tuple-element.32.refs_6_), channel_id=1, source_target_pairs={{0,64},{64,128},{128,192},{192,0},{1,65},{65,129},{129,193},{193,1... | collective-permute-start | bytes 331784 | tf_op jit(solution)/shard_map/ppermute | solution.py:492
  15.2 7.4 %collective-permute-start.3 = (bf16[9,48,128]{2,1,0:T(8,128)(2,1)S(1)}, bf16[9,48,128]{2,1,0:T(8,128)(2,1)S(1)}, u32[]{:S(2)}, u32[]{:S(2)}) collective-permute-start(bf16[9,48,128]{2,1,0:T(8,128)(2,1)S(1)} %get-tuple-element.37), channel_id=1, source_target_pairs={{0,64},{64,128},{128,192},{192,0},{1,65},{65,129},{129,193},{193,1... | collective-permute-start | bytes 331784 | tf_op jit(solution)/shard_map/ppermute | solution.py:492
  18.0 1.8 %copy-start.1 = (bf16[3,3,3,192,192]{4,3,2,1,0:T(8,128)(2,1)S(1)}, bf16[3,3,3,192,192]{4,3,2,1,0:T(8,128)(2,1)}, u32[]{:S(2)}) copy-start(bf16[3,3,3,192,192]{4,3,2,1,0:T(8,128)(2,1)} %refs_2_.3) | copy-start | bytes 5971972
  18.0 1.7 %copy-start.4 = (f32[192]{0:T(256)S(1)}, f32[192]{0:T(256)}, u32[]{:S(2)}) copy-start(f32[192]{0:T(256)} %refs_4_.3) | copy-start | bytes 2308
  21.0 3.6 %copy-start.3 = (bf16[384,192]{0,1:T(8,128)(2,1)S(1)}, bf16[384,192]{0,1:T(8,128)(2,1)}, u32[]{:S(2)}) copy-start(bf16[384,192]{0,1:T(8,128)(2,1)} %param.13) | copy-start | bytes 442372
  21.0 7.9 %collective-permute-start.6 = (bf16[15,48,128]{2,1,0:T(8,128)(2,1)S(1)}, bf16[15,48,128]{2,1,0:T(8,128)(2,1)S(1)}, u32[]{:S(2)}, u32[]{:S(2)}) collective-permute-start(bf16[15,48,128]{2,1,0:T(8,128)(2,1)S(1)} %get-tuple-element.42), channel_id=1, source_target_pairs={{0,64},{64,128},{128,192},{192,0},{1,65},{65,129},{129,193},{193,1... | collective-permute-start | bytes 552968 | tf_op jit(solution)/shard_map/ppermute | solution.py:492
  24.3 8.7 %collective-permute-start.5 = (bf16[15,48,128]{2,1,0:T(8,128)(2,1)S(1)}, bf16[15,48,128]{2,1,0:T(8,128)(2,1)S(1)}, u32[]{:S(2)}, u32[]{:S(2)}) collective-permute-start(bf16[15,48,128]{2,1,0:T(8,128)(2,1)S(1)} %get-tuple-element.40), channel_id=1, source_target_pairs={{0,64},{64,128},{128,192},{192,0},{1,65},{65,129},{129,193},{193,1... | collective-permute-start | bytes 552968 | tf_op jit(solution)/shard_map/ppermute | solution.py:492
  24.6 4.3 %copy-start.5 = (f32[192]{0:T(256)S(1)}, f32[192]{0:T(256)}, u32[]{:S(2)}) copy-start(f32[192]{0:T(256)} %refs_2_.5) | copy-start | bytes 2308
  24.6 4.8 %copy-start.2 = (bf16[3,3,3,192,192]{4,3,2,1,0:T(8,128)(2,1)S(1)}, bf16[3,3,3,192,192]{4,3,2,1,0:T(8,128)(2,1)}, u32[]{:S(2)}) copy-start(bf16[3,3,3,192,192]{4,3,2,1,0:T(8,128)(2,1)} %refs_0_.3) | copy-start | bytes 5971972
  29.4 7.2 %collective-permute-start.8 = (bf16[15,48,128]{2,1,0:T(8,128)(2,1)S(1)}, bf16[15,48,128]{2,1,0:T(8,128)(2,1)S(1)}, u32[]{:S(2)}, u32[]{:S(2)}) collective-permute-start(bf16[15,48,128]{2,1,0:T(8,128)(2,1)S(1)} %get-tuple-element.43.refs_1_), channel_id=1, source_target_pairs={{0,64},{64,128},{128,192},{192,0},{1,65},{65,129},{129,193},{193,1... | collective-permute-start | bytes 552968 | tf_op jit(solution)/shard_map/ppermute | solution.py:492
  33.5 6.8 %collective-permute-start.7 = (bf16[15,48,128]{2,1,0:T(8,128)(2,1)S(1)}, bf16[15,48,128]{2,1,0:T(8,128)(2,1)S(1)}, u32[]{:S(2)}, u32[]{:S(2)}) collective-permute-start(bf16[15,48,128]{2,1,0:T(8,128)(2,1)S(1)} %get-tuple-element.41.refs_0_), channel_id=1, source_target_pairs={{0,64},{64,128},{128,192},{192,0},{1,65},{65,129},{129,193},{193,1... | collective-permute-start | bytes 552968 | tf_op jit(solution)/shard_map/ppermute | solution.py:492

commit v6 on v5

--- a/solution.py
+++ b/solution.py
@@ -184,18 +184,24 @@
 OWN = (((0, 2),), ((0, 1), (1, 2)))
 
 
-def activate_rows(ref, gain, squares, scale, out):
-    rows, width, channels = ref.shape
+def activate_rows(fields, gain, squares, scale, put):
+    rows, width, channels = fields[0].shape
     pixels = rows * width
-    v = ref[...].astype(F32)
-    squares[0:pixels] = (v * v).astype(BF16).reshape(pixels, channels)
-    scale[0:pixels] = scales(squares[0:pixels], channels)
-    for row in range(rows):
-        part = slice(row * width, (row + 1) * width)
-        for at, lanes in spans(channels):
-            out[row, :, at : at + lanes] = activated(
-                ref[row, :, at : at + lanes].astype(F32), scale[part], gain[at : at + lanes].reshape(1, lanes)
-            ).astype(BF16)
+    for i, ref in enumerate(fields):
+        v = ref[...].astype(F32)
+        squares[i * pixels : (i + 1) * pixels] = (v * v).astype(BF16).reshape(pixels, channels)
+    every = len(fields) * pixels
+    scale[0:every] = scales(squares[0:every], channels)
+    for i, ref in enumerate(fields):
+        for row in range(rows):
+            part = slice(i * pixels + row * width, i * pixels + (row + 1) * width)
+            for at, lanes in spans(channels):
+                v = activated(
+                    ref[row, :, at : at + lanes].astype(F32),
+                    scale[part],
+                    gain[at : at + lanes].reshape(1, lanes),
+                )
+                put(i, row, slice(at, at + lanes), v.astype(BF16))
 
 
 def rim_kernel(place, latents, gain, held, held_gain, near, far, sems):
@@ -214,8 +220,14 @@
 
 def inner_kernel(place, held, gain, weights, active, packed, squares, scale, sums):
     frames, rows, width, channels = held.shape
+
+    def put(frame, row, lanes, value):
+        active[frame, row, :, lanes] = value
+
     for frame in range(frames):
-        activate_rows(held.at[frame], gain, squares, scale, active.at[frame])
+        activate_rows(
+            [held.at[frame]], gain, squares, scale, lambda _, *args, frame=frame: put(frame, *args)
+        )
     count = rows - 2
     for out, taps in ((1, ((1, 0),)), (0, ((0, 0), (1, 1)))):
         terms = [(windows(active.at[frame], count), a) for frame, a in taps]
@@ -238,8 +250,12 @@
         next_chip = jnp.where(inner, far[frame, row], jnp.zeros_like(chip))
         raw[row] = jnp.where(odd, chip, next_chip)
         raw[HALO + row] = jnp.where(odd, next_chip, chip)
-    activate_rows(raw.at[0:HALO], gain, squares, scale, edges.at[0, 0:HALO])
-    activate_rows(raw.at[HALO : 2 * HALO], gain, squares, scale, edges.at[1, 2 : 2 + HALO])
+
+    def put(_, row, lanes, value):
+        side, at = divmod(row, HALO)
+        edges[side, at + 2 * side, :, lanes] = value
+
+    activate_rows([raw], gain, squares, scale, put)
     edges[0, HALO : HALO + 2] = active[frame, 0:2]
     edges[1, 0:2] = active[frame, rows - 2 : rows]
 
@@ -274,11 +290,13 @@
     convolve(own, dot_t, weights, terms, 2 * HALO, early.shape[2])
 
 
-def early_own_kernel(place, active, early, weights, inner, edges):
-    count, width = active.shape[1] - 2, active.shape[2]
+def early_own_kernel(place, active, early, weights, own, tall):
+    rows, width = active.shape[1], active.shape[2]
+    tall[0:HALO] = early[0, 0:HALO]
+    tall[HALO : HALO + rows] = active[0]
+    tall[HALO + rows :] = early[1, 2:]
     (frame, a), = OWN[0]
-    convolve(inner, dot_t, weights, [(windows(active.at[frame], count), a)], count, width)
-    convolve(edges, dot_t, weights, [(edge_windows(early), a)], 2 * HALO, width)
+    convolve(own, dot_t, weights, [(windows(tall, rows + 4), a)], rows + 4, width)
 
 
 def finish(place, own, before, gain, raw, squares, scale, keep):
@@ -358,10 +376,10 @@
 
 
 def early_second_kernel(
-    place, own_inner, own_edges, inner, edges, gain, kernel, late, partial, field, raw, squares, scale
+    place, own, inner, edges, gain, kernel, late, partial, field, raw, squares, scale
 ):
     before = joined(inner.at[0], edges)
-    own = joined_own(own_inner, own_edges, field.shape[2])
+    own = rows_of(own, field.shape[2])
     second(place, own, before, gain, kernel, [(field, 0), (late, 1)], partial, field, raw, squares, scale)
 
 
@@ -409,13 +427,13 @@
 
     for a in range(3):
         for i in range(2):
-            rows = [halves([kernel[a, b, e].astype(F32) for b in range(3)], i) for e in range(3)]
+            rows = [halves([kernel[a, b, e] for b in range(3)], i) for e in range(3)]
             for j in range(2):
                 upper = halves([rows[e][0] for e in range(3)], j)
                 lower = halves([rows[e][1] for e in range(3)], j)
                 for column in range(2):
                     at = 384 * column
-                    for part in two_rows_weights(upper[column].astype(BF16), lower[column].astype(BF16)):
+                    for part in two_rows_weights(upper[column], lower[column]):
                         out[a, 2 * i + j, at : at + part.shape[0]] = part
                         at += part.shape[0]
 
@@ -464,8 +482,10 @@
         for row in range(rows):
             fine[i, row, :, 0:128] = woven[i, row, 0].astype(BF16)
             fine[i, row, :, 128:192] = woven[i, row, 1, :, 0:64].astype(BF16)
-        copies.append(pltpu.make_async_copy(fine.at[i], out.at[:, i], sems.at[i]))
-        copies[-1].start()
+            if row % 2:
+                part = slice(row - 1, row + 1)
+                copies.append(pltpu.make_async_copy(fine.at[i, part], out.at[part, i], sems.at[i, row // 2]))
+                copies[-1].start()
     return copies
 
 
@@ -485,6 +505,11 @@
     fill_field(field, *packed_parts(packed, place[0] > 0))
     for copy in write_out(rest, field, kernel, 0, rows, width, woven, fine, decoded.at[0], sems):
         copy.wait()
+
+
+def onward_open(value):
+    count = lax.axis_size("tm")
+    return lax.ppermute(value, "tm", [(i, i + 1) for i in range(count - 1)])
 
 
 def onward(value):
@@ -558,7 +583,7 @@
     )
     edge_sums = shape((2 * HALO * width, 192), F32)
     edge_work = [pltpu.VMEM(edge_sums.shape, F32), pltpu.VMEM((2 * HALO, width, channels), BF16)]
-    edge_work += work(HALO, channels)
+    edge_work += work(2 * HALO, channels)
     ends = shape((2, HALO + 2, width, channels), BF16)
     packed1 = shape((HALO * 3, width, 128), BF16)
     partial, late = call(
@@ -579,15 +604,15 @@
         after=(partial,),
     )
     early_edges = onward(partial)
-    (late_rest,) = call(late_edge_own_kernel, (edge_sums,), [], flops1, (early, late, across))
+    (late_rest,) = call(late_edge_own_kernel, (edge_sums,), [], 1 << 20, (early, late, across))
     second_work = [pltpu.VMEM((pixels1, 192), BF16)] + work(wide1, 192)
     packed2 = shape((wide2 * 3 // 2, width, 128), BF16)
     field = shape((3, wide1, width, 256), BF16)
-    early_inner, early_rest = call(
+    (early_own,) = call(
         early_own_kernel,
-        (shape((inner_pixels, 192), F32), edge_sums),
-        [],
-        flops1,
+        (shape((pixels1, 192), F32),),
+        [pltpu.VMEM((wide1 + 2, width, channels), BF16)],
+        1 << 20,
         (active, early, across),
         after=(late_rest,),
     )
@@ -597,7 +622,7 @@
         second_work,
         flops2,
         (late_inner, late_rest, inner, late_edges, gain_second, kernel_second),
-        after=(early_rest,),
+        after=(early_own,),
     )
     before_late = onward(partial)
     partial, early = call(
@@ -605,7 +630,7 @@
         (packed2, field),
         second_work,
         2 * flops2,
-        (early_inner, early_rest, inner, early_edges, gain_second, kernel_second, late),
+        (early_own, inner, early_edges, gain_second, kernel_second, late),
     )
     before_early = onward(partial)
     (own,) = call(
@@ -636,7 +661,7 @@
         (own, before_early, gain_third),
         after=(mixed,),
     )
-    before_early = onward(early)
+    before_early = onward_open(early)
     own, block_out = call(
         third_own_kernel,
         (shape((2, 4, pixels, 192), F32), shape((2, rows, width, 192), BF16)),
@@ -649,7 +674,7 @@
         pltpu.VMEM((3, wide2, width, 256), BF16),
         pltpu.VMEM((2, rows, 2, 2 * width, 128), F32),
         pltpu.VMEM((2, rows, 2 * width, 192), BF16),
-        dma((2,)),
+        dma((2, rows // 2)),
     ]
     fine = shape((2, rows, 2, 2 * width, 192), BF16)
     decoded, rest = call(

time: 42.3 us -> 41 us (0.969)
  waiting for transfers between devices: 8.17 us -> 6.1 us
  starting transfers between devices: 9.4 us -> 10.8 us
  Pallas kernels: 23.4 us -> 22.7 us
    ppermute x7 -> x6, waiting for transfers between devices: 7.22 us -> 5.15 us  [onward(): lax.ppermute(value, 'tm', [(i, (i + 1) % count) for i in range(count)])]
    ppermute x0 -> x1, starting transfers between devices: none -> 1.48 us  [onward_open(): return lax.ppermute(value, 'tm', [(i, i + 1) for i in range(count - 1)])]
    pallas_call x16, Pallas kernels: 23.4 us -> 22.7 us  [call(): pl.pallas_call(placed, out_shape=out_shape, in_specs=[far if i in hbm els...]
    ppermute x7 -> x6, starting transfers between devices: 6.9 us -> 6.82 us  [onward(): lax.ppermute(value, 'tm', [(i, (i + 1) % count) for i in range(count)])]
  transfers between devices with their start and end apart: 9 -> 9, of which waited for: 5 -> 3; matrix products, arithmetic and copies ran while one was open for 0% -> 0% of each run, Pallas kernels for 48% -> 48%
where the time goes in v6:
time: 41 us; the launch traced here: 40.9 us
  Pallas kernels  22.7 us (55%)
  starting transfers between devices  10.8 us (26%)
  waiting for transfers between devices  6.1 us (15%)
  between operations  0.96 us (2%)
    pallas_call x16, Pallas kernels, call(): pl.pallas_call(placed, out_shape=out_shape, in_specs=[far if i in hbm els...  22.7 us
    ppermute x6, starting transfers between devices, onward(): lax.ppermute(value, 'tm', [(i, (i + 1) % count) for i in range(count)])  6.82 us
    ppermute x6, waiting for transfers between devices, onward(): lax.ppermute(value, 'tm', [(i, (i + 1) % count) for i in range(count)])  5.15 us
    ppermute x2, starting transfers between devices, swap(): lax.ppermute(value, ('tm', 'rows'), pairs + [(b, a) for a, b in pairs] +...  2.5 us
    ppermute x1, starting transfers between devices, onward_open(): return lax.ppermute(value, 'tm', [(i, i + 1) for i in range(count - 1)])  1.48 us
    ppermute x2, waiting for transfers between devices, swap(): lax.ppermute(value, ('tm', 'rows'), pairs + [(b, a) for a, b in pairs] +...  0.95 us
  transfers between devices with their start and end apart: 9, of which 3 were waited for; matrix products, arithmetic and copies ran while one was open for 0% of the time, Pallas kernels for 48%

profile of v6, /device:TPU:128, one launch (start us, length us, event | category | flops | bytes accessed | tf_op | source)
XLA Modules:
  0.0 40.9 jit_solution(14645828398266606026)
XLA Ops:
  0.6 0.0 copy-start
  0.6 1.2 %shard_map.95 = (bf16[2,8,48,384]{3,2,1,0:T(8,128)(2,1)S(1)}, f32[384]{0:T(512)S(1)}, bf16[2,3,48,384]{3,2,1,0:T(8,128)(2,1)S(1)}, bf16[2,3,48,384]{3,2,1,0:T(8,128)(2,1)S(1)}) custom-call(bf16[2,8,48,384]{3,2,1,0:T(8,128)(2,1)} %refs_0_.2, f32[384]{0:T(512)} %refs_1_.1), custom_call_target="tpu_custom_call" | custom-call | flops 17179869184 | bytes 4194304 | tf_op jit(solution)/shard_map/pallas_call | solution.py:59
  1.9 0.1 collective-permute-start
  2.0 2.4 %collective-permute-start.1 = (bf16[2,3,48,384]{3,2,1,0:T(8,128)(2,1)S(1)}, bf16[2,3,48,384]{3,2,1,0:T(8,128)(2,1)S(1)}, u32[]{:S(2)}, u32[]{:S(2)}) collective-permute-start(bf16[2,3,48,384]{3,2,1,0:T(8,128)(2,1)S(1)} %get-tuple-element.28), channel_id=1, source_target_pairs={{1,2},{3,4},{5,6},{7,8},{9,10},{11,12},{13,14},{15,16},{17,18},{19... | collective-permute-start | bytes 663560 | tf_op jit(solution)/shard_map/ppermute | solution.py:526
  4.4 0.0 copy-done
  4.4 2.5 %shard_map.96 = (bf16[2,8,48,384]{3,2,1,0:T(8,128)(2,1)S(1)}, bf16[2,9,48,128]{3,2,1,0:T(8,128)(2,1)S(1)}) custom-call(bf16[2,8,48,384]{3,2,1,0:T(8,128)(2,1)S(1)} %get-tuple-element.24.refs_0_.refs_3_, f32[384]{0:T(512)S(1)} %get-tuple-element.25.refs_1_.refs_2_, bf16[3,3,3,192,384]{4,3,2,1,0:T(8,128)(2,1)S(1)} %bitcast.3), custom_call_target="tpu_custom_call" | custom-call | flops 1528823808 | bytes 4194304 | tf_op jit(solution)/shard_map/pallas_call | solution.py:59
  6.9 1.6 %collective-permute-start.2 = (bf16[2,9,48,128]{3,2,1,0:T(8,128)(2,1)S(1)}, bf16[2,9,48,128]{3,2,1,0:T(8,128)(2,1)S(1)}, u32[]{:S(2)}, u32[]{:S(2)}) collective-permute-start(bf16[2,9,48,128]{3,2,1,0:T(8,128)(2,1)S(1)} %get-tuple-element.32), channel_id=1, source_target_pairs={{0,64},{64,128},{128,192},{192,0},{1,65},{65,129},{129,193},{193,1... | collective-permute-start | bytes 663560 | tf_op jit(solution)/shard_map/ppermute | solution.py:517
  8.6 1.2 %shard_map.97.refs_5_.refs_0_ = f32[288,192]{1,0:T(8,128)S(1)} custom-call(bf16[2,8,48,384]{3,2,1,0:T(8,128)(2,1)S(1)} %get-tuple-element.26.refs_0_.refs_3_, bf16[3,3,3,192,384]{4,3,2,1,0:T(8,128)(2,1)S(1)} %bitcast.4), custom_call_target="tpu_custom_call" | custom-call | flops 764411904 | bytes 4194304 | tf_op jit(solution)/shard_map/pallas_call | solution.py:59
  9.8 0.0 collective-permute-done.refs_0_.refs_4_
  9.8 0.9 %collective-permute-done.1.refs_1_.refs_5_ = bf16[2,3,48,384]{3,2,1,0:T(8,128)(2,1)S(1)} collective-permute-done((bf16[2,3,48,384]{3,2,1,0:T(8,128)(2,1)S(1)}, bf16[2,3,48,384]{3,2,1,0:T(8,128)(2,1)S(1)}, u32[]{:S(2)}, u32[]{:S(2)}) %collective-permute-start.1) | collective-permute-done | bytes 221216 | tf_op jit(solution)/shard_map/ppermute | solution.py:526
  10.8 1.1 %shard_map.98 = (bf16[9,48,128]{2,1,0:T(8,128)(2,1)S(1)}, bf16[2,5,48,384]{3,2,1,0:T(8,128)(2,1)S(1)}) custom-call(bf16[2,3,48,384]{3,2,1,0:T(8,128)(2,1)S(1)} %collective-permute-done.refs_0_.refs_4_, bf16[2,3,48,384]{3,2,1,0:T(8,128)(2,1)S(1)} %collective-permute-done.1.refs_1_.refs_5_, f32[384]{0:T(512)S(1)} %get-tuple-element.25.refs_1_.refs_2_, ...), custom_call_target="tpu_custom_call" | custom-call | flops 382205952 | bytes 4194304 | tf_op jit(solution)/shard_map/pallas_call | solution.py:59
  11.9 1.6 %collective-permute-start.4 = (bf16[9,48,128]{2,1,0:T(8,128)(2,1)S(1)}, bf16[9,48,128]{2,1,0:T(8,128)(2,1)S(1)}, u32[]{:S(2)}, u32[]{:S(2)}) collective-permute-start(bf16[9,48,128]{2,1,0:T(8,128)(2,1)S(1)} %get-tuple-element.30.refs_6_), channel_id=1, source_target_pairs={{0,64},{64,128},{128,192},{192,0},{1,65},{65,129},{129,193},{193,1... | collective-permute-start | bytes 331784 | tf_op jit(solution)/shard_map/ppermute | solution.py:517
  13.5 1.6 %shard_map.99 = (bf16[9,48,128]{2,1,0:T(8,128)(2,1)S(1)}, bf16[2,5,48,384]{3,2,1,0:T(8,128)(2,1)S(1)}) custom-call(bf16[2,3,48,384]{3,2,1,0:T(8,128)(2,1)S(1)} %collective-permute-done.refs_0_.refs_4_, bf16[2,3,48,384]{3,2,1,0:T(8,128)(2,1)S(1)} %collective-permute-done.1.refs_1_.refs_5_, f32[384]{0:T(512)S(1)} %get-tuple-element.25.refs_1_.refs_2_, ...), custom_call_target="tpu_custom_call" | custom-call | flops 764411904 | bytes 4194304 | tf_op jit(solution)/shard_map/pallas_call | solution.py:59
  15.1 1.6 %collective-permute-start.3 = (bf16[9,48,128]{2,1,0:T(8,128)(2,1)S(1)}, bf16[9,48,128]{2,1,0:T(8,128)(2,1)S(1)}, u32[]{:S(2)}, u32[]{:S(2)}) collective-permute-start(bf16[9,48,128]{2,1,0:T(8,128)(2,1)S(1)} %get-tuple-element.33), channel_id=1, source_target_pairs={{0,64},{64,128},{128,192},{192,0},{1,65},{65,129},{129,193},{193,1... | collective-permute-start | bytes 331784 | tf_op jit(solution)/shard_map/ppermute | solution.py:517
  16.7 1.2 %shard_map.100.refs_3_.refs_1_ = f32[288,192]{1,0:T(8,128)S(1)} custom-call(bf16[2,5,48,384]{3,2,1,0:T(8,128)(2,1)S(1)} %get-tuple-element.31.refs_0_.refs_1_, bf16[2,5,48,384]{3,2,1,0:T(8,128)(2,1)S(1)} %get-tuple-element.29.refs_5_.refs_1_, bf16[3,3,3,192,384]{4,3,2,1,0:T(8,128)(2,1)S(1)} %bitcast.7), custom_call_target="tpu_custom_call" | custom-call | flops 1048576 | bytes 4194304 | tf_op jit(solution)/shard_map/pallas_call | solution.py:59
  18.0 0.0 copy-start.1
  18.0 0.0 copy-start.5
  18.0 1.4 %shard_map.101.refs_6_.refs_0_ = f32[576,192]{1,0:T(8,128)S(1)} custom-call(bf16[2,8,48,384]{3,2,1,0:T(8,128)(2,1)S(1)} %get-tuple-element.26.refs_0_.refs_3_, bf16[2,5,48,384]{3,2,1,0:T(8,128)(2,1)S(1)} %get-tuple-element.31.refs_0_.refs_1_, bf16[3,3,3,192,384]{4,3,2,1,0:T(8,128)(2,1)S(1)} %bitcast.8, f32[288,192]{1,0:T(8,128)S(1)} %shard_map.100.refs_3_.refs_1_), custom_call_target="tpu_custom_call" | custom-call | flops 1048576 | bytes 4194304 | tf_op jit(solution)/shard_map/pallas_call | solution.py:59
  19.4 0.0 collective-permute-done.2.refs_2_.refs_1_
  19.4 0.0 collective-permute-done.4.refs_3_
  19.4 0.3 copy-done.1
  19.7 0.0 copy-done.5
  19.7 1.2 %shard_map.102 = (bf16[15,48,128]{2,1,0:T(8,128)(2,1)S(1)}, bf16[3,12,48,256]{3,2,1,0:T(8,128)(2,1)S(1)}) custom-call(f32[288,192]{1,0:T(8,128)S(1)} %shard_map.97.refs_5_.refs_0_, f32[288,192]{1,0:T(8,128)S(1)} %shard_map.100.refs_3_.refs_1_, bf16[2,9,48,128]{3,2,1,0:T(8,128)(2,1)S(1)} %collective-permute-done.2.refs_2_.refs_1_, ...), custom_call_target="tpu_custom_call" | custom-call | flops 318504960 | bytes 4194304 | tf_op jit(solution)/shard_map/pallas_call | solution.py:59
  21.0 0.0 copy-start.3
  21.0 1.5 %collective-permute-start.6 = (bf16[15,48,128]{2,1,0:T(8,128)(2,1)S(1)}, bf16[15,48,128]{2,1,0:T(8,128)(2,1)S(1)}, u32[]{:S(2)}, u32[]{:S(2)}) collective-permute-start(bf16[15,48,128]{2,1,0:T(8,128)(2,1)S(1)} %get-tuple-element.38), channel_id=1, source_target_pairs={{0,64},{64,128},{128,192},{192,0},{1,65},{65,129},{129,193},{193,1... | collective-permute-start | bytes 552968 | tf_op jit(solution)/shard_map/ppermute | solution.py:517
  22.5 0.0 collective-permute-done.3.refs_2_
  22.5 1.7 %shard_map.103 = (bf16[15,48,128]{2,1,0:T(8,128)(2,1)S(1)}, bf16[3,12,48,256]{3,2,1,0:T(8,128)(2,1)S(1)}) custom-call(f32[576,192]{1,0:T(8,128)S(1)} %shard_map.101.refs_6_.refs_0_, bf16[2,9,48,128]{3,2,1,0:T(8,128)(2,1)S(1)} %collective-permute-done.2.refs_2_.refs_1_, bf16[9,48,128]{2,1,0:T(8,128)(2,1)S(1)} %collective-permute-done.3.refs_2_, ...), custom_call_target="tpu_custom_call" | custom-call | flops 637009920 | bytes 4194304 | tf_op jit(solution)/shard_map/pallas_call | solution.py:59
  24.3 0.3 collective-permute-start.5
  24.6 0.0 copy-done.3
  24.6 0.0 copy-start.4
  24.6 0.0 copy-start.2
  24.6 2.1 %shard_map.104.refs_1_.refs_0_ = f32[2,480,192]{2,1,0:T(8,128)S(1)} custom-call(bf16[3,12,48,256]{3,2,1,0:T(8,128)(2,1)S(1)} %get-tuple-element.35.refs_0_, bf16[3,12,48,256]{3,2,1,0:T(8,128)(2,1)S(1)} %get-tuple-element.34.refs_5_.refs_1_, bf16[3,3,3,192,192]{4,3,2,1,0:T(8,128)(2,1)S(1)} %copy-done.1, ...), custom_call_target="tpu_custom_call" | custom-call | flops 955514880 | bytes 4194304 | tf_op jit(solution)/shard_map/pallas_call | solution.py:59
  26.7 2.4 %collective-permute-done.6.refs_1_ = bf16[15,48,128]{2,1,0:T(8,128)(2,1)S(1)} collective-permute-done((bf16[15,48,128]{2,1,0:T(8,128)(2,1)S(1)}, bf16[15,48,128]{2,1,0:T(8,128)(2,1)S(1)}, u32[]{:S(2)}, u32[]{:S(2)}) %collective-permute-start.6) | collective-permute-done | bytes 184352 | tf_op jit(solution)/shard_map/ppermute | solution.py:517
  29.0 0.0 copy-done.4
  29.0 0.4 %shard_map.107 = (bf16[8,48,192]{2,1,0:T(8,128)(2,1)S(1)}, bf16[15,48,128]{2,1,0:T(8,128)(2,1)S(1)}) custom-call(f32[2,480,192]{2,1,0:T(8,128)S(1)} %shard_map.104.refs_1_.refs_0_, bf16[15,48,128]{2,1,0:T(8,128)(2,1)S(1)} %collective-permute-done.6.refs_1_, f32[192]{0:T(256)S(1)} %copy-done.4), custom_call_target="tpu_custom_call" | custom-call | flops 16777216 | bytes 4194304 | tf_op jit(solution)/shard_map/pallas_call | solution.py:59
  29.5 0.1 collective-permute-start.8
  29.6 0.0 copy-done.2
  29.6 0.3 shard_map.105.refs_3_.refs_2_.refs_1_
  29.9 2.8 %collective-permute-done.5.refs_1_ = bf16[15,48,128]{2,1,0:T(8,128)(2,1)S(1)} collective-permute-done((bf16[15,48,128]{2,1,0:T(8,128)(2,1)S(1)}, bf16[15,48,128]{2,1,0:T(8,128)(2,1)S(1)}, u32[]{:S(2)}, u32[]{:S(2)}) %collective-permute-start.5) | collective-permute-done | bytes 184352 | tf_op jit(solution)/shard_map/ppermute | solution.py:517
  32.7 0.4 %shard_map.106 = (bf16[8,48,192]{2,1,0:T(8,128)(2,1)S(1)}, bf16[15,48,128]{2,1,0:T(8,128)(2,1)S(1)}) custom-call(f32[2,480,192]{2,1,0:T(8,128)S(1)} %shard_map.104.refs_1_.refs_0_, bf16[15,48,128]{2,1,0:T(8,128)(2,1)S(1)} %collective-permute-done.5.refs_1_, f32[192]{0:T(256)S(1)} %copy-done.4, bf16[3,4,768,192]{3,2,1,0:T(8,128)(2,1)S(1)} %shard_map.105.refs_3_.refs_2_.refs_1_), custom_call_target="tpu_custom_call" | custom-call | flops 16777216 | bytes 4194304 | tf_op jit(solution)/shard_map/pallas_call | solution.py:59
  33.1 1.5 %collective-permute-start.7 = (bf16[15,48,128]{2,1,0:T(8,128)(2,1)S(1)}, bf16[15,48,128]{2,1,0:T(8,128)(2,1)S(1)}, u32[]{:S(2)}, u32[]{:S(2)}) collective-permute-start(bf16[15,48,128]{2,1,0:T(8,128)(2,1)S(1)} %get-tuple-element.37.refs_0_), channel_id=1, source_target_pairs={{0,64},{64,128},{128,192},{1,65},{65,129},{129,193},{2,66},{66,130... | collective-permute-start | bytes 552968 | tf_op jit(solution)/shard_map/ppermute | solution.py:512
  34.6 2.7 %shard_map.108 = (f32[2,4,384,192]{3,2,1,0:T(8,128)S(1)}, bf16[2,8,48,192]{3,2,1,0:T(8,128)(2,1)}) custom-call(bf16[15,48,128]{2,1,0:T(8,128)(2,1)S(1)} %get-tuple-element.37.refs_0_, bf16[15,48,128]{2,1,0:T(8,128)(2,1)S(1)} %get-tuple-element.39.refs_1_, bf16[3,4,768,192]{3,2,1,0:T(8,128)(2,1)S(1)} %shard_map.105.refs_3_.refs_2_.refs_1_, ...), custom_call_target="tpu_custom_call" | custom-call | flops 764411904 | bytes 4194304 | tf_op jit(solution)/shard_map/pallas_call | solution.py:59
  37.3 0.0 collective-permute-done.8.refs_0_
  37.3 1.7 %shard_map.109 = (bf16[2,8,2,96,192]{4,3,2,1,0:T(8,128)(2,1)}, f32[4,384,192]{2,1,0:T(8,128)S(1)}) custom-call(bf16[15,48,128]{2,1,0:T(8,128)(2,1)S(1)} %collective-permute-done.8.refs_0_, bf16[3,4,768,192]{3,2,1,0:T(8,128)(2,1)S(1)} %shard_map.105.refs_3_.refs_2_.refs_1_, f32[2,4,384,192]{3,2,1,0:T(8,128)S(1)} %get-tuple-element.43.refs_2_), custom_call_target="tpu_custom_call" | custom-call | flops 509607936 | bytes 4194304 | tf_op jit(solution)/shard_map/pallas_call | solution.py:59
  39.0 0.0 collective-permute-done.7.refs_0_
  39.0 1.7 %shard_map.110 = bf16[2,8,2,96,192]{4,3,2,1,0:T(8,128)(2,1)} custom-call(bf16[15,48,128]{2,1,0:T(8,128)(2,1)S(1)} %collective-permute-done.7.refs_0_, bf16[3,4,768,192]{3,2,1,0:T(8,128)(2,1)S(1)} %shard_map.105.refs_3_.refs_2_.refs_1_, f32[4,384,192]{2,1,0:T(8,128)S(1)} %get-tuple-element.44.refs_2_, ...), custom_call_target="tpu_custom_call", output_to_operand_aliasing={{}: (3, {})} | custom-call | flops 254803968 | bytes 4194304 | tf_op jit(solution)/shard_map/pallas_call | solution.py:59
Async XLA Ops:
  0.6 3.8 %copy-start = (bf16[3,3,3,384,192]{3,4,2,1,0:T(8,128)(2,1)S(1)}, bf16[3,3,3,384,192]{3,4,2,1,0:T(8,128)(2,1)}, u32[]{:S(2)}) copy-start(bf16[3,3,3,384,192]{3,4,2,1,0:T(8,128)(2,1)} %param.10) | copy-start | bytes 11943940
  1.9 7.9 %collective-permute-start = (bf16[2,3,48,384]{3,2,1,0:T(8,128)(2,1)S(1)}, bf16[2,3,48,384]{3,2,1,0:T(8,128)(2,1)S(1)}, u32[]{:S(2)}, u32[]{:S(2)}) collective-permute-start(bf16[2,3,48,384]{3,2,1,0:T(8,128)(2,1)S(1)} %get-tuple-element.27), channel_id=1, source_target_pairs={{0,1},{2,3},{4,5},{6,7},{8,9},{10,11},{12,13},{14,15},{16,17},{18,... | collective-permute-start | bytes 663560 | tf_op jit(solution)/shard_map/ppermute | solution.py:526
  2.0 8.8 %collective-permute-start.1 = (bf16[2,3,48,384]{3,2,1,0:T(8,128)(2,1)S(1)}, bf16[2,3,48,384]{3,2,1,0:T(8,128)(2,1)S(1)}, u32[]{:S(2)}, u32[]{:S(2)}) collective-permute-start(bf16[2,3,48,384]{3,2,1,0:T(8,128)(2,1)S(1)} %get-tuple-element.28), channel_id=1, source_target_pairs={{1,2},{3,4},{5,6},{7,8},{9,10},{11,12},{13,14},{15,16},{17,18},{19... | collective-permute-start | bytes 663560 | tf_op jit(solution)/shard_map/ppermute | solution.py:526
  6.9 12.5 %collective-permute-start.2 = (bf16[2,9,48,128]{3,2,1,0:T(8,128)(2,1)S(1)}, bf16[2,9,48,128]{3,2,1,0:T(8,128)(2,1)S(1)}, u32[]{:S(2)}, u32[]{:S(2)}) collective-permute-start(bf16[2,9,48,128]{3,2,1,0:T(8,128)(2,1)S(1)} %get-tuple-element.32), channel_id=1, source_target_pairs={{0,64},{64,128},{128,192},{192,0},{1,65},{65,129},{129,193},{193,1... | collective-permute-start | bytes 663560 | tf_op jit(solution)/shard_map/ppermute | solution.py:517
  11.9 7.5 %collective-permute-start.4 = (bf16[9,48,128]{2,1,0:T(8,128)(2,1)S(1)}, bf16[9,48,128]{2,1,0:T(8,128)(2,1)S(1)}, u32[]{:S(2)}, u32[]{:S(2)}) collective-permute-start(bf16[9,48,128]{2,1,0:T(8,128)(2,1)S(1)} %get-tuple-element.30.refs_6_), channel_id=1, source_target_pairs={{0,64},{64,128},{128,192},{192,0},{1,65},{65,129},{129,193},{193,1... | collective-permute-start | bytes 331784 | tf_op jit(solution)/shard_map/ppermute | solution.py:517
  15.1 7.4 %collective-permute-start.3 = (bf16[9,48,128]{2,1,0:T(8,128)(2,1)S(1)}, bf16[9,48,128]{2,1,0:T(8,128)(2,1)S(1)}, u32[]{:S(2)}, u32[]{:S(2)}) collective-permute-start(bf16[9,48,128]{2,1,0:T(8,128)(2,1)S(1)} %get-tuple-element.33), channel_id=1, source_target_pairs={{0,64},{64,128},{128,192},{192,0},{1,65},{65,129},{129,193},{193,1... | collective-permute-start | bytes 331784 | tf_op jit(solution)/shard_map/ppermute | solution.py:517
  18.0 1.8 %copy-start.1 = (bf16[3,3,3,192,192]{4,3,2,1,0:T(8,128)(2,1)S(1)}, bf16[3,3,3,192,192]{4,3,2,1,0:T(8,128)(2,1)}, u32[]{:S(2)}) copy-start(bf16[3,3,3,192,192]{4,3,2,1,0:T(8,128)(2,1)} %refs_2_.3) | copy-start | bytes 5971972
  18.0 1.7 %copy-start.5 = (f32[192]{0:T(256)S(1)}, f32[192]{0:T(256)}, u32[]{:S(2)}) copy-start(f32[192]{0:T(256)} %refs_3_.1) | copy-start | bytes 2308
  21.0 3.6 %copy-start.3 = (bf16[384,192]{0,1:T(8,128)(2,1)S(1)}, bf16[384,192]{0,1:T(8,128)(2,1)}, u32[]{:S(2)}) copy-start(bf16[384,192]{0,1:T(8,128)(2,1)} %param.13) | copy-start | bytes 442372
  21.0 8.0 %collective-permute-start.6 = (bf16[15,48,128]{2,1,0:T(8,128)(2,1)S(1)}, bf16[15,48,128]{2,1,0:T(8,128)(2,1)S(1)}, u32[]{:S(2)}, u32[]{:S(2)}) collective-permute-start(bf16[15,48,128]{2,1,0:T(8,128)(2,1)S(1)} %get-tuple-element.38), channel_id=1, source_target_pairs={{0,64},{64,128},{128,192},{192,0},{1,65},{65,129},{129,193},{193,1... | collective-permute-start | bytes 552968 | tf_op jit(solution)/shard_map/ppermute | solution.py:517
  24.3 8.4 %collective-permute-start.5 = (bf16[15,48,128]{2,1,0:T(8,128)(2,1)S(1)}, bf16[15,48,128]{2,1,0:T(8,128)(2,1)S(1)}, u32[]{:S(2)}, u32[]{:S(2)}) collective-permute-start(bf16[15,48,128]{2,1,0:T(8,128)(2,1)S(1)} %get-tuple-element.36), channel_id=1, source_target_pairs={{0,64},{64,128},{128,192},{192,0},{1,65},{65,129},{129,193},{193,1... | collective-permute-start | bytes 552968 | tf_op jit(solution)/shard_map/ppermute | solution.py:517
  24.6 4.5 %copy-start.4 = (f32[192]{0:T(256)S(1)}, f32[192]{0:T(256)}, u32[]{:S(2)}) copy-start(f32[192]{0:T(256)} %refs_2_.5) | copy-start | bytes 2308
  24.6 5.0 %copy-start.2 = (bf16[3,3,3,192,192]{4,3,2,1,0:T(8,128)(2,1)S(1)}, bf16[3,3,3,192,192]{4,3,2,1,0:T(8,128)(2,1)}, u32[]{:S(2)}) copy-start(bf16[3,3,3,192,192]{4,3,2,1,0:T(8,128)(2,1)} %refs_0_.3) | copy-start | bytes 5971972
  29.5 7.8 %collective-permute-start.8 = (bf16[15,48,128]{2,1,0:T(8,128)(2,1)S(1)}, bf16[15,48,128]{2,1,0:T(8,128)(2,1)S(1)}, u32[]{:S(2)}, u32[]{:S(2)}) collective-permute-start(bf16[15,48,128]{2,1,0:T(8,128)(2,1)S(1)} %get-tuple-element.39.refs_1_), channel_id=1, source_target_pairs={{0,64},{64,128},{128,192},{192,0},{1,65},{65,129},{129,193},{193,1... | collective-permute-start | bytes 552968 | tf_op jit(solution)/shard_map/ppermute | solution.py:517
  33.1 5.9 %collective-permute-start.7 = (bf16[15,48,128]{2,1,0:T(8,128)(2,1)S(1)}, bf16[15,48,128]{2,1,0:T(8,128)(2,1)S(1)}, u32[]{:S(2)}, u32[]{:S(2)}) collective-permute-start(bf16[15,48,128]{2,1,0:T(8,128)(2,1)S(1)} %get-tuple-element.37.refs_0_), channel_id=1, source_target_pairs={{0,64},{64,128},{128,192},{1,65},{65,129},{129,193},{2,66},{66,130... | collective-permute-start | bytes 552968 | tf_op jit(solution)/shard_map/ppermute | solution.py:512

commit v7 on v6

--- a/solution.py
+++ b/solution.py
@@ -447,21 +447,27 @@
     return dot(jnp.concatenate(lanes, axis=1), jnp.concatenate(weights, axis=0))
 
 
-def third_own_kernel(place, early, late, kernel, early_out, late_out, own, block_out, fields, sems):
+def third_late_own_kernel(place, packed, kernel, own, field):
+    rows = packed.shape[0] * 2 // 3 - 2
+    fill_field(field, *packed_parts(packed))
+    for i in range(2):
+        for j in range(2):
+            own[2 * i + j] = phase([(field, 2)], kernel, i, j, rows)
+
+
+def third_own_kernel(place, packed, late, kernel, early_out, late_out, own, block_out, field, sems):
     copies = [
         pltpu.make_async_copy(block, block_out.at[frame], sems.at[frame])
         for frame, block in enumerate((early_out, late_out))
     ]
     for copy in copies:
         copy.start()
-    for frame, packed in enumerate((early, late)):
-        fill_field(fields.at[frame], *packed_parts(packed))
+    fill_field(field, *packed_parts(packed))
     rows = early_out.shape[0]
-    for out in (1, 0):
-        terms = [(fields.at[frame], a) for frame, a in OWN[out]]
-        for i in range(2):
-            for j in range(2):
-                own[out, 2 * i + j] = phase(terms, kernel, i, j, rows)
+    for i in range(2):
+        for j in range(2):
+            own[1, 2 * i + j] = late[2 * i + j] + phase([(field, 1)], kernel, i, j, rows)
+            own[0, 2 * i + j] = phase([(field, 2)], kernel, i, j, rows)
     for copy in copies:
         copy.wait()
 
@@ -604,7 +610,9 @@
         after=(partial,),
     )
     early_edges = onward(partial)
-    (late_rest,) = call(late_edge_own_kernel, (edge_sums,), [], 1 << 20, (early, late, across))
+    (late_rest,) = call(
+        late_edge_own_kernel, (edge_sums,), [], flops1, (early, late, across), after=(kernel_second,)
+    )
     second_work = [pltpu.VMEM((pixels1, 192), BF16)] + work(wide1, 192)
     packed2 = shape((wide2 * 3 // 2, width, 128), BF16)
     field = shape((3, wide1, width, 256), BF16)
@@ -653,21 +661,28 @@
         (own, before_late, gain_third),
     )
     before_late = onward(late)
+    (late_own,) = call(
+        third_late_own_kernel,
+        (shape((4, pixels, 192), F32),),
+        [pltpu.VMEM((3, wide2, width, 256), BF16)],
+        flops3,
+        (late, mixed),
+    )
     early_out, early = call(
         early_third_kernel,
         (block, packed2),
         third_work,
         1 << 24,
         (own, before_early, gain_third),
-        after=(mixed,),
+        after=(late_own,),
     )
     before_early = onward_open(early)
     own, block_out = call(
         third_own_kernel,
         (shape((2, 4, pixels, 192), F32), shape((2, rows, width, 192), BF16)),
-        [pltpu.VMEM((2, 3, wide2, width, 256), BF16), dma((2,))],
-        3 * flops3,
-        (early, late, mixed, early_out, late_out),
+        [pltpu.VMEM((3, wide2, width, 256), BF16), dma((2,))],
+        2 * flops3,
+        (early, late_own, mixed, early_out, late_out),
         out_hbm=(1,),
     )
     last_work = [

time: 41 us -> 41.2 us (level)
  the two profiles are of different devices: /device:TPU:128 before, /device:TPU:152 now
where the time goes in v7:
time: 41.2 us; the launch traced here: 41 us
  Pallas kernels  22.3 us (54%)
  starting transfers between devices  12.3 us (30%)
  waiting for transfers between devices  5.45 us (13%)
  between operations  0.95 us (2%)
    pallas_call x17, Pallas kernels, call(): pl.pallas_call(placed, out_shape=out_shape, in_specs=[far if i in hbm els...  22.3 us
    ppermute x6, starting transfers between devices, onward(): lax.ppermute(value, 'tm', [(i, (i + 1) % count) for i in range(count)])  8.52 us
    ppermute x1, waiting for transfers between devices, onward_open(): return lax.ppermute(value, 'tm', [(i, i + 1) for i in range(count - 1)])  2.87 us
    ppermute x2, starting transfers between devices, swap(): lax.ppermute(value, ('tm', 'rows'), pairs + [(b, a) for a, b in pairs] +...  2.5 us
    ppermute x2, waiting for transfers between devices, swap(): lax.ppermute(value, ('tm', 'rows'), pairs + [(b, a) for a, b in pairs] +...  2.31 us
    ppermute x1, starting transfers between devices, onward_open(): return lax.ppermute(value, 'tm', [(i, i + 1) for i in range(count - 1)])  1.29 us
  transfers between devices with their start and end apart: 9, of which 3 were waited for; matrix products, arithmetic and copies ran while one was open for 0% of the time, Pallas kernels for 47%

profile of v7, /device:TPU:152, one launch (start us, length us, event | category | flops | bytes accessed | tf_op | source)
XLA Modules:
  0.0 41.0 jit_solution(14135088131811907762)
XLA Ops:
  0.6 0.0 copy-start
  0.6 1.2 %shard_map.95 = (bf16[2,8,48,384]{3,2,1,0:T(8,128)(2,1)S(1)}, f32[384]{0:T(512)S(1)}, bf16[2,3,48,384]{3,2,1,0:T(8,128)(2,1)S(1)}, bf16[2,3,48,384]{3,2,1,0:T(8,128)(2,1)S(1)}) custom-call(bf16[2,8,48,384]{3,2,1,0:T(8,128)(2,1)} %refs_0_.2, f32[384]{0:T(512)} %refs_1_.1), custom_call_target="tpu_custom_call" | custom-call | flops 17179869184 | bytes 4194304 | tf_op jit(solution)/shard_map/pallas_call | solution.py:59
  1.9 0.1 collective-permute-start
  2.0 2.4 %collective-permute-start.1 = (bf16[2,3,48,384]{3,2,1,0:T(8,128)(2,1)S(1)}, bf16[2,3,48,384]{3,2,1,0:T(8,128)(2,1)S(1)}, u32[]{:S(2)}, u32[]{:S(2)}) collective-permute-start(bf16[2,3,48,384]{3,2,1,0:T(8,128)(2,1)S(1)} %get-tuple-element.28), channel_id=1, source_target_pairs={{1,2},{3,4},{5,6},{7,8},{9,10},{11,12},{13,14},{15,16},{17,18},{19... | collective-permute-start | bytes 663560 | tf_op jit(solution)/shard_map/ppermute | solution.py:532
  4.4 0.0 copy-done
  4.4 2.5 %shard_map.96 = (bf16[2,8,48,384]{3,2,1,0:T(8,128)(2,1)S(1)}, bf16[2,9,48,128]{3,2,1,0:T(8,128)(2,1)S(1)}) custom-call(bf16[2,8,48,384]{3,2,1,0:T(8,128)(2,1)S(1)} %get-tuple-element.24.refs_0_.refs_3_, f32[384]{0:T(512)S(1)} %get-tuple-element.25.refs_1_.refs_2_, bf16[3,3,3,192,384]{4,3,2,1,0:T(8,128)(2,1)S(1)} %bitcast.3), custom_call_target="tpu_custom_call" | custom-call | flops 1528823808 | bytes 4194304 | tf_op jit(solution)/shard_map/pallas_call | solution.py:59
  6.9 0.3 collective-permute-start.2
  7.2 1.2 %shard_map.97.refs_5_.refs_0_ = f32[288,192]{1,0:T(8,128)S(1)} custom-call(bf16[2,8,48,384]{3,2,1,0:T(8,128)(2,1)S(1)} %get-tuple-element.26.refs_0_.refs_3_, bf16[3,3,3,192,384]{4,3,2,1,0:T(8,128)(2,1)S(1)} %bitcast.4), custom_call_target="tpu_custom_call" | custom-call | flops 764411904 | bytes 4194304 | tf_op jit(solution)/shard_map/pallas_call | solution.py:59
  8.4 0.0 collective-permute-done.refs_0_.refs_4_
  8.5 2.3 %collective-permute-done.1.refs_1_.refs_5_ = bf16[2,3,48,384]{3,2,1,0:T(8,128)(2,1)S(1)} collective-permute-done((bf16[2,3,48,384]{3,2,1,0:T(8,128)(2,1)S(1)}, bf16[2,3,48,384]{3,2,1,0:T(8,128)(2,1)S(1)}, u32[]{:S(2)}, u32[]{:S(2)}) %collective-permute-start.1) | collective-permute-done | bytes 221216 | tf_op jit(solution)/shard_map/ppermute | solution.py:532
  10.8 1.1 %shard_map.98 = (bf16[9,48,128]{2,1,0:T(8,128)(2,1)S(1)}, bf16[2,5,48,384]{3,2,1,0:T(8,128)(2,1)S(1)}) custom-call(bf16[2,3,48,384]{3,2,1,0:T(8,128)(2,1)S(1)} %collective-permute-done.refs_0_.refs_4_, bf16[2,3,48,384]{3,2,1,0:T(8,128)(2,1)S(1)} %collective-permute-done.1.refs_1_.refs_5_, f32[384]{0:T(512)S(1)} %get-tuple-element.25.refs_1_.refs_2_, ...), custom_call_target="tpu_custom_call" | custom-call | flops 382205952 | bytes 4194304 | tf_op jit(solution)/shard_map/pallas_call | solution.py:59
  11.9 0.3 collective-permute-start.4
  12.2 0.0 copy-start.1
  12.2 1.6 %shard_map.99 = (bf16[9,48,128]{2,1,0:T(8,128)(2,1)S(1)}, bf16[2,5,48,384]{3,2,1,0:T(8,128)(2,1)S(1)}) custom-call(bf16[2,3,48,384]{3,2,1,0:T(8,128)(2,1)S(1)} %collective-permute-done.refs_0_.refs_4_, bf16[2,3,48,384]{3,2,1,0:T(8,128)(2,1)S(1)} %collective-permute-done.1.refs_1_.refs_5_, f32[384]{0:T(512)S(1)} %get-tuple-element.25.refs_1_.refs_2_, ...), custom_call_target="tpu_custom_call" | custom-call | flops 764411904 | bytes 4194304 | tf_op jit(solution)/shard_map/pallas_call | solution.py:59
  13.7 1.6 %collective-permute-start.3 = (bf16[9,48,128]{2,1,0:T(8,128)(2,1)S(1)}, bf16[9,48,128]{2,1,0:T(8,128)(2,1)S(1)}, u32[]{:S(2)}, u32[]{:S(2)}) collective-permute-start(bf16[9,48,128]{2,1,0:T(8,128)(2,1)S(1)} %get-tuple-element.33), channel_id=1, source_target_pairs={{0,64},{64,128},{128,192},{192,0},{1,65},{65,129},{129,193},{193,1... | collective-permute-start | bytes 331784 | tf_op jit(solution)/shard_map/ppermute | solution.py:523
  15.3 0.0 copy-done.1
  15.3 1.2 %shard_map.100.refs_3_.refs_1_ = f32[288,192]{1,0:T(8,128)S(1)} custom-call(bf16[2,5,48,384]{3,2,1,0:T(8,128)(2,1)S(1)} %get-tuple-element.31.refs_0_.refs_1_, bf16[2,5,48,384]{3,2,1,0:T(8,128)(2,1)S(1)} %get-tuple-element.29.refs_5_.refs_1_, bf16[3,3,3,192,384]{4,3,2,1,0:T(8,128)(2,1)S(1)} %bitcast.7, bf16[3,3,3,192,192]{4,3,2,1,0:T(8,128)(2,1)S(1)} %copy-done.1), custom_call_target="tpu_custom_call" | custom-call | flops 764411904 | bytes 4194304 | tf_op jit(solution)/shard_map/pallas_call | solution.py:59
  16.6 0.0 copy-start.5
  16.6 1.4 %shard_map.101.refs_6_.refs_0_ = f32[576,192]{1,0:T(8,128)S(1)} custom-call(bf16[2,8,48,384]{3,2,1,0:T(8,128)(2,1)S(1)} %get-tuple-element.26.refs_0_.refs_3_, bf16[2,5,48,384]{3,2,1,0:T(8,128)(2,1)S(1)} %get-tuple-element.31.refs_0_.refs_1_, bf16[3,3,3,192,384]{4,3,2,1,0:T(8,128)(2,1)S(1)} %bitcast.8, f32[288,192]{1,0:T(8,128)S(1)} %shard_map.100.refs_3_.refs_1_), custom_call_target="tpu_custom_call" | custom-call | flops 1048576 | bytes 4194304 | tf_op jit(solution)/shard_map/pallas_call | solution.py:59
  18.0 0.0 collective-permute-done.2.refs_2_.refs_1_
  18.0 0.0 collective-permute-done.4.refs_3_
  18.0 0.0 copy-done.5
  18.0 1.2 %shard_map.102 = (bf16[15,48,128]{2,1,0:T(8,128)(2,1)S(1)}, bf16[3,12,48,256]{3,2,1,0:T(8,128)(2,1)S(1)}) custom-call(f32[288,192]{1,0:T(8,128)S(1)} %shard_map.97.refs_5_.refs_0_, f32[288,192]{1,0:T(8,128)S(1)} %shard_map.100.refs_3_.refs_1_, bf16[2,9,48,128]{3,2,1,0:T(8,128)(2,1)S(1)} %collective-permute-done.2.refs_2_.refs_1_, ...), custom_call_target="tpu_custom_call" | custom-call | flops 318504960 | bytes 4194304 | tf_op jit(solution)/shard_map/pallas_call | solution.py:59
  19.3 0.0 copy-start.3
  19.3 1.8 %collective-permute-start.6 = (bf16[15,48,128]{2,1,0:T(8,128)(2,1)S(1)}, bf16[15,48,128]{2,1,0:T(8,128)(2,1)S(1)}, u32[]{:S(2)}, u32[]{:S(2)}) collective-permute-start(bf16[15,48,128]{2,1,0:T(8,128)(2,1)S(1)} %get-tuple-element.37), channel_id=1, source_target_pairs={{0,64},{64,128},{128,192},{192,0},{1,65},{65,129},{129,193},{193,1... | collective-permute-start | bytes 552968 | tf_op jit(solution)/shard_map/ppermute | solution.py:523
  21.1 0.0 collective-permute-done.3.refs_2_
  21.1 1.7 %shard_map.103 = (bf16[15,48,128]{2,1,0:T(8,128)(2,1)S(1)}, bf16[3,12,48,256]{3,2,1,0:T(8,128)(2,1)S(1)}) custom-call(f32[576,192]{1,0:T(8,128)S(1)} %shard_map.101.refs_6_.refs_0_, bf16[2,9,48,128]{3,2,1,0:T(8,128)(2,1)S(1)} %collective-permute-done.2.refs_2_.refs_1_, bf16[9,48,128]{2,1,0:T(8,128)(2,1)S(1)} %collective-permute-done.3.refs_2_, ...), custom_call_target="tpu_custom_call" | custom-call | flops 637009920 | bytes 4194304 | tf_op jit(solution)/shard_map/pallas_call | solution.py:59
  22.8 1.3 %collective-permute-start.5 = (bf16[15,48,128]{2,1,0:T(8,128)(2,1)S(1)}, bf16[15,48,128]{2,1,0:T(8,128)(2,1)S(1)}, u32[]{:S(2)}, u32[]{:S(2)}) collective-permute-start(bf16[15,48,128]{2,1,0:T(8,128)(2,1)S(1)} %get-tuple-element.36), channel_id=1, source_target_pairs={{0,64},{64,128},{128,192},{192,0},{1,65},{65,129},{129,193},{193,1... | collective-permute-start | bytes 552968 | tf_op jit(solution)/shard_map/ppermute | solution.py:523
  24.2 0.0 copy-done.3
  24.2 0.0 copy-start.4
  24.2 0.0 copy-start.2
  24.2 2.1 %shard_map.104.refs_0_.refs_1_ = f32[2,480,192]{2,1,0:T(8,128)S(1)} custom-call(bf16[3,12,48,256]{3,2,1,0:T(8,128)(2,1)S(1)} %get-tuple-element.35.refs_0_, bf16[3,12,48,256]{3,2,1,0:T(8,128)(2,1)S(1)} %get-tuple-element.34.refs_5_.refs_1_, bf16[3,3,3,192,192]{4,3,2,1,0:T(8,128)(2,1)S(1)} %copy-done.1, ...), custom_call_target="tpu_custom_call" | custom-call | flops 955514880 | bytes 4194304 | tf_op jit(solution)/shard_map/pallas_call | solution.py:59
  26.3 0.3 collective-permute-done.6.refs_1_
  26.6 0.0 copy-done.4
  26.6 0.4 %shard_map.105 = (bf16[8,48,192]{2,1,0:T(8,128)(2,1)S(1)}, bf16[15,48,128]{2,1,0:T(8,128)(2,1)S(1)}) custom-call(f32[2,480,192]{2,1,0:T(8,128)S(1)} %shard_map.104.refs_0_.refs_1_, bf16[15,48,128]{2,1,0:T(8,128)(2,1)S(1)} %collective-permute-done.6.refs_1_, f32[192]{0:T(256)S(1)} %copy-done.4), custom_call_target="tpu_custom_call" | custom-call | flops 16777216 | bytes 4194304 | tf_op jit(solution)/shard_map/pallas_call | solution.py:59
  27.0 3.1 %collective-permute-start.8 = (bf16[15,48,128]{2,1,0:T(8,128)(2,1)S(1)}, bf16[15,48,128]{2,1,0:T(8,128)(2,1)S(1)}, u32[]{:S(2)}, u32[]{:S(2)}) collective-permute-start(bf16[15,48,128]{2,1,0:T(8,128)(2,1)S(1)} %get-tuple-element.38.refs_0_), channel_id=1, source_target_pairs={{0,64},{64,128},{128,192},{192,0},{1,65},{65,129},{129,193},{193,1... | collective-permute-start | bytes 552968 | tf_op jit(solution)/shard_map/ppermute | solution.py:523
  30.1 0.0 copy-done.2
  30.1 0.3 shard_map.106.refs_1_.refs_2_
  30.5 0.9 %shard_map.107.refs_3_.refs_1_ = f32[4,384,192]{2,1,0:T(8,128)S(1)} custom-call(bf16[15,48,128]{2,1,0:T(8,128)(2,1)S(1)} %get-tuple-element.38.refs_0_, bf16[3,4,768,192]{3,2,1,0:T(8,128)(2,1)S(1)} %shard_map.106.refs_1_.refs_2_), custom_call_target="tpu_custom_call" | custom-call | flops 254803968 | bytes 4194304 | tf_op jit(solution)/shard_map/pallas_call | solution.py:59
  31.3 0.0 collective-permute-done.5.refs_1_
  31.3 0.4 %shard_map.108 = (bf16[8,48,192]{2,1,0:T(8,128)(2,1)S(1)}, bf16[15,48,128]{2,1,0:T(8,128)(2,1)S(1)}) custom-call(f32[2,480,192]{2,1,0:T(8,128)S(1)} %shard_map.104.refs_0_.refs_1_, bf16[15,48,128]{2,1,0:T(8,128)(2,1)S(1)} %collective-permute-done.5.refs_1_, f32[192]{0:T(256)S(1)} %copy-done.4, f32[4,384,192]{2,1,0:T(8,128)S(1)} %shard_map.107.refs_3_.refs_1_), custom_call_target="tpu_custom_call" | custom-call | flops 16777216 | bytes 4194304 | tf_op jit(solution)/shard_map/pallas_call | solution.py:59
  31.8 1.3 %collective-permute-start.7 = (bf16[15,48,128]{2,1,0:T(8,128)(2,1)S(1)}, bf16[15,48,128]{2,1,0:T(8,128)(2,1)S(1)}, u32[]{:S(2)}, u32[]{:S(2)}) collective-permute-start(bf16[15,48,128]{2,1,0:T(8,128)(2,1)S(1)} %get-tuple-element.39.refs_0_), channel_id=1, source_target_pairs={{0,64},{64,128},{128,192},{1,65},{65,129},{129,193},{2,66},{66,130... | collective-permute-start | bytes 552968 | tf_op jit(solution)/shard_map/ppermute | solution.py:518
  33.0 1.5 %shard_map.109 = (f32[2,4,384,192]{3,2,1,0:T(8,128)S(1)}, bf16[2,8,48,192]{3,2,1,0:T(8,128)(2,1)}) custom-call(bf16[15,48,128]{2,1,0:T(8,128)(2,1)S(1)} %get-tuple-element.39.refs_0_, f32[4,384,192]{2,1,0:T(8,128)S(1)} %shard_map.107.refs_3_.refs_1_, bf16[3,4,768,192]{3,2,1,0:T(8,128)(2,1)S(1)} %shard_map.106.refs_1_.refs_2_, ...), custom_call_target="tpu_custom_call" | custom-call | flops 509607936 | bytes 4194304 | tf_op jit(solution)/shard_map/pallas_call | solution.py:59
  34.6 0.0 collective-permute-done.8.refs_0_
  34.6 1.7 %shard_map.110 = (bf16[2,8,2,96,192]{4,3,2,1,0:T(8,128)(2,1)}, f32[4,384,192]{2,1,0:T(8,128)S(1)}) custom-call(bf16[15,48,128]{2,1,0:T(8,128)(2,1)S(1)} %collective-permute-done.8.refs_0_, bf16[3,4,768,192]{3,2,1,0:T(8,128)(2,1)S(1)} %shard_map.106.refs_1_.refs_2_, f32[2,4,384,192]{3,2,1,0:T(8,128)S(1)} %get-tuple-element.43.refs_2_), custom_call_target="tpu_custom_call" | custom-call | flops 509607936 | bytes 4194304 | tf_op jit(solution)/shard_map/pallas_call | solution.py:59
  36.3 2.9 %collective-permute-done.7.refs_0_ = bf16[15,48,128]{2,1,0:T(8,128)(2,1)S(1)} collective-permute-done((bf16[15,48,128]{2,1,0:T(8,128)(2,1)S(1)}, bf16[15,48,128]{2,1,0:T(8,128)(2,1)S(1)}, u32[]{:S(2)}, u32[]{:S(2)}) %collective-permute-start.7) | collective-permute-done | bytes 184352 | tf_op jit(solution)/shard_map/ppermute | solution.py:518
  39.2 1.7 %shard_map.111 = bf16[2,8,2,96,192]{4,3,2,1,0:T(8,128)(2,1)} custom-call(bf16[15,48,128]{2,1,0:T(8,128)(2,1)S(1)} %collective-permute-done.7.refs_0_, bf16[3,4,768,192]{3,2,1,0:T(8,128)(2,1)S(1)} %shard_map.106.refs_1_.refs_2_, f32[4,384,192]{2,1,0:T(8,128)S(1)} %get-tuple-element.44.refs_2_, ...), custom_call_target="tpu_custom_call", output_to_operand_aliasing={{}: (3, {})} | custom-call | flops 254803968 | bytes 4194304 | tf_op jit(solution)/shard_map/pallas_call | solution.py:59
Async XLA Ops:
  0.6 3.8 %copy-start = (bf16[3,3,3,384,192]{3,4,2,1,0:T(8,128)(2,1)S(1)}, bf16[3,3,3,384,192]{3,4,2,1,0:T(8,128)(2,1)}, u32[]{:S(2)}) copy-start(bf16[3,3,3,384,192]{3,4,2,1,0:T(8,128)(2,1)} %param.10) | copy-start | bytes 11943940
  1.9 6.5 %collective-permute-start = (bf16[2,3,48,384]{3,2,1,0:T(8,128)(2,1)S(1)}, bf16[2,3,48,384]{3,2,1,0:T(8,128)(2,1)S(1)}, u32[]{:S(2)}, u32[]{:S(2)}) collective-permute-start(bf16[2,3,48,384]{3,2,1,0:T(8,128)(2,1)S(1)} %get-tuple-element.27), channel_id=1, source_target_pairs={{0,1},{2,3},{4,5},{6,7},{8,9},{10,11},{12,13},{14,15},{16,17},{18,... | collective-permute-start | bytes 663560 | tf_op jit(solution)/shard_map/ppermute | solution.py:532
  2.0 8.8 %collective-permute-start.1 = (bf16[2,3,48,384]{3,2,1,0:T(8,128)(2,1)S(1)}, bf16[2,3,48,384]{3,2,1,0:T(8,128)(2,1)S(1)}, u32[]{:S(2)}, u32[]{:S(2)}) collective-permute-start(bf16[2,3,48,384]{3,2,1,0:T(8,128)(2,1)S(1)} %get-tuple-element.28), channel_id=1, source_target_pairs={{1,2},{3,4},{5,6},{7,8},{9,10},{11,12},{13,14},{15,16},{17,18},{19... | collective-permute-start | bytes 663560 | tf_op jit(solution)/shard_map/ppermute | solution.py:532
  6.9 11.1 %collective-permute-start.2 = (bf16[2,9,48,128]{3,2,1,0:T(8,128)(2,1)S(1)}, bf16[2,9,48,128]{3,2,1,0:T(8,128)(2,1)S(1)}, u32[]{:S(2)}, u32[]{:S(2)}) collective-permute-start(bf16[2,9,48,128]{3,2,1,0:T(8,128)(2,1)S(1)} %get-tuple-element.32), channel_id=1, source_target_pairs={{0,64},{64,128},{128,192},{192,0},{1,65},{65,129},{129,193},{193,1... | collective-permute-start | bytes 663560 | tf_op jit(solution)/shard_map/ppermute | solution.py:523
  11.9 6.1 %collective-permute-start.4 = (bf16[9,48,128]{2,1,0:T(8,128)(2,1)S(1)}, bf16[9,48,128]{2,1,0:T(8,128)(2,1)S(1)}, u32[]{:S(2)}, u32[]{:S(2)}) collective-permute-start(bf16[9,48,128]{2,1,0:T(8,128)(2,1)S(1)} %get-tuple-element.30.refs_6_), channel_id=1, source_target_pairs={{0,64},{64,128},{128,192},{192,0},{1,65},{65,129},{129,193},{193,1... | collective-permute-start | bytes 331784 | tf_op jit(solution)/shard_map/ppermute | solution.py:523
  12.2 3.2 %copy-start.1 = (bf16[3,3,3,192,192]{4,3,2,1,0:T(8,128)(2,1)S(1)}, bf16[3,3,3,192,192]{4,3,2,1,0:T(8,128)(2,1)}, u32[]{:S(2)}) copy-start(bf16[3,3,3,192,192]{4,3,2,1,0:T(8,128)(2,1)} %refs_2_.3) | copy-start | bytes 5971972
  13.7 7.4 %collective-permute-start.3 = (bf16[9,48,128]{2,1,0:T(8,128)(2,1)S(1)}, bf16[9,48,128]{2,1,0:T(8,128)(2,1)S(1)}, u32[]{:S(2)}, u32[]{:S(2)}) collective-permute-start(bf16[9,48,128]{2,1,0:T(8,128)(2,1)S(1)} %get-tuple-element.33), channel_id=1, source_target_pairs={{0,64},{64,128},{128,192},{192,0},{1,65},{65,129},{129,193},{193,1... | collective-permute-start | bytes 331784 | tf_op jit(solution)/shard_map/ppermute | solution.py:523
  16.6 1.4 %copy-start.5 = (f32[192]{0:T(256)S(1)}, f32[192]{0:T(256)}, u32[]{:S(2)}) copy-start(f32[192]{0:T(256)} %refs_3_.3) | copy-start | bytes 2308
  19.3 4.9 %copy-start.3 = (bf16[384,192]{0,1:T(8,128)(2,1)S(1)}, bf16[384,192]{0,1:T(8,128)(2,1)}, u32[]{:S(2)}) copy-start(bf16[384,192]{0,1:T(8,128)(2,1)} %param.13) | copy-start | bytes 442372
  19.3 7.3 %collective-permute-start.6 = (bf16[15,48,128]{2,1,0:T(8,128)(2,1)S(1)}, bf16[15,48,128]{2,1,0:T(8,128)(2,1)S(1)}, u32[]{:S(2)}, u32[]{:S(2)}) collective-permute-start(bf16[15,48,128]{2,1,0:T(8,128)(2,1)S(1)} %get-tuple-element.37), channel_id=1, source_target_pairs={{0,64},{64,128},{128,192},{192,0},{1,65},{65,129},{129,193},{193,1... | collective-permute-start | bytes 552968 | tf_op jit(solution)/shard_map/ppermute | solution.py:523
  22.8 8.5 %collective-permute-start.5 = (bf16[15,48,128]{2,1,0:T(8,128)(2,1)S(1)}, bf16[15,48,128]{2,1,0:T(8,128)(2,1)S(1)}, u32[]{:S(2)}, u32[]{:S(2)}) collective-permute-start(bf16[15,48,128]{2,1,0:T(8,128)(2,1)S(1)} %get-tuple-element.36), channel_id=1, source_target_pairs={{0,64},{64,128},{128,192},{192,0},{1,65},{65,129},{129,193},{193,1... | collective-permute-start | bytes 552968 | tf_op jit(solution)/shard_map/ppermute | solution.py:523
  24.2 2.4 %copy-start.4 = (f32[192]{0:T(256)S(1)}, f32[192]{0:T(256)}, u32[]{:S(2)}) copy-start(f32[192]{0:T(256)} %refs_2_.5) | copy-start | bytes 2308
  24.2 5.9 %copy-start.2 = (bf16[3,3,3,192,192]{4,3,2,1,0:T(8,128)(2,1)S(1)}, bf16[3,3,3,192,192]{4,3,2,1,0:T(8,128)(2,1)}, u32[]{:S(2)}) copy-start(bf16[3,3,3,192,192]{4,3,2,1,0:T(8,128)(2,1)} %refs_0_.3) | copy-start | bytes 5971972
  27.0 7.6 %collective-permute-start.8 = (bf16[15,48,128]{2,1,0:T(8,128)(2,1)S(1)}, bf16[15,48,128]{2,1,0:T(8,128)(2,1)S(1)}, u32[]{:S(2)}, u32[]{:S(2)}) collective-permute-start(bf16[15,48,128]{2,1,0:T(8,128)(2,1)S(1)} %get-tuple-element.38.refs_0_), channel_id=1, source_target_pairs={{0,64},{64,128},{128,192},{192,0},{1,65},{65,129},{129,193},{193,1... | collective-permute-start | bytes 552968 | tf_op jit(solution)/shard_map/ppermute | solution.py:523
  31.8 7.4 %collective-permute-start.7 = (bf16[15,48,128]{2,1,0:T(8,128)(2,1)S(1)}, bf16[15,48,128]{2,1,0:T(8,128)(2,1)S(1)}, u32[]{:S(2)}, u32[]{:S(2)}) collective-permute-start(bf16[15,48,128]{2,1,0:T(8,128)(2,1)S(1)} %get-tuple-element.39.refs_0_), channel_id=1, source_target_pairs={{0,64},{64,128},{128,192},{1,65},{65,129},{129,193},{2,66},{66,130... | collective-permute-start | bytes 552968 | tf_op jit(solution)/shard_map/ppermute | solution.py:518

commit v8 on v7

--- a/solution.py
+++ b/solution.py
@@ -218,16 +218,18 @@
     copies[2].wait()
 
 
-def inner_kernel(place, held, gain, weights, active, packed, squares, scale, sums):
-    frames, rows, width, channels = held.shape
-
+def active_kernel(place, held, gain, active, squares, scale):
     def put(frame, row, lanes, value):
         active[frame, row, :, lanes] = value
 
-    for frame in range(frames):
+    for frame in range(held.shape[0]):
         activate_rows(
             [held.at[frame]], gain, squares, scale, lambda _, *args, frame=frame: put(frame, *args)
         )
+
+
+def inner_kernel(place, active, weights, packed, sums):
+    frames, rows, width, channels = active.shape
     count = rows - 2
     for out, taps in ((1, ((1, 0),)), (0, ((0, 0), (1, 1)))):
         terms = [(windows(active.at[frame], count), a) for frame, a in taps]
@@ -573,15 +575,15 @@
     inner_rows = rows - 2
     inner_pixels = inner_rows * width
     across = jnp.swapaxes(kernel_first, 3, 4)
-    active, inner = call(
+    (active,) = call(
+        active_kernel, (shape(latents.shape, BF16),), work(rows, channels), 1 << 20, (held, gain_first)
+    )
+    (inner,) = call(
         inner_kernel,
-        (
-            shape(latents.shape, BF16),
-            shape((2, inner_rows * 3 // 2, width, 128), BF16),
-        ),
-        work(rows, channels) + [pltpu.VMEM((2, inner_pixels, 192), F32)],
+        (shape((2, inner_rows * 3 // 2, width, 128), BF16),),
+        [pltpu.VMEM((2, inner_pixels, 192), F32)],
         2 * flops1,
-        (held, gain_first, across),
+        (active, across),
     )
     inner = onward(inner)
     (late_inner,) = call(

time: 41.2 us -> 41.2 us (level)
    pallas_call x17 -> x18, Pallas kernels: 22.3 us -> 22.3 us  [call(): pl.pallas_call(placed, out_shape=out_shape, in_specs=[far if i in hbm els...]
where the time goes in v8:
time: 41.2 us; the launch traced here: 41.1 us
  Pallas kernels  22.3 us (54%)
  starting transfers between devices  12.3 us (30%)
  waiting for transfers between devices  5.44 us (13%)
  between operations  0.97 us (2%)
    pallas_call x18, Pallas kernels, call(): pl.pallas_call(placed, out_shape=out_shape, in_specs=[far if i in hbm els...  22.3 us
    ppermute x6, starting transfers between devices, onward(): lax.ppermute(value, 'tm', [(i, (i + 1) % count) for i in range(count)])  8.54 us
    ppermute x1, waiting for transfers between devices, onward_open(): return lax.ppermute(value, 'tm', [(i, i + 1) for i in range(count - 1)])  2.88 us
    ppermute x2, starting transfers between devices, swap(): lax.ppermute(value, ('tm', 'rows'), pairs + [(b, a) for a, b in pairs] +...  2.5 us
    ppermute x2, waiting for transfers between devices, swap(): lax.ppermute(value, ('tm', 'rows'), pairs + [(b, a) for a, b in pairs] +...  2.32 us
    ppermute x1, starting transfers between devices, onward_open(): return lax.ppermute(value, 'tm', [(i, i + 1) for i in range(count - 1)])  1.29 us
  transfers between devices with their start and end apart: 9, of which 3 were waited for; matrix products, arithmetic and copies ran while one was open for 0% of the time, Pallas kernels for 47%

profile of v8, /device:TPU:152, one launch (start us, length us, event | category | flops | bytes accessed | tf_op | source)
XLA Modules:
  0.0 41.1 jit_solution(4980399439176586069)
XLA Ops:
  0.6 0.0 copy-start
  0.6 1.2 %shard_map.95 = (bf16[2,8,48,384]{3,2,1,0:T(8,128)(2,1)S(1)}, f32[384]{0:T(512)S(1)}, bf16[2,3,48,384]{3,2,1,0:T(8,128)(2,1)S(1)}, bf16[2,3,48,384]{3,2,1,0:T(8,128)(2,1)S(1)}) custom-call(bf16[2,8,48,384]{3,2,1,0:T(8,128)(2,1)} %refs_0_.2, f32[384]{0:T(512)} %refs_1_.1), custom_call_target="tpu_custom_call" | custom-call | flops 17179869184 | bytes 4194304 | tf_op jit(solution)/shard_map/pallas_call | solution.py:59
  1.9 0.1 collective-permute-start
  2.0 2.4 %collective-permute-start.1 = (bf16[2,3,48,384]{3,2,1,0:T(8,128)(2,1)S(1)}, bf16[2,3,48,384]{3,2,1,0:T(8,128)(2,1)S(1)}, u32[]{:S(2)}, u32[]{:S(2)}) collective-permute-start(bf16[2,3,48,384]{3,2,1,0:T(8,128)(2,1)S(1)} %get-tuple-element.25), channel_id=1, source_target_pairs={{1,2},{3,4},{5,6},{7,8},{9,10},{11,12},{13,14},{15,16},{17,18},{19... | collective-permute-start | bytes 663560 | tf_op jit(solution)/shard_map/ppermute | solution.py:534
  4.4 0.6 %shard_map.96.refs_0_.refs_3_ = bf16[2,8,48,384]{3,2,1,0:T(8,128)(2,1)S(1)} custom-call(bf16[2,8,48,384]{3,2,1,0:T(8,128)(2,1)S(1)} %get-tuple-element.22.refs_0_.refs_3_, f32[384]{0:T(512)S(1)} %get-tuple-element.23.refs_1_.refs_2_), custom_call_target="tpu_custom_call" | custom-call | flops 1048576 | bytes 4194304 | tf_op jit(solution)/shard_map/pallas_call | solution.py:59
  5.0 0.0 copy-done
  5.0 1.9 %shard_map.102 = bf16[2,9,48,128]{3,2,1,0:T(8,128)(2,1)S(1)} custom-call(bf16[2,8,48,384]{3,2,1,0:T(8,128)(2,1)S(1)} %shard_map.96.refs_0_.refs_3_, bf16[3,3,3,192,384]{4,3,2,1,0:T(8,128)(2,1)S(1)} %bitcast.3), custom_call_target="tpu_custom_call" | custom-call | flops 1528823808 | bytes 4194304 | tf_op jit(solution)/shard_map/pallas_call | solution.py:59
  6.9 0.3 collective-permute-start.2
  7.2 1.2 %shard_map.97.refs_5_.refs_0_ = f32[288,192]{1,0:T(8,128)S(1)} custom-call(bf16[2,8,48,384]{3,2,1,0:T(8,128)(2,1)S(1)} %shard_map.96.refs_0_.refs_3_, bf16[3,3,3,192,384]{4,3,2,1,0:T(8,128)(2,1)S(1)} %bitcast.4), custom_call_target="tpu_custom_call" | custom-call | flops 764411904 | bytes 4194304 | tf_op jit(solution)/shard_map/pallas_call | solution.py:59
  8.4 0.0 collective-permute-done.refs_0_.refs_4_
  8.4 2.3 %collective-permute-done.1.refs_1_.refs_5_ = bf16[2,3,48,384]{3,2,1,0:T(8,128)(2,1)S(1)} collective-permute-done((bf16[2,3,48,384]{3,2,1,0:T(8,128)(2,1)S(1)}, bf16[2,3,48,384]{3,2,1,0:T(8,128)(2,1)S(1)}, u32[]{:S(2)}, u32[]{:S(2)}) %collective-permute-start.1) | collective-permute-done | bytes 221216 | tf_op jit(solution)/shard_map/ppermute | solution.py:534
  10.8 1.1 %shard_map.98 = (bf16[9,48,128]{2,1,0:T(8,128)(2,1)S(1)}, bf16[2,5,48,384]{3,2,1,0:T(8,128)(2,1)S(1)}) custom-call(bf16[2,3,48,384]{3,2,1,0:T(8,128)(2,1)S(1)} %collective-permute-done.refs_0_.refs_4_, bf16[2,3,48,384]{3,2,1,0:T(8,128)(2,1)S(1)} %collective-permute-done.1.refs_1_.refs_5_, f32[384]{0:T(512)S(1)} %get-tuple-element.23.refs_1_.refs_2_, ...), custom_call_target="tpu_custom_call" | custom-call | flops 382205952 | bytes 4194304 | tf_op jit(solution)/shard_map/pallas_call | solution.py:59
  11.9 0.3 collective-permute-start.4
  12.2 0.0 copy-start.1
  12.2 1.6 %shard_map.99 = (bf16[9,48,128]{2,1,0:T(8,128)(2,1)S(1)}, bf16[2,5,48,384]{3,2,1,0:T(8,128)(2,1)S(1)}) custom-call(bf16[2,3,48,384]{3,2,1,0:T(8,128)(2,1)S(1)} %collective-permute-done.refs_0_.refs_4_, bf16[2,3,48,384]{3,2,1,0:T(8,128)(2,1)S(1)} %collective-permute-done.1.refs_1_.refs_5_, f32[384]{0:T(512)S(1)} %get-tuple-element.23.refs_1_.refs_2_, ...), custom_call_target="tpu_custom_call" | custom-call | flops 764411904 | bytes 4194304 | tf_op jit(solution)/shard_map/pallas_call | solution.py:59
  13.7 1.6 %collective-permute-start.3 = (bf16[9,48,128]{2,1,0:T(8,128)(2,1)S(1)}, bf16[9,48,128]{2,1,0:T(8,128)(2,1)S(1)}, u32[]{:S(2)}, u32[]{:S(2)}) collective-permute-start(bf16[9,48,128]{2,1,0:T(8,128)(2,1)S(1)} %get-tuple-element.29), channel_id=1, source_target_pairs={{0,64},{64,128},{128,192},{192,0},{1,65},{65,129},{129,193},{193,1... | collective-permute-start | bytes 331784 | tf_op jit(solution)/shard_map/ppermute | solution.py:525
  15.4 0.0 copy-done.1
  15.4 1.2 %shard_map.100.refs_3_.refs_1_ = f32[288,192]{1,0:T(8,128)S(1)} custom-call(bf16[2,5,48,384]{3,2,1,0:T(8,128)(2,1)S(1)} %get-tuple-element.28.refs_0_.refs_1_, bf16[2,5,48,384]{3,2,1,0:T(8,128)(2,1)S(1)} %get-tuple-element.26.refs_5_.refs_1_, bf16[3,3,3,192,384]{4,3,2,1,0:T(8,128)(2,1)S(1)} %bitcast.7, bf16[3,3,3,192,192]{4,3,2,1,0:T(8,128)(2,1)S(1)} %copy-done.1), custom_call_target="tpu_custom_call" | custom-call | flops 764411904 | bytes 4194304 | tf_op jit(solution)/shard_map/pallas_call | solution.py:59
  16.6 0.0 copy-start.5
  16.6 1.4 %shard_map.101.refs_6_.refs_0_ = f32[576,192]{1,0:T(8,128)S(1)} custom-call(bf16[2,8,48,384]{3,2,1,0:T(8,128)(2,1)S(1)} %shard_map.96.refs_0_.refs_3_, bf16[2,5,48,384]{3,2,1,0:T(8,128)(2,1)S(1)} %get-tuple-element.28.refs_0_.refs_1_, bf16[3,3,3,192,384]{4,3,2,1,0:T(8,128)(2,1)S(1)} %bitcast.8, f32[288,192]{1,0:T(8,128)S(1)} %shard_map.100.refs_3_.refs_1_), custom_call_target="tpu_custom_call" | custom-call | flops 1048576 | bytes 4194304 | tf_op jit(solution)/shard_map/pallas_call | solution.py:59
  18.0 0.0 collective-permute-done.2.refs_2_.refs_1_
  18.0 0.0 collective-permute-done.4.refs_3_
  18.0 0.0 copy-done.5
  18.0 1.2 %shard_map.103 = (bf16[15,48,128]{2,1,0:T(8,128)(2,1)S(1)}, bf16[3,12,48,256]{3,2,1,0:T(8,128)(2,1)S(1)}) custom-call(f32[288,192]{1,0:T(8,128)S(1)} %shard_map.97.refs_5_.refs_0_, f32[288,192]{1,0:T(8,128)S(1)} %shard_map.100.refs_3_.refs_1_, bf16[2,9,48,128]{3,2,1,0:T(8,128)(2,1)S(1)} %collective-permute-done.2.refs_2_.refs_1_, ...), custom_call_target="tpu_custom_call" | custom-call | flops 318504960 | bytes 4194304 | tf_op jit(solution)/shard_map/pallas_call | solution.py:59
  19.3 0.0 copy-start.3
  19.3 1.8 %collective-permute-start.6 = (bf16[15,48,128]{2,1,0:T(8,128)(2,1)S(1)}, bf16[15,48,128]{2,1,0:T(8,128)(2,1)S(1)}, u32[]{:S(2)}, u32[]{:S(2)}) collective-permute-start(bf16[15,48,128]{2,1,0:T(8,128)(2,1)S(1)} %get-tuple-element.33), channel_id=1, source_target_pairs={{0,64},{64,128},{128,192},{192,0},{1,65},{65,129},{129,193},{193,1... | collective-permute-start | bytes 552968 | tf_op jit(solution)/shard_map/ppermute | solution.py:525
  21.1 0.0 collective-permute-done.3.refs_2_
  21.1 1.7 %shard_map.104 = (bf16[15,48,128]{2,1,0:T(8,128)(2,1)S(1)}, bf16[3,12,48,256]{3,2,1,0:T(8,128)(2,1)S(1)}) custom-call(f32[576,192]{1,0:T(8,128)S(1)} %shard_map.101.refs_6_.refs_0_, bf16[2,9,48,128]{3,2,1,0:T(8,128)(2,1)S(1)} %collective-permute-done.2.refs_2_.refs_1_, bf16[9,48,128]{2,1,0:T(8,128)(2,1)S(1)} %collective-permute-done.3.refs_2_, ...), custom_call_target="tpu_custom_call" | custom-call | flops 637009920 | bytes 4194304 | tf_op jit(solution)/shard_map/pallas_call | solution.py:59
  22.8 1.3 %collective-permute-start.5 = (bf16[15,48,128]{2,1,0:T(8,128)(2,1)S(1)}, bf16[15,48,128]{2,1,0:T(8,128)(2,1)S(1)}, u32[]{:S(2)}, u32[]{:S(2)}) collective-permute-start(bf16[15,48,128]{2,1,0:T(8,128)(2,1)S(1)} %get-tuple-element.32), channel_id=1, source_target_pairs={{0,64},{64,128},{128,192},{192,0},{1,65},{65,129},{129,193},{193,1... | collective-permute-start | bytes 552968 | tf_op jit(solution)/shard_map/ppermute | solution.py:525
  24.2 0.0 copy-done.3
  24.2 0.0 copy-start.4
  24.2 0.0 copy-start.2
  24.2 2.1 %shard_map.105.refs_0_.refs_1_ = f32[2,480,192]{2,1,0:T(8,128)S(1)} custom-call(bf16[3,12,48,256]{3,2,1,0:T(8,128)(2,1)S(1)} %get-tuple-element.31.refs_0_, bf16[3,12,48,256]{3,2,1,0:T(8,128)(2,1)S(1)} %get-tuple-element.30.refs_5_.refs_1_, bf16[3,3,3,192,192]{4,3,2,1,0:T(8,128)(2,1)S(1)} %copy-done.1, ...), custom_call_target="tpu_custom_call" | custom-call | flops 955514880 | bytes 4194304 | tf_op jit(solution)/shard_map/pallas_call | solution.py:59
  26.3 0.2 collective-permute-done.6.refs_1_
  26.5 0.0 copy-done.4
  26.5 0.4 %shard_map.106 = (bf16[8,48,192]{2,1,0:T(8,128)(2,1)S(1)}, bf16[15,48,128]{2,1,0:T(8,128)(2,1)S(1)}) custom-call(f32[2,480,192]{2,1,0:T(8,128)S(1)} %shard_map.105.refs_0_.refs_1_, bf16[15,48,128]{2,1,0:T(8,128)(2,1)S(1)} %collective-permute-done.6.refs_1_, f32[192]{0:T(256)S(1)} %copy-done.4), custom_call_target="tpu_custom_call" | custom-call | flops 16777216 | bytes 4194304 | tf_op jit(solution)/shard_map/pallas_call | solution.py:59
  27.0 3.2 %collective-permute-start.8 = (bf16[15,48,128]{2,1,0:T(8,128)(2,1)S(1)}, bf16[15,48,128]{2,1,0:T(8,128)(2,1)S(1)}, u32[]{:S(2)}, u32[]{:S(2)}) collective-permute-start(bf16[15,48,128]{2,1,0:T(8,128)(2,1)S(1)} %get-tuple-element.34.refs_0_), channel_id=1, source_target_pairs={{0,64},{64,128},{128,192},{192,0},{1,65},{65,129},{129,193},{193,1... | collective-permute-start | bytes 552968 | tf_op jit(solution)/shard_map/ppermute | solution.py:525
  30.1 0.0 copy-done.2
  30.1 0.3 shard_map.107.refs_1_.refs_2_
  30.5 0.8 %shard_map.108.refs_3_.refs_1_ = f32[4,384,192]{2,1,0:T(8,128)S(1)} custom-call(bf16[15,48,128]{2,1,0:T(8,128)(2,1)S(1)} %get-tuple-element.34.refs_0_, bf16[3,4,768,192]{3,2,1,0:T(8,128)(2,1)S(1)} %shard_map.107.refs_1_.refs_2_), custom_call_target="tpu_custom_call" | custom-call | flops 254803968 | bytes 4194304 | tf_op jit(solution)/shard_map/pallas_call | solution.py:59
  31.3 0.0 collective-permute-done.5.refs_1_
  31.3 0.4 %shard_map.109 = (bf16[8,48,192]{2,1,0:T(8,128)(2,1)S(1)}, bf16[15,48,128]{2,1,0:T(8,128)(2,1)S(1)}) custom-call(f32[2,480,192]{2,1,0:T(8,128)S(1)} %shard_map.105.refs_0_.refs_1_, bf16[15,48,128]{2,1,0:T(8,128)(2,1)S(1)} %collective-permute-done.5.refs_1_, f32[192]{0:T(256)S(1)} %copy-done.4, f32[4,384,192]{2,1,0:T(8,128)S(1)} %shard_map.108.refs_3_.refs_1_), custom_call_target="tpu_custom_call" | custom-call | flops 16777216 | bytes 4194304 | tf_op jit(solution)/shard_map/pallas_call | solution.py:59
  31.8 1.3 %collective-permute-start.7 = (bf16[15,48,128]{2,1,0:T(8,128)(2,1)S(1)}, bf16[15,48,128]{2,1,0:T(8,128)(2,1)S(1)}, u32[]{:S(2)}, u32[]{:S(2)}) collective-permute-start(bf16[15,48,128]{2,1,0:T(8,128)(2,1)S(1)} %get-tuple-element.35.refs_0_), channel_id=1, source_target_pairs={{0,64},{64,128},{128,192},{1,65},{65,129},{129,193},{2,66},{66,130... | collective-permute-start | bytes 552968 | tf_op jit(solution)/shard_map/ppermute | solution.py:520
  33.1 1.5 %shard_map.110 = (f32[2,4,384,192]{3,2,1,0:T(8,128)S(1)}, bf16[2,8,48,192]{3,2,1,0:T(8,128)(2,1)}) custom-call(bf16[15,48,128]{2,1,0:T(8,128)(2,1)S(1)} %get-tuple-element.35.refs_0_, f32[4,384,192]{2,1,0:T(8,128)S(1)} %shard_map.108.refs_3_.refs_1_, bf16[3,4,768,192]{3,2,1,0:T(8,128)(2,1)S(1)} %shard_map.107.refs_1_.refs_2_, ...), custom_call_target="tpu_custom_call" | custom-call | flops 509607936 | bytes 4194304 | tf_op jit(solution)/shard_map/pallas_call | solution.py:59
  34.6 0.0 collective-permute-done.8.refs_0_
  34.6 1.7 %shard_map.111 = (bf16[2,8,2,96,192]{4,3,2,1,0:T(8,128)(2,1)}, f32[4,384,192]{2,1,0:T(8,128)S(1)}) custom-call(bf16[15,48,128]{2,1,0:T(8,128)(2,1)S(1)} %collective-permute-done.8.refs_0_, bf16[3,4,768,192]{3,2,1,0:T(8,128)(2,1)S(1)} %shard_map.107.refs_1_.refs_2_, f32[2,4,384,192]{3,2,1,0:T(8,128)S(1)} %get-tuple-element.39.refs_2_), custom_call_target="tpu_custom_call" | custom-call | flops 509607936 | bytes 4194304 | tf_op jit(solution)/shard_map/pallas_call | solution.py:59
  36.3 2.9 %collective-permute-done.7.refs_0_ = bf16[15,48,128]{2,1,0:T(8,128)(2,1)S(1)} collective-permute-done((bf16[15,48,128]{2,1,0:T(8,128)(2,1)S(1)}, bf16[15,48,128]{2,1,0:T(8,128)(2,1)S(1)}, u32[]{:S(2)}, u32[]{:S(2)}) %collective-permute-start.7) | collective-permute-done | bytes 184352 | tf_op jit(solution)/shard_map/ppermute | solution.py:520
  39.2 1.7 %shard_map.112 = bf16[2,8,2,96,192]{4,3,2,1,0:T(8,128)(2,1)} custom-call(bf16[15,48,128]{2,1,0:T(8,128)(2,1)S(1)} %collective-permute-done.7.refs_0_, bf16[3,4,768,192]{3,2,1,0:T(8,128)(2,1)S(1)} %shard_map.107.refs_1_.refs_2_, f32[4,384,192]{2,1,0:T(8,128)S(1)} %get-tuple-element.40.refs_2_, ...), custom_call_target="tpu_custom_call", output_to_operand_aliasing={{}: (3, {})} | custom-call | flops 254803968 | bytes 4194304 | tf_op jit(solution)/shard_map/pallas_call | solution.py:59
Async XLA Ops:
  0.6 4.4 %copy-start = (bf16[3,3,3,384,192]{3,4,2,1,0:T(8,128)(2,1)S(1)}, bf16[3,3,3,384,192]{3,4,2,1,0:T(8,128)(2,1)}, u32[]{:S(2)}) copy-start(bf16[3,3,3,384,192]{3,4,2,1,0:T(8,128)(2,1)} %param.10) | copy-start | bytes 11943940
  1.9 6.5 %collective-permute-start = (bf16[2,3,48,384]{3,2,1,0:T(8,128)(2,1)S(1)}, bf16[2,3,48,384]{3,2,1,0:T(8,128)(2,1)S(1)}, u32[]{:S(2)}, u32[]{:S(2)}) collective-permute-start(bf16[2,3,48,384]{3,2,1,0:T(8,128)(2,1)S(1)} %get-tuple-element.24), channel_id=1, source_target_pairs={{0,1},{2,3},{4,5},{6,7},{8,9},{10,11},{12,13},{14,15},{16,17},{18,... | collective-permute-start | bytes 663560 | tf_op jit(solution)/shard_map/ppermute | solution.py:534
  2.0 8.8 %collective-permute-start.1 = (bf16[2,3,48,384]{3,2,1,0:T(8,128)(2,1)S(1)}, bf16[2,3,48,384]{3,2,1,0:T(8,128)(2,1)S(1)}, u32[]{:S(2)}, u32[]{:S(2)}) collective-permute-start(bf16[2,3,48,384]{3,2,1,0:T(8,128)(2,1)S(1)} %get-tuple-element.25), channel_id=1, source_target_pairs={{1,2},{3,4},{5,6},{7,8},{9,10},{11,12},{13,14},{15,16},{17,18},{19... | collective-permute-start | bytes 663560 | tf_op jit(solution)/shard_map/ppermute | solution.py:534
  6.9 11.1 %collective-permute-start.2 = (bf16[2,9,48,128]{3,2,1,0:T(8,128)(2,1)S(1)}, bf16[2,9,48,128]{3,2,1,0:T(8,128)(2,1)S(1)}, u32[]{:S(2)}, u32[]{:S(2)}) collective-permute-start(bf16[2,9,48,128]{3,2,1,0:T(8,128)(2,1)S(1)} %shard_map.102), channel_id=1, source_target_pairs={{0,64},{64,128},{128,192},{192,0},{1,65},{65,129},{129,193},{193,1... | collective-permute-start | bytes 663560 | tf_op jit(solution)/shard_map/ppermute | solution.py:525
  11.9 6.1 %collective-permute-start.4 = (bf16[9,48,128]{2,1,0:T(8,128)(2,1)S(1)}, bf16[9,48,128]{2,1,0:T(8,128)(2,1)S(1)}, u32[]{:S(2)}, u32[]{:S(2)}) collective-permute-start(bf16[9,48,128]{2,1,0:T(8,128)(2,1)S(1)} %get-tuple-element.27.refs_6_), channel_id=1, source_target_pairs={{0,64},{64,128},{128,192},{192,0},{1,65},{65,129},{129,193},{193,1... | collective-permute-start | bytes 331784 | tf_op jit(solution)/shard_map/ppermute | solution.py:525
  12.2 3.2 %copy-start.1 = (bf16[3,3,3,192,192]{4,3,2,1,0:T(8,128)(2,1)S(1)}, bf16[3,3,3,192,192]{4,3,2,1,0:T(8,128)(2,1)}, u32[]{:S(2)}) copy-start(bf16[3,3,3,192,192]{4,3,2,1,0:T(8,128)(2,1)} %refs_2_.3) | copy-start | bytes 5971972
  13.7 7.4 %collective-permute-start.3 = (bf16[9,48,128]{2,1,0:T(8,128)(2,1)S(1)}, bf16[9,48,128]{2,1,0:T(8,128)(2,1)S(1)}, u32[]{:S(2)}, u32[]{:S(2)}) collective-permute-start(bf16[9,48,128]{2,1,0:T(8,128)(2,1)S(1)} %get-tuple-element.29), channel_id=1, source_target_pairs={{0,64},{64,128},{128,192},{192,0},{1,65},{65,129},{129,193},{193,1... | collective-permute-start | bytes 331784 | tf_op jit(solution)/shard_map/ppermute | solution.py:525
  16.6 1.4 %copy-start.5 = (f32[192]{0:T(256)S(1)}, f32[192]{0:T(256)}, u32[]{:S(2)}) copy-start(f32[192]{0:T(256)} %refs_3_.3) | copy-start | bytes 2308
  19.3 4.9 %copy-start.3 = (bf16[384,192]{0,1:T(8,128)(2,1)S(1)}, bf16[384,192]{0,1:T(8,128)(2,1)}, u32[]{:S(2)}) copy-start(bf16[384,192]{0,1:T(8,128)(2,1)} %param.13) | copy-start | bytes 442372
  19.3 7.3 %collective-permute-start.6 = (bf16[15,48,128]{2,1,0:T(8,128)(2,1)S(1)}, bf16[15,48,128]{2,1,0:T(8,128)(2,1)S(1)}, u32[]{:S(2)}, u32[]{:S(2)}) collective-permute-start(bf16[15,48,128]{2,1,0:T(8,128)(2,1)S(1)} %get-tuple-element.33), channel_id=1, source_target_pairs={{0,64},{64,128},{128,192},{192,0},{1,65},{65,129},{129,193},{193,1... | collective-permute-start | bytes 552968 | tf_op jit(solution)/shard_map/ppermute | solution.py:525
  22.8 8.5 %collective-permute-start.5 = (bf16[15,48,128]{2,1,0:T(8,128)(2,1)S(1)}, bf16[15,48,128]{2,1,0:T(8,128)(2,1)S(1)}, u32[]{:S(2)}, u32[]{:S(2)}) collective-permute-start(bf16[15,48,128]{2,1,0:T(8,128)(2,1)S(1)} %get-tuple-element.32), channel_id=1, source_target_pairs={{0,64},{64,128},{128,192},{192,0},{1,65},{65,129},{129,193},{193,1... | collective-permute-start | bytes 552968 | tf_op jit(solution)/shard_map/ppermute | solution.py:525
  24.2 2.3 %copy-start.4 = (f32[192]{0:T(256)S(1)}, f32[192]{0:T(256)}, u32[]{:S(2)}) copy-start(f32[192]{0:T(256)} %refs_2_.5) | copy-start | bytes 2308
  24.2 5.9 %copy-start.2 = (bf16[3,3,3,192,192]{4,3,2,1,0:T(8,128)(2,1)S(1)}, bf16[3,3,3,192,192]{4,3,2,1,0:T(8,128)(2,1)}, u32[]{:S(2)}) copy-start(bf16[3,3,3,192,192]{4,3,2,1,0:T(8,128)(2,1)} %refs_0_.3) | copy-start | bytes 5971972
  27.0 7.6 %collective-permute-start.8 = (bf16[15,48,128]{2,1,0:T(8,128)(2,1)S(1)}, bf16[15,48,128]{2,1,0:T(8,128)(2,1)S(1)}, u32[]{:S(2)}, u32[]{:S(2)}) collective-permute-start(bf16[15,48,128]{2,1,0:T(8,128)(2,1)S(1)} %get-tuple-element.34.refs_0_), channel_id=1, source_target_pairs={{0,64},{64,128},{128,192},{192,0},{1,65},{65,129},{129,193},{193,1... | collective-permute-start | bytes 552968 | tf_op jit(solution)/shard_map/ppermute | solution.py:525
  31.8 7.4 %collective-permute-start.7 = (bf16[15,48,128]{2,1,0:T(8,128)(2,1)S(1)}, bf16[15,48,128]{2,1,0:T(8,128)(2,1)S(1)}, u32[]{:S(2)}, u32[]{:S(2)}) collective-permute-start(bf16[15,48,128]{2,1,0:T(8,128)(2,1)S(1)} %get-tuple-element.35.refs_0_), channel_id=1, source_target_pairs={{0,64},{64,128},{128,192},{1,65},{65,129},{129,193},{2,66},{66,130... | collective-permute-start | bytes 552968 | tf_op jit(solution)/shard_map/ppermute | solution.py:520

commit v9 on v8

--- a/solution.py
+++ b/solution.py
@@ -662,7 +662,7 @@
         1 << 24,
         (own, before_late, gain_third),
     )
-    before_late = onward(late)
+    before_late = onward_open(late)
     (late_own,) = call(
         third_late_own_kernel,
         (shape((4, pixels, 192), F32),),

time: 41.2 us -> 41.4 us (level)
  the two profiles are of different devices: /device:TPU:152 before, /device:TPU:128 now
where the time goes in v9:
time: 41.4 us; the launch traced here: 40.6 us
  Pallas kernels  22.3 us (54%)
  starting transfers between devices  13.8 us (33%)
  waiting for transfers between devices  3.41 us (8%)
  between operations  0.99 us (2%)
    pallas_call x18, Pallas kernels, call(): pl.pallas_call(placed, out_shape=out_shape, in_specs=[far if i in hbm els...  22.3 us
    ppermute x5, starting transfers between devices, onward(): lax.ppermute(value, 'tm', [(i, (i + 1) % count) for i in range(count)])  6.74 us
    ppermute x2, starting transfers between devices, onward_open(): return lax.ppermute(value, 'tm', [(i, i + 1) for i in range(count - 1)])  4.61 us
    ppermute x2, starting transfers between devices, swap(): lax.ppermute(value, ('tm', 'rows'), pairs + [(b, a) for a, b in pairs] +...  2.5 us
    ppermute x5, waiting for transfers between devices, onward(): lax.ppermute(value, 'tm', [(i, (i + 1) % count) for i in range(count)])  2.44 us
    ppermute x2, waiting for transfers between devices, swap(): lax.ppermute(value, ('tm', 'rows'), pairs + [(b, a) for a, b in pairs] +...  0.97 us
  transfers between devices with their start and end apart: 9, of which 2 were waited for; matrix products, arithmetic and copies ran while one was open for 0% of the time, Pallas kernels for 48%

profile of v9, /device:TPU:128, one launch (start us, length us, event | category | flops | bytes accessed | tf_op | source)
XLA Modules:
  0.0 40.6 jit_solution(16635468115425994013)
XLA Ops:
  0.6 0.0 copy-start
  0.6 1.2 %shard_map.95 = (bf16[2,8,48,384]{3,2,1,0:T(8,128)(2,1)S(1)}, f32[384]{0:T(512)S(1)}, bf16[2,3,48,384]{3,2,1,0:T(8,128)(2,1)S(1)}, bf16[2,3,48,384]{3,2,1,0:T(8,128)(2,1)S(1)}) custom-call(bf16[2,8,48,384]{3,2,1,0:T(8,128)(2,1)} %refs_0_.2, f32[384]{0:T(512)} %refs_1_.1), custom_call_target="tpu_custom_call" | custom-call | flops 17179869184 | bytes 4194304 | tf_op jit(solution)/shard_map/pallas_call | solution.py:59
  1.9 0.1 collective-permute-start
  2.0 2.4 %collective-permute-start.1 = (bf16[2,3,48,384]{3,2,1,0:T(8,128)(2,1)S(1)}, bf16[2,3,48,384]{3,2,1,0:T(8,128)(2,1)S(1)}, u32[]{:S(2)}, u32[]{:S(2)}) collective-permute-start(bf16[2,3,48,384]{3,2,1,0:T(8,128)(2,1)S(1)} %get-tuple-element.25), channel_id=1, source_target_pairs={{1,2},{3,4},{5,6},{7,8},{9,10},{11,12},{13,14},{15,16},{17,18},{19... | collective-permute-start | bytes 663560 | tf_op jit(solution)/shard_map/ppermute | solution.py:534
  4.4 0.6 %shard_map.96.refs_0_.refs_3_ = bf16[2,8,48,384]{3,2,1,0:T(8,128)(2,1)S(1)} custom-call(bf16[2,8,48,384]{3,2,1,0:T(8,128)(2,1)S(1)} %get-tuple-element.22.refs_0_.refs_3_, f32[384]{0:T(512)S(1)} %get-tuple-element.23.refs_1_.refs_2_), custom_call_target="tpu_custom_call" | custom-call | flops 1048576 | bytes 4194304 | tf_op jit(solution)/shard_map/pallas_call | solution.py:59
  5.0 0.0 copy-done
  5.0 1.9 %shard_map.102 = bf16[2,9,48,128]{3,2,1,0:T(8,128)(2,1)S(1)} custom-call(bf16[2,8,48,384]{3,2,1,0:T(8,128)(2,1)S(1)} %shard_map.96.refs_0_.refs_3_, bf16[3,3,3,192,384]{4,3,2,1,0:T(8,128)(2,1)S(1)} %bitcast.3), custom_call_target="tpu_custom_call" | custom-call | flops 1528823808 | bytes 4194304 | tf_op jit(solution)/shard_map/pallas_call | solution.py:59
  6.9 1.6 %collective-permute-start.2 = (bf16[2,9,48,128]{3,2,1,0:T(8,128)(2,1)S(1)}, bf16[2,9,48,128]{3,2,1,0:T(8,128)(2,1)S(1)}, u32[]{:S(2)}, u32[]{:S(2)}) collective-permute-start(bf16[2,9,48,128]{3,2,1,0:T(8,128)(2,1)S(1)} %shard_map.102), channel_id=1, source_target_pairs={{0,64},{64,128},{128,192},{192,0},{1,65},{65,129},{129,193},{193,1... | collective-permute-start | bytes 663560 | tf_op jit(solution)/shard_map/ppermute | solution.py:525
  8.6 1.2 %shard_map.97.refs_5_.refs_0_ = f32[288,192]{1,0:T(8,128)S(1)} custom-call(bf16[2,8,48,384]{3,2,1,0:T(8,128)(2,1)S(1)} %shard_map.96.refs_0_.refs_3_, bf16[3,3,3,192,384]{4,3,2,1,0:T(8,128)(2,1)S(1)} %bitcast.4), custom_call_target="tpu_custom_call" | custom-call | flops 764411904 | bytes 4194304 | tf_op jit(solution)/shard_map/pallas_call | solution.py:59
  9.8 0.0 collective-permute-done.refs_0_.refs_4_
  9.8 1.0 %collective-permute-done.1.refs_1_.refs_5_ = bf16[2,3,48,384]{3,2,1,0:T(8,128)(2,1)S(1)} collective-permute-done((bf16[2,3,48,384]{3,2,1,0:T(8,128)(2,1)S(1)}, bf16[2,3,48,384]{3,2,1,0:T(8,128)(2,1)S(1)}, u32[]{:S(2)}, u32[]{:S(2)}) %collective-permute-start.1) | collective-permute-done | bytes 221216 | tf_op jit(solution)/shard_map/ppermute | solution.py:534
  10.8 1.1 %shard_map.98 = (bf16[9,48,128]{2,1,0:T(8,128)(2,1)S(1)}, bf16[2,5,48,384]{3,2,1,0:T(8,128)(2,1)S(1)}) custom-call(bf16[2,3,48,384]{3,2,1,0:T(8,128)(2,1)S(1)} %collective-permute-done.refs_0_.refs_4_, bf16[2,3,48,384]{3,2,1,0:T(8,128)(2,1)S(1)} %collective-permute-done.1.refs_1_.refs_5_, f32[384]{0:T(512)S(1)} %get-tuple-element.23.refs_1_.refs_2_, ...), custom_call_target="tpu_custom_call" | custom-call | flops 382205952 | bytes 4194304 | tf_op jit(solution)/shard_map/pallas_call | solution.py:59
  11.9 1.6 %collective-permute-start.4 = (bf16[9,48,128]{2,1,0:T(8,128)(2,1)S(1)}, bf16[9,48,128]{2,1,0:T(8,128)(2,1)S(1)}, u32[]{:S(2)}, u32[]{:S(2)}) collective-permute-start(bf16[9,48,128]{2,1,0:T(8,128)(2,1)S(1)} %get-tuple-element.27.refs_6_), channel_id=1, source_target_pairs={{0,64},{64,128},{128,192},{192,0},{1,65},{65,129},{129,193},{193,1... | collective-permute-start | bytes 331784 | tf_op jit(solution)/shard_map/ppermute | solution.py:525
  13.5 0.0 copy-start.1
  13.5 1.6 %shard_map.99 = (bf16[9,48,128]{2,1,0:T(8,128)(2,1)S(1)}, bf16[2,5,48,384]{3,2,1,0:T(8,128)(2,1)S(1)}) custom-call(bf16[2,3,48,384]{3,2,1,0:T(8,128)(2,1)S(1)} %collective-permute-done.refs_0_.refs_4_, bf16[2,3,48,384]{3,2,1,0:T(8,128)(2,1)S(1)} %collective-permute-done.1.refs_1_.refs_5_, f32[384]{0:T(512)S(1)} %get-tuple-element.23.refs_1_.refs_2_, ...), custom_call_target="tpu_custom_call" | custom-call | flops 764411904 | bytes 4194304 | tf_op jit(solution)/shard_map/pallas_call | solution.py:59
  15.1 1.6 %collective-permute-start.3 = (bf16[9,48,128]{2,1,0:T(8,128)(2,1)S(1)}, bf16[9,48,128]{2,1,0:T(8,128)(2,1)S(1)}, u32[]{:S(2)}, u32[]{:S(2)}) collective-permute-start(bf16[9,48,128]{2,1,0:T(8,128)(2,1)S(1)} %get-tuple-element.29), channel_id=1, source_target_pairs={{0,64},{64,128},{128,192},{192,0},{1,65},{65,129},{129,193},{193,1... | collective-permute-start | bytes 331784 | tf_op jit(solution)/shard_map/ppermute | solution.py:525
  16.7 0.0 copy-done.1
  16.7 1.2 %shard_map.100.refs_3_.refs_1_ = f32[288,192]{1,0:T(8,128)S(1)} custom-call(bf16[2,5,48,384]{3,2,1,0:T(8,128)(2,1)S(1)} %get-tuple-element.28.refs_0_.refs_1_, bf16[2,5,48,384]{3,2,1,0:T(8,128)(2,1)S(1)} %get-tuple-element.26.refs_5_.refs_1_, bf16[3,3,3,192,384]{4,3,2,1,0:T(8,128)(2,1)S(1)} %bitcast.7, bf16[3,3,3,192,192]{4,3,2,1,0:T(8,128)(2,1)S(1)} %copy-done.1), custom_call_target="tpu_custom_call" | custom-call | flops 764411904 | bytes 4194304 | tf_op jit(solution)/shard_map/pallas_call | solution.py:59
  17.9 0.0 copy-start.5
  17.9 1.4 %shard_map.101.refs_6_.refs_0_ = f32[576,192]{1,0:T(8,128)S(1)} custom-call(bf16[2,8,48,384]{3,2,1,0:T(8,128)(2,1)S(1)} %shard_map.96.refs_0_.refs_3_, bf16[2,5,48,384]{3,2,1,0:T(8,128)(2,1)S(1)} %get-tuple-element.28.refs_0_.refs_1_, bf16[3,3,3,192,384]{4,3,2,1,0:T(8,128)(2,1)S(1)} %bitcast.8, f32[288,192]{1,0:T(8,128)S(1)} %shard_map.100.refs_3_.refs_1_), custom_call_target="tpu_custom_call" | custom-call | flops 1048576 | bytes 4194304 | tf_op jit(solution)/shard_map/pallas_call | solution.py:59
  19.3 0.0 collective-permute-done.2.refs_2_.refs_1_
  19.4 0.0 collective-permute-done.4.refs_3_
  19.4 0.0 copy-done.5
  19.4 1.2 %shard_map.103 = (bf16[15,48,128]{2,1,0:T(8,128)(2,1)S(1)}, bf16[3,12,48,256]{3,2,1,0:T(8,128)(2,1)S(1)}) custom-call(f32[288,192]{1,0:T(8,128)S(1)} %shard_map.97.refs_5_.refs_0_, f32[288,192]{1,0:T(8,128)S(1)} %shard_map.100.refs_3_.refs_1_, bf16[2,9,48,128]{3,2,1,0:T(8,128)(2,1)S(1)} %collective-permute-done.2.refs_2_.refs_1_, ...), custom_call_target="tpu_custom_call" | custom-call | flops 318504960 | bytes 4194304 | tf_op jit(solution)/shard_map/pallas_call | solution.py:59
  20.6 0.0 copy-start.3
  20.6 1.5 %collective-permute-start.6 = (bf16[15,48,128]{2,1,0:T(8,128)(2,1)S(1)}, bf16[15,48,128]{2,1,0:T(8,128)(2,1)S(1)}, u32[]{:S(2)}, u32[]{:S(2)}) collective-permute-start(bf16[15,48,128]{2,1,0:T(8,128)(2,1)S(1)} %get-tuple-element.33), channel_id=1, source_target_pairs={{0,64},{64,128},{128,192},{192,0},{1,65},{65,129},{129,193},{193,1... | collective-permute-start | bytes 552968 | tf_op jit(solution)/shard_map/ppermute | solution.py:525
  22.2 0.0 collective-permute-done.3.refs_2_
  22.2 1.7 %shard_map.104 = (bf16[15,48,128]{2,1,0:T(8,128)(2,1)S(1)}, bf16[3,12,48,256]{3,2,1,0:T(8,128)(2,1)S(1)}) custom-call(f32[576,192]{1,0:T(8,128)S(1)} %shard_map.101.refs_6_.refs_0_, bf16[2,9,48,128]{3,2,1,0:T(8,128)(2,1)S(1)} %collective-permute-done.2.refs_2_.refs_1_, bf16[9,48,128]{2,1,0:T(8,128)(2,1)S(1)} %collective-permute-done.3.refs_2_, ...), custom_call_target="tpu_custom_call" | custom-call | flops 637009920 | bytes 4194304 | tf_op jit(solution)/shard_map/pallas_call | solution.py:59
  23.9 0.3 collective-permute-start.5
  24.2 0.0 copy-done.3
  24.2 0.0 copy-start.4
  24.2 0.0 copy-start.2
  24.2 2.1 %shard_map.105.refs_0_.refs_1_ = f32[2,480,192]{2,1,0:T(8,128)S(1)} custom-call(bf16[3,12,48,256]{3,2,1,0:T(8,128)(2,1)S(1)} %get-tuple-element.31.refs_0_, bf16[3,12,48,256]{3,2,1,0:T(8,128)(2,1)S(1)} %get-tuple-element.30.refs_5_.refs_1_, bf16[3,3,3,192,192]{4,3,2,1,0:T(8,128)(2,1)S(1)} %copy-done.1, ...), custom_call_target="tpu_custom_call" | custom-call | flops 955514880 | bytes 4194304 | tf_op jit(solution)/shard_map/pallas_call | solution.py:59
  26.3 2.4 %collective-permute-done.6.refs_1_ = bf16[15,48,128]{2,1,0:T(8,128)(2,1)S(1)} collective-permute-done((bf16[15,48,128]{2,1,0:T(8,128)(2,1)S(1)}, bf16[15,48,128]{2,1,0:T(8,128)(2,1)S(1)}, u32[]{:S(2)}, u32[]{:S(2)}) %collective-permute-start.6) | collective-permute-done | bytes 184352 | tf_op jit(solution)/shard_map/ppermute | solution.py:525
  28.7 0.0 copy-done.4
  28.7 0.4 %shard_map.106 = (bf16[8,48,192]{2,1,0:T(8,128)(2,1)S(1)}, bf16[15,48,128]{2,1,0:T(8,128)(2,1)S(1)}) custom-call(f32[2,480,192]{2,1,0:T(8,128)S(1)} %shard_map.105.refs_0_.refs_1_, bf16[15,48,128]{2,1,0:T(8,128)(2,1)S(1)} %collective-permute-done.6.refs_1_, f32[192]{0:T(256)S(1)} %copy-done.4), custom_call_target="tpu_custom_call" | custom-call | flops 16777216 | bytes 4194304 | tf_op jit(solution)/shard_map/pallas_call | solution.py:59
  29.2 1.3 %collective-permute-start.8 = (bf16[15,48,128]{2,1,0:T(8,128)(2,1)S(1)}, bf16[15,48,128]{2,1,0:T(8,128)(2,1)S(1)}, u32[]{:S(2)}, u32[]{:S(2)}) collective-permute-start(bf16[15,48,128]{2,1,0:T(8,128)(2,1)S(1)} %get-tuple-element.34.refs_0_), channel_id=1, source_target_pairs={{0,64},{64,128},{128,192},{1,65},{65,129},{129,193},{2,66},{66,130... | collective-permute-start | bytes 552968 | tf_op jit(solution)/shard_map/ppermute | solution.py:520
  30.5 0.0 copy-done.2
  30.5 0.3 shard_map.107.refs_1_.refs_2_
  30.8 0.9 %shard_map.108.refs_3_.refs_1_ = f32[4,384,192]{2,1,0:T(8,128)S(1)} custom-call(bf16[15,48,128]{2,1,0:T(8,128)(2,1)S(1)} %get-tuple-element.34.refs_0_, bf16[3,4,768,192]{3,2,1,0:T(8,128)(2,1)S(1)} %shard_map.107.refs_1_.refs_2_), custom_call_target="tpu_custom_call" | custom-call | flops 254803968 | bytes 4194304 | tf_op jit(solution)/shard_map/pallas_call | solution.py:59
  31.7 0.0 collective-permute-done.5.refs_1_
  31.7 0.4 %shard_map.109 = (bf16[8,48,192]{2,1,0:T(8,128)(2,1)S(1)}, bf16[15,48,128]{2,1,0:T(8,128)(2,1)S(1)}) custom-call(f32[2,480,192]{2,1,0:T(8,128)S(1)} %shard_map.105.refs_0_.refs_1_, bf16[15,48,128]{2,1,0:T(8,128)(2,1)S(1)} %collective-permute-done.5.refs_1_, f32[192]{0:T(256)S(1)} %copy-done.4, f32[4,384,192]{2,1,0:T(8,128)S(1)} %shard_map.108.refs_3_.refs_1_), custom_call_target="tpu_custom_call" | custom-call | flops 16777216 | bytes 4194304 | tf_op jit(solution)/shard_map/pallas_call | solution.py:59
  32.1 3.3 %collective-permute-start.7 = (bf16[15,48,128]{2,1,0:T(8,128)(2,1)S(1)}, bf16[15,48,128]{2,1,0:T(8,128)(2,1)S(1)}, u32[]{:S(2)}, u32[]{:S(2)}) collective-permute-start(bf16[15,48,128]{2,1,0:T(8,128)(2,1)S(1)} %get-tuple-element.35.refs_0_), channel_id=1, source_target_pairs={{0,64},{64,128},{128,192},{1,65},{65,129},{129,193},{2,66},{66,130... | collective-permute-start | bytes 552968 | tf_op jit(solution)/shard_map/ppermute | solution.py:520
  35.4 1.5 %shard_map.110 = (f32[2,4,384,192]{3,2,1,0:T(8,128)S(1)}, bf16[2,8,48,192]{3,2,1,0:T(8,128)(2,1)}) custom-call(bf16[15,48,128]{2,1,0:T(8,128)(2,1)S(1)} %get-tuple-element.35.refs_0_, f32[4,384,192]{2,1,0:T(8,128)S(1)} %shard_map.108.refs_3_.refs_1_, bf16[3,4,768,192]{3,2,1,0:T(8,128)(2,1)S(1)} %shard_map.107.refs_1_.refs_2_, ...), custom_call_target="tpu_custom_call" | custom-call | flops 509607936 | bytes 4194304 | tf_op jit(solution)/shard_map/pallas_call | solution.py:59
  36.9 0.0 collective-permute-done.8.refs_0_
  37.0 1.7 %shard_map.111 = (bf16[2,8,2,96,192]{4,3,2,1,0:T(8,128)(2,1)}, f32[4,384,192]{2,1,0:T(8,128)S(1)}) custom-call(bf16[15,48,128]{2,1,0:T(8,128)(2,1)S(1)} %collective-permute-done.8.refs_0_, bf16[3,4,768,192]{3,2,1,0:T(8,128)(2,1)S(1)} %shard_map.107.refs_1_.refs_2_, f32[2,4,384,192]{3,2,1,0:T(8,128)S(1)} %get-tuple-element.39.refs_2_), custom_call_target="tpu_custom_call" | custom-call | flops 509607936 | bytes 4194304 | tf_op jit(solution)/shard_map/pallas_call | solution.py:59
  38.7 0.0 collective-permute-done.7.refs_0_
  38.7 1.7 %shard_map.112 = bf16[2,8,2,96,192]{4,3,2,1,0:T(8,128)(2,1)} custom-call(bf16[15,48,128]{2,1,0:T(8,128)(2,1)S(1)} %collective-permute-done.7.refs_0_, bf16[3,4,768,192]{3,2,1,0:T(8,128)(2,1)S(1)} %shard_map.107.refs_1_.refs_2_, f32[4,384,192]{2,1,0:T(8,128)S(1)} %get-tuple-element.40.refs_2_, ...), custom_call_target="tpu_custom_call", output_to_operand_aliasing={{}: (3, {})} | custom-call | flops 254803968 | bytes 4194304 | tf_op jit(solution)/shard_map/pallas_call | solution.py:59
Async XLA Ops:
  0.6 4.4 %copy-start = (bf16[3,3,3,384,192]{3,4,2,1,0:T(8,128)(2,1)S(1)}, bf16[3,3,3,384,192]{3,4,2,1,0:T(8,128)(2,1)}, u32[]{:S(2)}) copy-start(bf16[3,3,3,384,192]{3,4,2,1,0:T(8,128)(2,1)} %param.10) | copy-start | bytes 11943940
  1.9 7.9 %collective-permute-start = (bf16[2,3,48,384]{3,2,1,0:T(8,128)(2,1)S(1)}, bf16[2,3,48,384]{3,2,1,0:T(8,128)(2,1)S(1)}, u32[]{:S(2)}, u32[]{:S(2)}) collective-permute-start(bf16[2,3,48,384]{3,2,1,0:T(8,128)(2,1)S(1)} %get-tuple-element.24), channel_id=1, source_target_pairs={{0,1},{2,3},{4,5},{6,7},{8,9},{10,11},{12,13},{14,15},{16,17},{18,... | collective-permute-start | bytes 663560 | tf_op jit(solution)/shard_map/ppermute | solution.py:534
  2.0 8.8 %collective-permute-start.1 = (bf16[2,3,48,384]{3,2,1,0:T(8,128)(2,1)S(1)}, bf16[2,3,48,384]{3,2,1,0:T(8,128)(2,1)S(1)}, u32[]{:S(2)}, u32[]{:S(2)}) collective-permute-start(bf16[2,3,48,384]{3,2,1,0:T(8,128)(2,1)S(1)} %get-tuple-element.25), channel_id=1, source_target_pairs={{1,2},{3,4},{5,6},{7,8},{9,10},{11,12},{13,14},{15,16},{17,18},{19... | collective-permute-start | bytes 663560 | tf_op jit(solution)/shard_map/ppermute | solution.py:534
  6.9 12.4 %collective-permute-start.2 = (bf16[2,9,48,128]{3,2,1,0:T(8,128)(2,1)S(1)}, bf16[2,9,48,128]{3,2,1,0:T(8,128)(2,1)S(1)}, u32[]{:S(2)}, u32[]{:S(2)}) collective-permute-start(bf16[2,9,48,128]{3,2,1,0:T(8,128)(2,1)S(1)} %shard_map.102), channel_id=1, source_target_pairs={{0,64},{64,128},{128,192},{192,0},{1,65},{65,129},{129,193},{193,1... | collective-permute-start | bytes 663560 | tf_op jit(solution)/shard_map/ppermute | solution.py:525
  11.9 7.5 %collective-permute-start.4 = (bf16[9,48,128]{2,1,0:T(8,128)(2,1)S(1)}, bf16[9,48,128]{2,1,0:T(8,128)(2,1)S(1)}, u32[]{:S(2)}, u32[]{:S(2)}) collective-permute-start(bf16[9,48,128]{2,1,0:T(8,128)(2,1)S(1)} %get-tuple-element.27.refs_6_), channel_id=1, source_target_pairs={{0,64},{64,128},{128,192},{192,0},{1,65},{65,129},{129,193},{193,1... | collective-permute-start | bytes 331784 | tf_op jit(solution)/shard_map/ppermute | solution.py:525
  13.5 3.2 %copy-start.1 = (bf16[3,3,3,192,192]{4,3,2,1,0:T(8,128)(2,1)S(1)}, bf16[3,3,3,192,192]{4,3,2,1,0:T(8,128)(2,1)}, u32[]{:S(2)}) copy-start(bf16[3,3,3,192,192]{4,3,2,1,0:T(8,128)(2,1)} %refs_2_.3) | copy-start | bytes 5971972
  15.1 7.1 %collective-permute-start.3 = (bf16[9,48,128]{2,1,0:T(8,128)(2,1)S(1)}, bf16[9,48,128]{2,1,0:T(8,128)(2,1)S(1)}, u32[]{:S(2)}, u32[]{:S(2)}) collective-permute-start(bf16[9,48,128]{2,1,0:T(8,128)(2,1)S(1)} %get-tuple-element.29), channel_id=1, source_target_pairs={{0,64},{64,128},{128,192},{192,0},{1,65},{65,129},{129,193},{193,1... | collective-permute-start | bytes 331784 | tf_op jit(solution)/shard_map/ppermute | solution.py:525
  17.9 1.4 %copy-start.5 = (f32[192]{0:T(256)S(1)}, f32[192]{0:T(256)}, u32[]{:S(2)}) copy-start(f32[192]{0:T(256)} %refs_3_.3) | copy-start | bytes 2308
  20.6 3.6 %copy-start.3 = (bf16[384,192]{0,1:T(8,128)(2,1)S(1)}, bf16[384,192]{0,1:T(8,128)(2,1)}, u32[]{:S(2)}) copy-start(bf16[384,192]{0,1:T(8,128)(2,1)} %param.13) | copy-start | bytes 442372
  20.6 8.1 %collective-permute-start.6 = (bf16[15,48,128]{2,1,0:T(8,128)(2,1)S(1)}, bf16[15,48,128]{2,1,0:T(8,128)(2,1)S(1)}, u32[]{:S(2)}, u32[]{:S(2)}) collective-permute-start(bf16[15,48,128]{2,1,0:T(8,128)(2,1)S(1)} %get-tuple-element.33), channel_id=1, source_target_pairs={{0,64},{64,128},{128,192},{192,0},{1,65},{65,129},{129,193},{193,1... | collective-permute-start | bytes 552968 | tf_op jit(solution)/shard_map/ppermute | solution.py:525
  23.9 7.8 %collective-permute-start.5 = (bf16[15,48,128]{2,1,0:T(8,128)(2,1)S(1)}, bf16[15,48,128]{2,1,0:T(8,128)(2,1)S(1)}, u32[]{:S(2)}, u32[]{:S(2)}) collective-permute-start(bf16[15,48,128]{2,1,0:T(8,128)(2,1)S(1)} %get-tuple-element.32), channel_id=1, source_target_pairs={{0,64},{64,128},{128,192},{192,0},{1,65},{65,129},{129,193},{193,1... | collective-permute-start | bytes 552968 | tf_op jit(solution)/shard_map/ppermute | solution.py:525
  24.2 4.5 %copy-start.4 = (f32[192]{0:T(256)S(1)}, f32[192]{0:T(256)}, u32[]{:S(2)}) copy-start(f32[192]{0:T(256)} %refs_2_.5) | copy-start | bytes 2308
  24.2 6.3 %copy-start.2 = (bf16[3,3,3,192,192]{4,3,2,1,0:T(8,128)(2,1)S(1)}, bf16[3,3,3,192,192]{4,3,2,1,0:T(8,128)(2,1)}, u32[]{:S(2)}) copy-start(bf16[3,3,3,192,192]{4,3,2,1,0:T(8,128)(2,1)} %refs_0_.3) | copy-start | bytes 5971972
  29.2 7.8 %collective-permute-start.8 = (bf16[15,48,128]{2,1,0:T(8,128)(2,1)S(1)}, bf16[15,48,128]{2,1,0:T(8,128)(2,1)S(1)}, u32[]{:S(2)}, u32[]{:S(2)}) collective-permute-start(bf16[15,48,128]{2,1,0:T(8,128)(2,1)S(1)} %get-tuple-element.34.refs_0_), channel_id=1, source_target_pairs={{0,64},{64,128},{128,192},{1,65},{65,129},{129,193},{2,66},{66,130... | collective-permute-start | bytes 552968 | tf_op jit(solution)/shard_map/ppermute | solution.py:520
  32.1 6.6 %collective-permute-start.7 = (bf16[15,48,128]{2,1,0:T(8,128)(2,1)S(1)}, bf16[15,48,128]{2,1,0:T(8,128)(2,1)S(1)}, u32[]{:S(2)}, u32[]{:S(2)}) collective-permute-start(bf16[15,48,128]{2,1,0:T(8,128)(2,1)S(1)} %get-tuple-element.35.refs_0_), channel_id=1, source_target_pairs={{0,64},{64,128},{128,192},{1,65},{65,129},{129,193},{2,66},{66,130... | collective-permute-start | bytes 552968 | tf_op jit(solution)/shard_map/ppermute | solution.py:520
